TPU v7x, 128 devices: a whole 4x4x4 slice. The times are simulated.
128 devices in a mesh: gx: 2 (over core), gy: 4 (over x), gz: 16 (over z, y).
Axes of the slice: x: 4, y: 4, z: 4, core: 2. Of those that a mesh axis runs over, the one named last changes fastest.
Arguments:
- jacobian: bfloat16 [4096, 7, 135, 135], P(('gx', 'gy', 'gz')), may hold values from -6 to 6
- prolong: bfloat16 [4096, 135, 135], P(('gx', 'gy', 'gz')), may hold values from -0.5 to 0.5
- residual: bfloat16 [4096, 135], P(('gx', 'gy', 'gz')), may hold values from -6 to 6
- neighbours: int32 [4096, 6], P(('gx', 'gy', 'gz')), may hold values from -1 to 4095, as said below
- agg_map: int32 [4096], P(('gx', 'gy', 'gz')), may hold values from 0 to 511, as said below
- owners: int32 [512], P(('gx', 'gy', 'gz')), may hold values from 0 to 12, as said below
Outputs:
- coarse: bfloat16 [2048, 7, 135, 135], P(('gx', 'gy', 'gz'))
- restricted: bfloat16 [2048, 135], P(('gx', 'gy', 'gz'))
Inputs may be any that keep to these rules, and one draw needn't show every extreme that they name: `neighbours`: elements form a structured grid of bricks of 4 x 4 x 2 per device, laid out by the device's gx, gy, gz index; inside a device their numbering is an arbitrary permutation. The neighbour in direction -x or +x lies on the same device or on the device one step along gx (likewise y with gy, z with gz); exactly 8, 8 and 16 elements of a device have their x, y and z neighbour of one side off the device or absent. `agg_map`: aggregates are cubes of 2 x 2 x 2 elements of one device's brick; device d holds aggregates d * 4 to (d + 1) * 4 - 1. `owners`: owners are multiples of 4; each device hands exactly 1 of its aggregates to each such owner.
All inputs are finite; a program needn't handle non-finite values.
Results may differ from a plain program's by a relative error of at most 0.0051.
Values may be sent and summed in bfloat16 or wider, within the bound.
No kernel may reach another device: no remote copies, remote signals or barrier semaphores. Data moves between devices by JAX's collectives and lax.ppermute only.
A program may use at most 192 MiB of HBM per device.

v0:
```python
import jax
import jax.numpy as jnp
from jax import lax
from jax.sharding import PartitionSpec as P


def from_behind(value, axis, steps):
    count = lax.axis_size(axis)
    initial, last = (max(0, -steps), min(count, count - steps))
    return lax.ppermute(value, axis, [(source, source + steps) for source in range(initial, last)])


def fetch_whole(blocks, axis_num, offset):
    if axis_num == 0:
        return from_behind(blocks, "gx", offset)
    if axis_num == 1:
        return from_behind(blocks, "gy", offset)
    return from_behind(blocks, "gz", offset)


def body(jacobian, prolong, residual, neighbours, agg_map, owners):
    elems = jacobian.shape[0]
    width = prolong.shape[1]
    aggs_here = owners.shape[0]
    size_y = lax.axis_size("gy")
    size_z = lax.axis_size("gz")
    per_owner = aggs_here // 4
    device = (lax.axis_index("gx") * size_y + lax.axis_index("gy")) * size_z + lax.axis_index("gz")
    id_base = device * elems
    local_ids = neighbours - id_base
    on_device = (local_ids >= 0) & (local_ids < elems)
    is_valid = neighbours >= 0
    strides = (size_y * size_z, size_z, 1)
    flat_blocks = prolong.reshape(elems, width * width)
    elem_counter = jnp.arange(elems, dtype=jnp.int32)
    pool_parts = [flat_blocks]
    columns = [elem_counter]
    live = [jnp.ones((elems,), bool)]
    pool_start = elems
    for direction in range(6):
        axis_num = direction // 2
        offset = 1 if direction % 2 == 0 else -1
        source_base = id_base - offset * strides[axis_num] * elems
        source_ids = neighbours[:, direction] - source_base
        fetched = fetch_whole(flat_blocks, axis_num, offset)
        far_column = pool_start + source_ids
        pool_start = pool_start + elems
        pool_parts.append(fetched)
        columns.append(jnp.where(on_device[:, direction], local_ids[:, direction], far_column))
        live.append(is_valid[:, direction])
    pool = jnp.concatenate(pool_parts, axis=0)
    column_ids = jnp.stack(columns, axis=1)
    live_pairs = jnp.stack(live, axis=1)
    pick = (
        (column_ids[:, :, None] == jnp.arange(pool_start, dtype=jnp.int32)[None, None, :])
        & live_pairs[:, :, None]
    ).astype(jnp.bfloat16)
    gathered = jnp.einsum("edt,tx->edx", pick, pool, preferred_element_type=jnp.float32).astype(
        jnp.bfloat16
    )
    gathered = gathered.reshape(elems, 7, width, width)
    products = jnp.einsum(
        "edij,edjk->edik", jacobian, gathered, preferred_element_type=jnp.float32
    ).astype(jnp.bfloat16)
    triple = jnp.einsum("eji,edjk->edik", prolong, products, preferred_element_type=jnp.float32)
    near_agg = agg_map[jnp.clip(local_ids, 0, elems - 1)]
    same_agg = on_device & (near_agg == agg_map[:, None])
    slot_ids = jnp.where(same_agg, 0, jnp.arange(1, 7, dtype=jnp.int32)[None, :])
    slot_ids = jnp.concatenate([jnp.zeros((elems, 1), jnp.int32), slot_ids], axis=1)
    present = jnp.concatenate([jnp.ones((elems, 1), bool), is_valid], axis=1)
    slot_hot = (
        (slot_ids[:, :, None] == jnp.arange(7, dtype=jnp.int32)) & present[:, :, None]
    ).astype(jnp.float32)
    agg_hot = (
        (agg_map - device * aggs_here)[:, None] == jnp.arange(aggs_here, dtype=jnp.int32)
    ).astype(jnp.float32)
    coarse_rows = jnp.einsum(
        "ea,eds,edik->asik", agg_hot, slot_hot, triple, precision=lax.Precision.HIGHEST
    ).astype(jnp.bfloat16)
    per_element = jnp.einsum("eji,ej->ei", prolong, residual, preferred_element_type=jnp.float32)
    restr = jnp.dot(agg_hot.T, per_element, precision=lax.Precision.HIGHEST).astype(jnp.bfloat16)
    agg_counter = jnp.arange(aggs_here, dtype=jnp.int32)
    earlier = (owners[None, :] == owners[:, None]) & (agg_counter[None, :] < agg_counter[:, None])
    within = jnp.sum(earlier.astype(jnp.int32), axis=1)
    send_slot = owners * per_owner + within
    select = (
        jnp.arange(size_z * per_owner, dtype=jnp.int32)[:, None] == send_slot[None, :]
    ).astype(jnp.bfloat16)
    send_rows = jnp.einsum(
        "pa,asik->psik", select, coarse_rows, preferred_element_type=jnp.float32
    ).astype(jnp.bfloat16)
    send_restr = jnp.dot(select, restr, preferred_element_type=jnp.float32).astype(jnp.bfloat16)
    received = (
        lax.all_to_all(send_rows, "gz", split_axis=0, concat_axis=0, tiled=True),
        lax.all_to_all(send_restr, "gz", split_axis=0, concat_axis=0, tiled=True),
    )
    return (received[0], received[1])


def solution(mesh):
    return jax.shard_map(
        body,
        mesh=mesh,
        in_specs=(
            P(("gx", "gy", "gz"), None, None, None),
            P(("gx", "gy", "gz"), None, None),
            P(("gx", "gy", "gz"), None),
            P(("gx", "gy", "gz"), None),
            P(("gx", "gy", "gz")),
            P(("gx", "gy", "gz")),
        ),
        out_specs=(P(("gx", "gy", "gz"), None, None, None), P(("gx", "gy", "gz"), None)),
        check_vma=False,
    )
```

profile of v0, /device:TPU:0, one launch (start us, length us, event | category | flops | bytes accessed | tf_op | source)
XLA Modules:
  0.0 369.0 jit_solution(17294846540678352143)
XLA Ops:
  0.7 2.9 copy.94
  3.6 2.1 reshape.25
  5.7 2.3 collective-permute-start
  8.0 1.3 collective-permute-start.1
  9.3 5.0 %collective-permute-start.2 = (bf16[32,18225]{1,0:T(8,128)(2,1)S(1)}, bf16[32,18225]{1,0:T(8,128)(2,1)}, u32[]{:S(2)}, u32[]{:S(2)}) collective-permute-start(bf16[32,18225]{1,0:T(8,128)(2,1)S(1)} %reshape.25), channel_id=1, source_target_pairs={{0,16},{16,32},{32,48},{1,17},{17,33},{33,49},{2,18},{18,34},{34,5... | collective-permute-start | bytes 3499208 | tf_op jit(solution)/shard_map/ppermute | solution.py:10
  14.2 1.3 collective-permute-start.3
  15.5 3.6 collective-permute-start.4
  19.1 0.9 convert_reduce_fusion
  20.0 0.7 add.69
  20.7 2.9 fusion.36
  24.0 0.6 copy.105
  24.6 7.7 %all-to-all-start.1 = ((bf16[16,1,135]{2,1,0:T(2,128)(2,1)}), bf16[16,1,135]{2,1,0:T(2,128)(2,1)S(1)}, u32[]{:S(2)}, u32[]{:S(2)}) async-start(bf16[16,1,135]{2,1,0:T(2,128)(2,1)} %copy.105), calls=%async_computation.1 | async-start | bytes 32768 | tf_op jit(solution)/shard_map/all_to_all | solution.py:95
  32.6 1.6 gather_fusion
  34.8 1.3 collective-permute-start.5
  36.1 1.4 constant_dynamic-update-slice_fusion.5
  37.5 1.4 constant_dynamic-update-slice_fusion.4
  39.0 1.4 constant_dynamic-update-slice_fusion.3
  40.4 3.7 collective-permute-done.3
  44.0 1.4 constant_dynamic-update-slice_fusion.2
  45.6 19.5 %collective-permute-done.5 = bf16[32,18225]{1,0:T(8,128)(2,1)S(1)} collective-permute-done((bf16[32,18225]{1,0:T(8,128)(2,1)S(1)}, bf16[32,18225]{1,0:T(8,128)(2,1)S(1)}, u32[]{:S(2)}, u32[]{:S(2)}) %collective-permute-start.5) | collective-permute-done | bytes 1166432 | tf_op jit(solution)/shard_map/ppermute | solution.py:10
  65.2 5.6 %convolution_convert_fusion = bf16[32,7,18225]{2,0,1:T(8,128)(2,1)} fusion(bf16[224,18225]{1,0:T(8,128)(2,1)S(1)} %constant_dynamic-update-slice_fusion, s32[32,7]{0,1:T(8,128)S(1)} %stack.5, pred[32,7]{0,1:T(8,128)(4,1)S(1)} %stack.6), kind=kOutput, calls=%fused_computation.3 | convolution fusion | flops 1833097984 | bytes 16330720 | tf_op jit(solution)/shard_map/edt,tx->edx/dot_general | solution.py:58
  70.8 21.9 %reshape.26 = bf16[32,7,135,135]{3,2,0,1:T(8,128)(2,1)} reshape(bf16[32,7,18225]{2,0,1:T(8,128)(2,1)} %convolution_convert_fusion) | data formatting | bytes 16329600 | tf_op jit(solution)/shard_map/reshape | solution.py:61
  92.7 27.3 %fusion.8 = f32[32,7,135,135]{2,3,1,0:T(8,128)} fusion(bf16[32,7,135,135]{3,2,0,1:T(8,128)(2,1)} %reshape.26, bf16[32,7,135,135]{3,0,2,1:T(8,128)(2,1)} %param.6, bf16[32,135,135,1]{2,0,1,3:T(8,128)(2,1)S(1)} %bitcast.41), kind=kOutput, calls=%fused_computation.10 | convolution fusion | flops 2208578304 | bytes 33825600 | tf_op jit(solution)/shard_map/eji,edjk->edik/dot_general | solution.py:65
  120.0 38.8 %copy.102 = f32[32,7,135,135]{3,1,2,0:T(8,128)} copy(f32[32,7,135,135]{2,3,1,0:T(8,128)} %fusion.8) | data formatting | bytes 32659200 | tf_op jit(solution)/shard_map/eji,edjk->edik/transpose | solution.py:65
  158.8 32.7 %fusion.28 = f32[32,135,135,7]{2,3,1,0:T(8,128)} fusion(f32[32,7,135,135]{3,1,2,0:T(8,128)} %copy.102, s32[32,7]{1,0:T(8,128)S(1)} %concatenate.8.clone, pred[32,7]{1,0:T(8,128)(4,1)S(1)} %copy.101), kind=kOutput, calls=%fused_computation.24 | convolution fusion | flops 342924736 | bytes 32660320 | tf_op jit(solution)/shard_map/ea,eds,edik->asik/dot_general | solution.py:77
  191.5 34.6 %fusion = bf16[135,135,7,4]{1,3,0,2:T(4,128)(2,1)S(1)} fusion(f32[32,135,135,7]{2,3,1,0:T(8,128)} %fusion.28, s32[32]{0:T(128)S(1)} %broadcast_subtract_fusion.1), kind=kOutput, calls=%fused_computation.1 | convolution fusion | flops 195955328 | bytes 17350328 | tf_op jit(solution)/shard_map/ea,eds,edik->asik/dot_general | solution.py:77
  226.1 3.0 convolution_convert_fusion.1
  229.1 6.2 %copy.104 = bf16[16,7,135,135]{3,2,1,0:T(8,128)(2,1)} copy(bf16[16,7,135,135]{3,0,2,1:T(8,128)(2,1)S(1)} %convolution_convert_fusion.1) | data formatting | bytes 8164800 | tf_op jit(solution)/shard_map/convert_element_type | solution.py:91
  235.3 9.4 %all-to-all-start = ((bf16[16,7,135,135]{3,2,1,0:T(8,128)(2,1)}), bf16[16,7,135,135]{3,2,1,0:T(8,128)(2,1)}, u32[]{:S(2)}, u32[]{:S(2)}) async-start(bf16[16,7,135,135]{3,2,1,0:T(8,128)(2,1)} %copy.104), calls=%async_computation | async-start | bytes 15597568 | tf_op jit(solution)/shard_map/all_to_all | solution.py:94
  244.7 0.6 copy.144
  245.3 115.6 %all-to-all-done = bf16[16,7,135,135]{3,2,1,0:T(8,128)(2,1)} async-done(((bf16[16,7,135,135]{3,2,1,0:T(8,128)(2,1)}), bf16[16,7,135,135]{3,2,1,0:T(8,128)(2,1)}, u32[]{:S(2)}, u32[]{:S(2)}) %all-to-all-start) | async-done | bytes 4082432 | tf_op jit(solution)/shard_map/all_to_all | solution.py:94
  360.9 8.0 %copy.106 = bf16[16,7,135,135]{3,0,2,1:T(8,128)(2,1)} copy(bf16[16,7,135,135]{3,2,1,0:T(8,128)(2,1)} %all-to-all-done) | data formatting | bytes 8164800
  (38 shorter events, 1.6 us)
Async XLA Ops:
  0.6 20.0 %copy-start = (bf16[32,135]{1,0:T(8,128)(2,1)S(1)}, bf16[32,135]{1,0:T(8,128)(2,1)}, u32[]{:S(2)}) copy-start(bf16[32,135]{1,0:T(8,128)(2,1)} %param.8) | copy-start | bytes 25924
  0.6 22.9 %copy-start.2 = (s32[32]{0:T(128)S(1)}, s32[32]{0:T(128)}, u32[]{:S(2)}) copy-start(s32[32]{0:T(128)} %param.10) | copy-start | bytes 388
  0.7 31.7 %copy-start.4 = (s32[32,6]{0,1:T(8,128)S(1)}, s32[32,6]{0,1:T(8,128)}, u32[]{:S(2)}) copy-start(s32[32,6]{0,1:T(8,128)} %param.9) | copy-start | bytes 2308
  5.7 29.2 %collective-permute-start = (bf16[32,18225]{1,0:T(8,128)(2,1)S(1)}, bf16[32,18225]{1,0:T(8,128)(2,1)}, u32[]{:S(2)}, u32[]{:S(2)}) collective-permute-start(bf16[32,18225]{1,0:T(8,128)(2,1)S(1)} %reshape.25), channel_id=1, source_target_pairs={{0,64},{1,65},{2,66},{3,67},{4,68},{5,69},{6,70},{7,71},{8,72},{9,... | collective-permute-start | bytes 3499208 | tf_op jit(solution)/shard_map/ppermute | solution.py:10
  8.0 29.6 %collective-permute-start.1 = (bf16[32,18225]{1,0:T(8,128)(2,1)S(1)}, bf16[32,18225]{1,0:T(8,128)(2,1)}, u32[]{:S(2)}, u32[]{:S(2)}) collective-permute-start(bf16[32,18225]{1,0:T(8,128)(2,1)S(1)} %reshape.25), channel_id=1, source_target_pairs={{64,0},{65,1},{66,2},{67,3},{68,4},{69,5},{70,6},{71,7},{72,8},{73... | collective-permute-start | bytes 3499208 | tf_op jit(solution)/shard_map/ppermute | solution.py:10
  9.3 29.7 %collective-permute-start.2 = (bf16[32,18225]{1,0:T(8,128)(2,1)S(1)}, bf16[32,18225]{1,0:T(8,128)(2,1)}, u32[]{:S(2)}, u32[]{:S(2)}) collective-permute-start(bf16[32,18225]{1,0:T(8,128)(2,1)S(1)} %reshape.25), channel_id=1, source_target_pairs={{0,16},{16,32},{32,48},{1,17},{17,33},{33,49},{2,18},{18,34},{34,5... | collective-permute-start | bytes 3499208 | tf_op jit(solution)/shard_map/ppermute | solution.py:10
  14.2 29.8 %collective-permute-start.3 = (bf16[32,18225]{1,0:T(8,128)(2,1)S(1)}, bf16[32,18225]{1,0:T(8,128)(2,1)}, u32[]{:S(2)}, u32[]{:S(2)}) collective-permute-start(bf16[32,18225]{1,0:T(8,128)(2,1)S(1)} %reshape.25), channel_id=1, source_target_pairs={{16,0},{32,16},{48,32},{17,1},{33,17},{49,33},{18,2},{34,18},{50,3... | collective-permute-start | bytes 3499208 | tf_op jit(solution)/shard_map/ppermute | solution.py:10
  15.5 29.9 %collective-permute-start.4 = (bf16[32,18225]{1,0:T(8,128)(2,1)S(1)}, bf16[32,18225]{1,0:T(8,128)(2,1)S(1)}, u32[]{:S(2)}, u32[]{:S(2)}) collective-permute-start(bf16[32,18225]{1,0:T(8,128)(2,1)S(1)} %reshape.25), channel_id=1, source_target_pairs={{0,1},{1,2},{2,3},{3,4},{4,5},{5,6},{6,7},{7,8},{8,9},{9,10},{10,1... | collective-permute-start | bytes 3499208 | tf_op jit(solution)/shard_map/ppermute | solution.py:10
  24.6 210.7 %all-to-all-start.1 = ((bf16[16,1,135]{2,1,0:T(2,128)(2,1)}), bf16[16,1,135]{2,1,0:T(2,128)(2,1)S(1)}, u32[]{:S(2)}, u32[]{:S(2)}) async-start(bf16[16,1,135]{2,1,0:T(2,128)(2,1)} %copy.105), calls=%async_computation.1 | async-start | bytes 32768 | tf_op jit(solution)/shard_map/all_to_all | solution.py:95
  34.8 30.2 %collective-permute-start.5 = (bf16[32,18225]{1,0:T(8,128)(2,1)S(1)}, bf16[32,18225]{1,0:T(8,128)(2,1)S(1)}, u32[]{:S(2)}, u32[]{:S(2)}) collective-permute-start(bf16[32,18225]{1,0:T(8,128)(2,1)S(1)} %reshape.25), channel_id=1, source_target_pairs={{1,0},{2,1},{3,2},{4,3},{5,4},{6,5},{7,6},{8,7},{9,8},{10,9},{11,1... | collective-permute-start | bytes 3499208 | tf_op jit(solution)/shard_map/ppermute | solution.py:10
  70.8 21.9 %copy-start.3 = (bf16[32,135,135]{2,0,1:T(8,128)(2,1)S(1)}, bf16[32,135,135]{2,0,1:T(8,128)(2,1)}, u32[]{:S(2)}) copy-start(bf16[32,135,135]{2,0,1:T(8,128)(2,1)} %param.7) | copy-start | bytes 3499204
  235.3 125.7 %all-to-all-start = ((bf16[16,7,135,135]{3,2,1,0:T(8,128)(2,1)}), bf16[16,7,135,135]{3,2,1,0:T(8,128)(2,1)}, u32[]{:S(2)}, u32[]{:S(2)}) async-start(bf16[16,7,135,135]{3,2,1,0:T(8,128)(2,1)} %copy.104), calls=%async_computation | async-start | bytes 15597568 | tf_op jit(solution)/shard_map/all_to_all | solution.py:94
  244.7 124.3 %copy-start.1 = (bf16[32,135]{1,0:T(8,128)(2,1)S(1)}, bf16[32,135]{1,0:T(8,128)(2,1)}, u32[]{:S(2)}) copy-start(bf16[32,135]{1,0:T(8,128)(2,1)} %param.8) | copy-start | bytes 25924
where the time goes:
time: 371 us; the launch traced here: 369 us
  waiting for transfers between devices  139 us (37%)
  matrix products  107 us (29%)
  local copies, waits for them, and re-layouts  89.2 us (24%)
  starting transfers between devices  31.8 us (9%)
    all_to_all x1, waiting for transfers between devices, body(): lax.all_to_all(send_rows, 'gz', split_axis=0, concat_axis=0, tiled=True)  116 us
    dot_general x2, matrix products, body(): jnp.einsum('ea,eds,edik->asik', agg_hot, slot_hot, triple, precision=lax....  67.3 us
    transpose x1, local copies, waits for them, and re-layouts, body(): jnp.einsum('eji,edjk->edik', prolong, products, preferred_element_type=jn...  38.8 us
    dot_general x1, matrix products, body(): jnp.einsum('eji,edjk->edik', prolong, products, preferred_element_type=jn...  27.3 us
    ppermute x6, waiting for transfers between devices, from_behind(): lax.ppermute(value, axis, [(source, source + steps) for source in range(i...  23.1 us
    reshape x1, local copies, waits for them, and re-layouts, body(): gathered = gathered.reshape(elems, 7, width, width)  21.9 us
    unnamed x20, local copies, waits for them, and re-layouts  17.5 us
    ppermute x6, starting transfers between devices, from_behind(): lax.ppermute(value, axis, [(source, source + steps) for source in range(i...  14.7 us
  transfers between devices with their start and end apart: 8, of which 3 were waited for; matrix products, arithmetic and copies ran while one was open for 50% of the time, Pallas kernels for 0%

commit v1 on v0

v1 whole, which is shorter than its diff:
```python
import functools

import jax
import jax.numpy as jnp
from jax import lax
from jax.experimental import pallas as pl
from jax.experimental.pallas import tpu as pltpu
from jax.sharding import Mesh, PartitionSpec as P

E = 32
W = 135
H = 136
L = 128
R = W - L
BF = jnp.bfloat16
F32 = jnp.float32
VMEM_LIMIT = 56 * 1024 * 1024


def smem():
    return pl.BlockSpec(memory_space=pltpu.SMEM)


def vmem():
    return pl.BlockSpec(memory_space=pltpu.VMEM)


def spread(block, main, rest):
    def step(i, carry):
        for u in range(5):
            row = i * 5 + u
            values = block(row).astype(F32)
            at = pl.ds(pl.multiple_of(row * E, E), E)
            main[at, :] = values[:, :L]
            rest[at, 0:R] = values[:, L:]
        return carry

    lax.fori_loop(0, W // 5, step, 0)


def clear(main, rest):
    main[W * E : H * E, :] = jnp.zeros((E, L), F32)
    rest[...] = jnp.zeros((H * E, L), F32)


def take(ref, element):
    return ref[pl.ds(element, H, stride=E), :]


def pack_kernel(scal, nbr, agg, own, p_ref, meta, pz, xs, ys, pt, main, rest):
    base = scal[0]

    def place(e, carry):
        def near(direction):
            local = nbr[direction, e] - base
            here = (local >= 0) & (local < E)
            safe = jnp.clip(local, 0, E - 1)
            same = here & (agg[safe] == agg[e])
            return here.astype(jnp.int32), same.astype(jnp.int32)

        here_xm, odd_x = near(0)
        here_xp, _ = near(1)
        here_ym, odd_y = near(2)
        here_yp, _ = near(3)
        _, odd_z = near(4)
        agg_x = jnp.where(odd_x == 1, 1 - here_xp, here_xm)
        agg_y = jnp.where(odd_y == 1, 1 - here_yp, here_ym)
        meta[odd_z * 16 + (2 * agg_x + odd_x) * 4 + 2 * agg_y + odd_y] = e
        owner = own[agg[e] - scal[1]]
        meta[E + agg_x * 2 + agg_y] = lax.rem(owner // 4 - scal[2] + 4, 4)
        return carry

    lax.fori_loop(0, E, place, 0)
    clear(main, rest)
    spread(lambda row: p_ref[row], main, rest)
    for oz in range(2):
        plane = jnp.zeros((H, L), F32)
        for xy in range(16):
            e = meta[oz * 16 + xy]
            a = take(main, e)
            b = take(rest, e)
            pz[oz, xy] = a.astype(BF)
            plane = plane + (pltpu.roll(b, R * xy, 1) if xy else b)
            pt[oz * 16 + xy] = jnp.concatenate([a.T, b.T[:8]], axis=0).astype(BF)
        pz[oz, 16] = plane.astype(BF)
    face = jnp.where(scal[3] == 0, 12, 0)
    for oz in range(2):
        for v in range(4):
            xs[oz * 4 + v] = pz[oz, face + v]
            ys[0, oz * 4 + v] = pz[oz, v * 4]
            ys[1, oz * 4 + v] = pz[oz, v * 4 + 3]
        xs[8 + oz] = pz[oz, 16]
        ys[0, 8 + oz] = pz[oz, 16]
        ys[1, 8 + oz] = pz[oz, 16]


def pair_kernel(axis, scal, meta, jac, pz, ghost_m, ghost_p, pt, *rest_refs):
    first = axis == 0
    last = axis == 2
    if first:
        res_t, rows, carry_out, rem_out, main, rest, x0, xs, keep = rest_refs
    elif last:
        carry_in, rem_in, rows, main, rest, x0, xs = rest_refs
    else:
        carry_in, rem_in, rows, carry_out, rem_out, main, rest, x0, xs = rest_refs
    step = pl.program_id(0)
    lane = lax.broadcasted_iota(jnp.int32, (H, L), 1)

    @pl.when(step == 0)
    def _():
        clear(main, rest)

    spread(lambda row: jac[0, row], main, rest)

    def product(c, plane_main, plane_rest, idx):
        e = meta[c]
        left = jnp.concatenate([take(main, e), take(rest, e)[:, :8]], axis=1).astype(BF)
        right = jnp.concatenate([plane_main, plane_rest], axis=1)
        out = jnp.dot(left, right, preferred_element_type=F32)
        low = R * idx
        good = (lane >= low) & (lane < low + R)
        return jnp.concatenate([out[:, :L], jnp.where(good, out[:, L:], 0.0)], axis=1)

    def where_is(q, octant):
        ax, ay = q // 2, lax.rem(q, 2)
        ox, oy, oz = octant // 4, octant // 2 % 2, octant % 2
        return 2 * ax + ox, 2 * ay + oy, oz

    def direct(q, carry):
        for octant in range(8):
            x, y, oz = where_is(q, octant)
            idx = x * 4 + y
            keep[q * 8 + octant] = product(oz * 16 + idx, pz[oz, idx], pz[oz, 16], idx)
        return carry

    def sided(minus):
        def run(q, carry):
            for octant in range(8):
                bit = (octant // 4, octant // 2 % 2, octant % 2)[axis]
                x, y, oz = where_is(q, octant)
                c = oz * 16 + x * 4 + y
                if (bit == 1) == minus:
                    shift = -1 if minus else 1
                    nx, ny, nz = x, y, oz
                    if axis == 0:
                        nx = x + shift
                    elif axis == 1:
                        ny = y + shift
                    else:
                        nz = oz + shift
                    idx = nx * 4 + ny
                    out = product(c, pz[nz, idx], pz[nz, 16], idx)
                    if first:
                        out = out + keep[q * 8 + octant]
                        low = L + 112
                        e = meta[c]
                        column = pltpu.roll(res_t[...], lax.rem(112 - e + L, L), 1)
                        out = jnp.concatenate(
                            [out[:, :L], jnp.where(lane == 112, column, out[:, L:])], axis=1
                        )
                    x0[q * 8 + octant] = out.astype(BF)
                    continue
                ghost = ghost_m if minus else ghost_p
                if axis == 2:
                    idx = x * 4 + y
                    out = product(c, ghost[idx], ghost[16], idx)
                else:
                    along, other = (x, y) if axis == 0 else (y, x)
                    spot = along + (-1 if minus else 1)
                    outside = (spot < 0) | (spot > 3)
                    spot = lax.rem(spot + 4, 4)
                    idx = spot * 4 + other if axis == 0 else other * 4 + spot
                    plane_main = jnp.where(outside, ghost[oz * 4 + other], pz[oz, idx])
                    plane_rest = jnp.where(outside, ghost[8 + oz], pz[oz, 16])
                    out = product(c, plane_main, plane_rest, idx)
                    if axis == 0:
                        absent = outside & (scal[3] == (0 if minus else 1))
                        out = out * jnp.where(absent, 0.0, 1.0)
                xs[q * 8 + octant] = out.astype(BF)
            return carry

        return run

    offset = 1 if first else 0
    if first:

        @pl.when(step == 0)
        def _():
            lax.fori_loop(0, 4, direct, 0)

    @pl.when(step == offset)
    def _():
        lax.fori_loop(0, 4, sided(True), 0)

    @pl.when(step == offset + 1)
    def _():
        lax.fori_loop(0, 4, sided(False), 0)

        def finish(q, carry):
            ax, ay = q // 2, lax.rem(q, 2)
            at = meta[E + q]

            def gather(ref, octants):
                acc = None
                for octant in octants:
                    x, y, oz = where_is(q, octant)
                    part = jnp.dot(
                        pt[oz * 16 + x * 4 + y], ref[q * 8 + octant], preferred_element_type=F32
                    )
                    acc = part if acc is None else acc + part
                return acc

            def fold(raw, spots, slot):
                total = None
                for spot in spots:
                    turned = pltpu.roll(raw, lax.rem(R * slot - R * spot + 2 * L, L), 1)
                    total = turned if total is None else total + turned
                good = (lane >= R * slot) & (lane < R * slot + R)
                return jnp.where(good, total, 0.0)

            acc0 = gather(x0, range(8))
            remainder = jnp.zeros((H, L), F32)
            for side in range(2):
                slot = 1 + 2 * axis + side
                chosen = [o for o in range(8) if (o // 4, o // 2 % 2, o % 2)[axis] == side]
                acc = gather(xs, chosen)
                rows[at, side] = acc[:, :L].astype(BF)
                if axis == 0:
                    nx = lax.rem(2 * ax + (-1 if side == 0 else 2) + 4, 4)
                    spots = [nx * 4 + 2 * ay + v for v in range(2)]
                elif axis == 1:
                    ny = lax.rem(2 * ay + (-1 if side == 0 else 2) + 4, 4)
                    spots = [(2 * ax + v) * 4 + ny for v in range(2)]
                else:
                    spots = [(2 * ax + v // 2) * 4 + 2 * ay + v % 2 for v in range(4)]
                remainder = remainder + fold(acc[:, L:], spots, slot)
            if not first:
                acc0 = acc0 + carry_in[at]
                remainder = remainder + rem_in[at]
            if not last:
                carry_out[at] = acc0
                rem_out[at] = remainder
            else:
                rows[at, 2] = acc0[:, :L].astype(BF)
                spots = [(2 * ax + v // 2) * 4 + 2 * ay + v % 2 for v in range(4)]
                raw = acc0[:, L:]
                remainder = remainder + fold(raw, spots, 0)
                moved = pltpu.roll(raw, 49 - 112 + L, 1)
                remainder = jnp.where(lane == 49, moved, remainder)
                rows[at, 3] = remainder.astype(BF)
            return carry

        lax.fori_loop(0, 4, finish, 0)


def pair_call(axis, scal, meta, jac, pz, ghost_m, ghost_p, pt, extra):
    first, last = axis == 0, axis == 2
    steps = 3 if first else 2
    start = 0 if first else 1 + 2 * axis
    planes = 4 if last else 2
    out_shape = [jax.ShapeDtypeStruct((4, planes, H, L), BF)]
    if not last:
        out_shape.append(jax.ShapeDtypeStruct((4, H, 2 * L), F32))
        out_shape.append(jax.ShapeDtypeStruct((4, H, L), F32))
    scratch = [
        pltpu.VMEM((H * E, L), F32),
        pltpu.VMEM((H * E, L), F32),
        pltpu.VMEM((E, H, 2 * L), BF),
        pltpu.VMEM((E, H, 2 * L), BF),
    ]
    if first:
        scratch.append(pltpu.VMEM((E, H, 2 * L), F32))
    operands = (scal, meta, jac, pz, ghost_m, ghost_p, pt) + extra
    in_specs = [smem(), smem(), pl.BlockSpec((1, W, E, W), lambda s: (start + s, 0, 0, 0))]
    in_specs += [vmem()] * (len(operands) - 3)
    return pl.pallas_call(
        functools.partial(pair_kernel, axis),
        grid=(steps,),
        in_specs=in_specs,
        out_specs=[vmem()] * len(out_shape),
        out_shape=out_shape,
        scratch_shapes=scratch,
        compiler_params=pltpu.CompilerParams(vmem_limit_bytes=VMEM_LIMIT),
        cost_estimate=pl.CostEstimate(
            flops=6_000_000_000, bytes_accessed=8_000_000, transcendentals=0
        ),
        name="pair_" + "xyz"[axis],
    )(*operands)


def final_kernel(scal, *refs):
    parts = [refs[6 * p : 6 * p + 6] for p in range(3)]
    coarse, restricted, s1, s2 = refs[18:]
    step = pl.program_id(0)
    lane = lax.broadcasted_iota(jnp.int32, (H, L), 1)
    layout = [
        [(0, 0), (0, 1), (1, 0), (1, 1)],
        [(2, 0), (2, 1), (4, 0), (4, 1)],
        [(4, 2), (4, 3), (5, 2), (5, 3)],
        [(5, 0), (5, 1), (3, 0), (3, 1)],
    ]

    def slot_of(y, d):
        return lax.rem(scal[2] - d + 4, 4) * 4 + y

    def fill(part, plane, dest, columns):
        acc = jnp.zeros((H, L), F32)
        for y in range(4):
            for d in range(4):
                which, row = layout[y][d]
                slot = slot_of(y, d)
                value = parts[part][which][row, plane].astype(F32)
                dest[pl.ds(slot, H, stride=16), :] = value
                if columns:
                    turned = pltpu.roll(value, lax.rem(slot - 49 + L, L), 1)
                    acc = jnp.where(lane == slot, turned, acc)
        return acc

    @pl.when(scal[4] == 0)
    def _():
        coarse[...] = jnp.zeros_like(coarse)
        restricted[...] = jnp.zeros_like(restricted)

    @pl.when(scal[4] == 1)
    def _():
        @pl.when(step == 0)
        def _():
            acc = fill(2, 3, s2, True)
            restricted[...] = acc.T[:16, :W].astype(BF)

        sources = [(2, 2), (0, 0), (0, 1), (1, 0), (1, 1), (2, 0), (2, 1)]
        for k in range(7):

            @pl.when(step == k)
            def _():
                fill(*sources[k], s1, False)

        turn = lax.rem(L - R * step, L)

        def write(i, carry):
            for u in range(5):
                row = i * 5 + u
                at = pl.ds(pl.multiple_of(row * 16, 16), 16)
                tail = pltpu.roll(s2[at, :], turn, 1)
                coarse[0, row] = jnp.concatenate([s1[at, :], tail[:, :R]], axis=1).astype(BF)
            return carry

        lax.fori_loop(0, W // 5, write, 0)


def final_call(scal, parts):
    operands = [scal] + [a for part in parts for a in part]
    return pl.pallas_call(
        final_kernel,
        grid=(7,),
        in_specs=[smem()] + [vmem()] * 18,
        out_specs=[pl.BlockSpec((1, W, 16, W), lambda s: (s, 0, 0, 0)), vmem()],
        out_shape=[jax.ShapeDtypeStruct((7, W, 16, W), BF), jax.ShapeDtypeStruct((16, W), BF)],
        scratch_shapes=[pltpu.VMEM((H * 16, L), F32), pltpu.VMEM((H * 16, L), F32)],
        compiler_params=pltpu.CompilerParams(vmem_limit_bytes=VMEM_LIMIT),
        name="assemble",
    )(*operands)


def ship(rows):
    near = [rows[0]]
    for d in range(1, 4):
        near.append(lax.ppermute(rows[d], "zz", [(i, (i + d) % 4) for i in range(4)]))
    low = jnp.stack(near[:2])
    high = jnp.stack(near[2:])
    down = lax.ppermute(low, "yy", [(1, 0), (2, 1)])
    up = lax.ppermute(high, "yy", [(3, 0), (2, 3)])
    down2 = lax.ppermute(jnp.concatenate([high, down]), "yy", [(1, 0)])
    up2 = lax.ppermute(jnp.concatenate([low, up]), "yy", [(3, 0)])
    return low, high, down, up, down2, up2


def body(jacobian, prolong, residual, neighbours, agg_map, owners):
    gx, gy = lax.axis_index("gx"), lax.axis_index("gy")
    zz, yy = lax.axis_index("zz"), lax.axis_index("yy")
    device = (gx * 4 + gy) * 16 + zz * 4 + yy
    scal = jnp.stack(
        [device * E, device * 4, zz, gx, (yy == 0).astype(jnp.int32)]
    ).astype(jnp.int32)
    jac = jnp.transpose(jacobian, (1, 2, 0, 3))
    pro = jnp.transpose(prolong, (1, 0, 2))
    res_t = jnp.pad(residual.T.astype(F32), ((0, 1), (0, L - E)))
    meta, pz, xs, ys, pt = pl.pallas_call(
        pack_kernel,
        in_specs=[smem()] * 4 + [vmem()],
        out_specs=[smem()] + [vmem()] * 4,
        out_shape=[
            jax.ShapeDtypeStruct((40,), jnp.int32),
            jax.ShapeDtypeStruct((2, 17, H, L), BF),
            jax.ShapeDtypeStruct((10, H, L), BF),
            jax.ShapeDtypeStruct((2, 10, H, L), BF),
            jax.ShapeDtypeStruct((E, H, H), BF),
        ],
        scratch_shapes=[pltpu.VMEM((H * E, L), F32), pltpu.VMEM((H * E, L), F32)],
        compiler_params=pltpu.CompilerParams(vmem_limit_bytes=VMEM_LIMIT),
        name="pack",
    )(scal, neighbours.T, agg_map, owners, pro)
    gz = ("zz", "yy")
    ghost_x = lax.ppermute(xs, "gx", [(0, 1), (1, 0)])
    ghost_zm = lax.ppermute(pz[1], gz, [(i, i + 1) for i in range(15)])
    ghost_zp = lax.ppermute(pz[0], gz, [(i + 1, i) for i in range(15)])
    ghost_ym = lax.ppermute(ys[1], "gy", [(i, i + 1) for i in range(3)])
    ghost_yp = lax.ppermute(ys[0], "gy", [(i + 1, i) for i in range(3)])
    rows_x, carry, rem = pair_call(0, scal, meta, jac, pz, ghost_x, ghost_x, pt, (res_t,))
    part_x = ship(rows_x)
    rows_y, carry, rem = pair_call(1, scal, meta, jac, pz, ghost_ym, ghost_yp, pt, (carry, rem))
    part_y = ship(rows_y)
    (rows_z,) = pair_call(2, scal, meta, jac, pz, ghost_zm, ghost_zp, pt, (carry, rem))
    part_z = ship(rows_z)
    coarse, restricted = final_call(scal, (part_x, part_y, part_z))
    return jnp.transpose(coarse, (2, 0, 1, 3)), restricted


def solution(mesh):
    fine = Mesh(mesh.devices.reshape(2, 4, 4, 4), ("gx", "gy", "zz", "yy"))
    every = ("gx", "gy", "zz", "yy")
    return jax.shard_map(
        body,
        mesh=fine,
        in_specs=(P(every), P(every), P(every), P(every), P(every), P(every)),
        out_specs=(P(every), P(every)),
        check_vma=False,
    )
```

time: 371 us -> 178 us (0.48)
  waiting for transfers between devices: 139 us -> 31.7 us
  matrix products: 107 us -> 0 us
  Pallas kernels: 0 us -> 91.1 us
  local copies, waits for them, and re-layouts: 89.2 us -> 8.08 us
  starting transfers between devices: 31.8 us -> 43.7 us
    all_to_all x2 -> x0, waiting for transfers between devices: 116 us -> none  [the longest x1 116 us: body(): lax.all_to_all(send_rows, 'gz', split_axis=0, concat_axis=0, tiled=True)]
    dot_general x8 -> x0, matrix products: 107 us -> none  [the longest x2 67.3 us: body(): jnp.einsum('ea,eds,edik->asik', agg_hot, slot_hot, triple, precision=lax....]
    pallas_call x0 -> x5, Pallas kernels: none -> 91.1 us  [the longest x3 59.4 us: pair_call(): pl.pallas_call(functools.partial(pair_kernel, axis), grid=(steps,), in_sp...]
    transpose x1 -> x0, local copies, waits for them, and re-layouts: 38.8 us -> none  [body(): jnp.einsum('eji,edjk->edik', prolong, products, preferred_element_type=jn...]
    ppermute x6 -> x26, starting transfers between devices: 14.7 us -> 43.7 us  [the longest x9 15.5 us: ship(): lax.ppermute(rows[d], 'zz', [(i, (i + d) % 4) for i in range(4)])]
    reshape x2 -> x0, local copies, waits for them, and re-layouts: 23.9 us -> none  [the longest x1 21.9 us: body(): gathered = gathered.reshape(elems, 7, width, width)]
    all_to_all x2 -> x0, starting transfers between devices: 17.1 us -> none  [the longest x1 9.4 us: body(): lax.all_to_all(send_rows, 'gz', split_axis=0, concat_axis=0, tiled=True)]
    unnamed x20 -> x45, local copies, waits for them, and re-layouts: 17.5 us -> 1.8 us
  transfers between devices with their start and end apart: 8 -> 26, of which waited for: 3 -> 8; matrix products, arithmetic and copies ran while one was open for 50% -> 4% of each run, Pallas kernels for 0% -> 34%
where the time goes in v1:
time: 178 us; the launch traced here: 177 us
  Pallas kernels  91.1 us (51%)
  starting transfers between devices  43.7 us (25%)
  waiting for transfers between devices  31.7 us (18%)
  local copies, waits for them, and re-layouts  8.08 us (5%)
    pallas_call x3, Pallas kernels, pair_call(): pl.pallas_call(functools.partial(pair_kernel, axis), grid=(steps,), in_sp...  59.4 us
    pallas_call x1, Pallas kernels, final_call(): pl.pallas_call(final_kernel, grid=(7,), in_specs=[smem()] + [vmem()] * 18...  21.4 us
    ppermute x3, waiting for transfers between devices, ship(): up2 = lax.ppermute(jnp.concatenate([low, up]), 'yy', [(3, 0)])  16.9 us
    ppermute x9, starting transfers between devices, ship(): lax.ppermute(rows[d], 'zz', [(i, (i + d) % 4) for i in range(4)])  15.5 us
    pallas_call x1, Pallas kernels, body(): pl.pallas_call(pack_kernel, in_specs=[smem()] * 4 + [vmem()], out_specs=[...  10.2 us
    ppermute x3, waiting for transfers between devices, ship(): down = lax.ppermute(low, 'yy', [(1, 0), (2, 1)])  6.35 us
    ppermute x1, starting transfers between devices, body(): ghost_ym = lax.ppermute(ys[1], 'gy', [(i, i + 1) for i in range(3)])  5.29 us
    ppermute x3, waiting for transfers between devices, ship(): down2 = lax.ppermute(jnp.concatenate([high, down]), 'yy', [(1, 0)])  4.63 us
  transfers between devices with their start and end apart: 26, of which 8 were waited for; matrix products, arithmetic and copies ran while one was open for 4% of the time, Pallas kernels for 34%

profile of v1, /device:TPU:0, one launch (start us, length us, event | category | flops | bytes accessed | tf_op | source)
XLA Modules:
  0.0 176.9 jit_solution(1204539268540043584)
XLA Ops:
  1.3 10.2 %pack.1 = (s32[40]{0:T(128)}, bf16[2,17,136,128]{3,2,1,0:T(8,128)(2,1)}, bf16[10,136,128]{2,1,0:T(8,128)(2,1)}, bf16[2,10,136,128]{3,2,1,0:T(8,128)(2,1)}, bf16[32,136,136]{2,1,0:T(8,128)(2,1)}) custom-call(s32[5]{0:T(128)} %stack.72.scal, s32[6,32]{1,0:T(8,128)} %bitcast.65, s32[32]{0:T(128)} %agg.1, s32[4]{0:T(128)} %own.1, bf16[135,32,135]{2,1,0:T(8,128)(2,1)} %bitcast.45), custom_call_target="tpu_custom_call" | custom-call | tf_op jit(solution)/shard_map/pack/pallas_call | solution.py:388
  12.8 1.3 collective-permute-start.9
  14.1 5.3 %collective-permute-start.8 = (bf16[10,136,128]{2,1,0:T(8,128)(2,1)S(1)}, bf16[10,136,128]{2,1,0:T(8,128)(2,1)}, u32[]{:S(2)}, u32[]{:S(2)}) collective-permute-start(bf16[10,136,128]{2,1,0:T(8,128)(2,1)S(1)} %get-tuple-element.31), channel_id=1, source_target_pairs={{0,16},{16,32},{32,48},{1,17},{17,33},{33,49},{2,18},{18,34},{34,5... | collective-permute-start | bytes 1044488 | tf_op jit(solution)/shard_map/ppermute | solution.py:407
  19.4 1.3 slice_bitcast_fusion
  20.7 1.3 collective-permute-start.18
  22.0 4.6 %collective-permute-start.17 = (bf16[17,136,128]{2,1,0:T(8,128)(2,1)S(1)}, bf16[17,136,128]{2,1,0:T(8,128)(2,1)S(1)}, u32[]{:S(2)}, u32[]{:S(2)}) collective-permute-start(bf16[17,136,128]{2,1,0:T(8,128)(2,1)S(1)} %get-tuple-element.29), channel_id=1, source_target_pairs={{0,1},{1,2},{2,3},{3,4},{4,5},{5,6},{6,7},{7,8},{8,9},{9,10},{10,1... | collective-permute-start | bytes 1775624 | tf_op jit(solution)/shard_map/ppermute | solution.py:405
  27.4 23.8 %pair_x.1 = (bf16[4,2,136,128]{3,2,1,0:T(8,128)(2,1)}, f32[4,136,256]{2,1,0:T(8,128)}, f32[4,136,128]{2,1,0:T(8,128)}) custom-call(s32[5]{0:T(128)} %stack.72.scal, s32[40]{0:T(128)} %get-tuple-element.15.meta, bf16[7,135,32,135]{3,2,1,0:T(8,128)(2,1)} %bitcast.66, bf16[2,17,136,128]{3,2,1,0:T(8,128)(2,1)} %get-tuple-element.16.pz, ...), custom_call_target="tpu_custom_call" | custom-call | flops 6000000000 | bytes 8000000 | tf_op jit(solution)/shard_map/pair_x/pallas_call | solution.py:276
  52.2 4.5 %collective-permute-start.2 = (bf16[2,136,128]{2,1,0:T(8,128)(2,1)S(1)}, bf16[2,136,128]{2,1,0:T(8,128)(2,1)S(1)}, u32[]{:S(2)}, u32[]{:S(2)}) collective-permute-start(bf16[2,136,128]{2,1,0:T(8,128)(2,1)S(1)} %get-tuple-element.40), channel_id=1, source_target_pairs={{0,8},{4,12},{8,0},{12,4},{1,9},{5,13},{9,1},{13,5},{2,10},{6,14},... | collective-permute-start | bytes 208904 | tf_op jit(solution)/shard_map/ppermute | solution.py:368
  57.5 1.3 collective-permute-start.1
  58.8 17.7 %pair_y.1 = (bf16[4,2,136,128]{3,2,1,0:T(8,128)(2,1)}, f32[4,136,256]{2,1,0:T(8,128)}, f32[4,136,128]{2,1,0:T(8,128)}) custom-call(s32[5]{0:T(128)} %stack.72.scal, s32[40]{0:T(128)} %get-tuple-element.15.meta, bf16[7,135,32,135]{3,2,1,0:T(8,128)(2,1)} %bitcast.67, bf16[2,17,136,128]{3,2,1,0:T(8,128)(2,1)} %get-tuple-element.16.pz, ...), custom_call_target="tpu_custom_call" | custom-call | flops 6000000000 | bytes 8000000 | tf_op jit(solution)/shard_map/pair_y/pallas_call | solution.py:276
  77.5 1.5 collective-permute-start.11
  79.0 2.6 %collective-permute-start.12 = (bf16[2,136,128]{2,1,0:T(8,128)(2,1)S(1)}, bf16[2,136,128]{2,1,0:T(8,128)(2,1)S(1)}, u32[]{:S(2)}, u32[]{:S(2)}) collective-permute-start(bf16[2,136,128]{2,1,0:T(8,128)(2,1)S(1)} %get-tuple-element.37), channel_id=1, source_target_pairs={{0,12},{4,0},{8,4},{12,8},{1,13},{5,1},{9,5},{13,9},{2,14},{6,2},{... | collective-permute-start | bytes 208904 | tf_op jit(solution)/shard_map/ppermute | solution.py:368
  81.7 1.3 collective-permute-start.5
  83.1 17.9 %pair_z.1 = bf16[4,4,136,128]{3,2,1,0:T(8,128)(2,1)} custom-call(s32[5]{0:T(128)} %stack.72.scal, s32[40]{0:T(128)} %get-tuple-element.15.meta, bf16[7,135,32,135]{3,2,1,0:T(8,128)(2,1)} %bitcast.68, bf16[2,17,136,128]{3,2,1,0:T(8,128)(2,1)} %get-tuple-element.16.pz, bf16[17,136,128]{2,1,0:T(8,128)(2,1)} %copy-done.20, bf16[17,136,128]{2,1,0:T(8,128)(2,1)} %copy-done.19, ...), custom_call_target="tpu_custom_call" | custom-call | flops 6000000000 | bytes 8000000 | tf_op jit(solution)/shard_map/pair_z/pallas_call | solution.py:276
  103.0 4.0 %collective-permute-start.20 = (bf16[4,136,128]{2,1,0:T(8,128)(2,1)S(1)}, bf16[4,136,128]{2,1,0:T(8,128)(2,1)S(1)}, u32[]{:S(2)}, u32[]{:S(2)}) collective-permute-start(bf16[4,136,128]{2,1,0:T(8,128)(2,1)S(1)} %get-tuple-element.32), channel_id=1, source_target_pairs={{0,8},{4,12},{8,0},{12,4},{1,9},{5,13},{9,1},{13,5},{2,10},{6,14},... | collective-permute-start | bytes 417800 | tf_op jit(solution)/shard_map/ppermute | solution.py:368
  107.0 2.9 %collective-permute-done.19 = bf16[4,136,128]{2,1,0:T(8,128)(2,1)S(1)} collective-permute-done((bf16[4,136,128]{2,1,0:T(8,128)(2,1)S(1)}, bf16[4,136,128]{2,1,0:T(8,128)(2,1)S(1)}, u32[]{:S(2)}, u32[]{:S(2)}) %collective-permute-start.19) | collective-permute-done | bytes 139296 | tf_op jit(solution)/shard_map/ppermute | solution.py:368
  109.9 1.3 collective-permute-start.4
  111.4 1.3 collective-permute-start.14
  112.7 1.3 collective-permute-start.22
  114.0 1.3 collective-permute-start.23
  115.3 3.0 %collective-permute-done.4.refs_2_ = bf16[2,2,136,128]{3,2,1,0:T(8,128)(2,1)S(1)} collective-permute-done((bf16[2,2,136,128]{3,2,1,0:T(8,128)(2,1)S(1)}, bf16[2,2,136,128]{3,2,1,0:T(8,128)(2,1)S(1)}, u32[]{:S(2)}, u32[]{:S(2)}) %collective-permute-start.4) | collective-permute-done | bytes 139296 | tf_op jit(solution)/shard_map/ppermute | solution.py:371
  118.3 1.3 collective-permute-start.13
  119.6 3.4 %collective-permute-done.22.refs_14_ = bf16[2,4,136,128]{3,2,1,0:T(8,128)(2,1)S(1)} collective-permute-done((bf16[2,4,136,128]{3,2,1,0:T(8,128)(2,1)S(1)}, bf16[2,4,136,128]{3,2,1,0:T(8,128)(2,1)S(1)}, u32[]{:S(2)}, u32[]{:S(2)}) %collective-permute-start.22) | collective-permute-done | bytes 278560 | tf_op jit(solution)/shard_map/ppermute | solution.py:371
  123.0 1.3 collective-permute-start.6
  126.5 1.3 collective-permute-start.25
  127.9 1.3 collective-permute-start.7
  129.2 1.3 collective-permute-start.15
  130.6 4.6 %collective-permute-done.6.refs_4_ = bf16[4,2,136,128]{3,2,1,0:T(8,128)(2,1)S(1)} collective-permute-done((bf16[4,2,136,128]{3,2,1,0:T(8,128)(2,1)S(1)}, bf16[4,2,136,128]{3,2,1,0:T(8,128)(2,1)S(1)}, u32[]{:S(2)}, u32[]{:S(2)}) %collective-permute-start.6) | collective-permute-done | bytes 278560 | tf_op jit(solution)/shard_map/ppermute | solution.py:373
  135.2 1.5 collective-permute-start.16
  136.7 13.9 %collective-permute-done.7.refs_5_ = bf16[4,2,136,128]{3,2,1,0:T(8,128)(2,1)S(1)} collective-permute-done((bf16[4,2,136,128]{3,2,1,0:T(8,128)(2,1)S(1)}, bf16[4,2,136,128]{3,2,1,0:T(8,128)(2,1)S(1)}, u32[]{:S(2)}, u32[]{:S(2)}) %collective-permute-start.7) | collective-permute-done | bytes 278560 | tf_op jit(solution)/shard_map/ppermute | solution.py:374
  150.6 3.0 %collective-permute-done.16.refs_11_ = bf16[4,2,136,128]{3,2,1,0:T(8,128)(2,1)S(1)} collective-permute-done((bf16[4,2,136,128]{3,2,1,0:T(8,128)(2,1)S(1)}, bf16[4,2,136,128]{3,2,1,0:T(8,128)(2,1)S(1)}, u32[]{:S(2)}, u32[]{:S(2)}) %collective-permute-start.16) | collective-permute-done | bytes 278560 | tf_op jit(solution)/shard_map/ppermute | solution.py:374
  155.3 21.4 %assemble.1 = (bf16[7,135,16,135]{3,2,1,0:T(8,128)(2,1)}, bf16[16,135]{1,0:T(8,128)(2,1)}) custom-call(s32[5]{0:T(128)} %stack.72.scal, bf16[2,2,136,128]{3,2,1,0:T(8,128)(2,1)} %copy-done.8, bf16[2,2,136,128]{3,2,1,0:T(8,128)(2,1)} %copy-done.6, bf16[2,2,136,128]{3,2,1,0:T(8,128)(2,1)} %copy-done.10, bf16[2,2,136,128]{3,2,1,0:T(8,128)(2,1)} %copy-done.7, ...), custom_call_target="tpu_custom_call" | custom-call | tf_op jit(solution)/shard_map/assemble/pallas_call | solution.py:353
  (89 shorter events, 11.7 us)
Async XLA Ops:
  11.6 15.8 %collective-permute-start = (bf16[10,136,128]{2,1,0:T(8,128)(2,1)}, bf16[10,136,128]{2,1,0:T(8,128)(2,1)}, u32[]{:S(2)}, u32[]{:S(2)}) collective-permute-start(bf16[10,136,128]{2,1,0:T(8,128)(2,1)} %get-tuple-element.17), channel_id=1, source_target_pairs={{0,64},{64,0},{1,65},{65,1},{2,66},{66,2},{3,67},{67,3},{4,68},{68... | collective-permute-start | bytes 1044488 | tf_op jit(solution)/shard_map/ppermute | solution.py:404
  12.8 43.9 %collective-permute-start.9 = (bf16[10,136,128]{2,1,0:T(8,128)(2,1)S(1)}, bf16[10,136,128]{2,1,0:T(8,128)(2,1)S(1)}, u32[]{:S(2)}, u32[]{:S(2)}) collective-permute-start(bf16[10,136,128]{2,1,0:T(8,128)(2,1)S(1)} %get-tuple-element.30), channel_id=1, source_target_pairs={{16,0},{32,16},{48,32},{17,1},{33,17},{49,33},{18,2},{34,18},{50,3... | collective-permute-start | bytes 1044488 | tf_op jit(solution)/shard_map/ppermute | solution.py:408
  14.1 43.4 %collective-permute-start.8 = (bf16[10,136,128]{2,1,0:T(8,128)(2,1)S(1)}, bf16[10,136,128]{2,1,0:T(8,128)(2,1)}, u32[]{:S(2)}, u32[]{:S(2)}) collective-permute-start(bf16[10,136,128]{2,1,0:T(8,128)(2,1)S(1)} %get-tuple-element.31), channel_id=1, source_target_pairs={{0,16},{16,32},{32,48},{1,17},{17,33},{33,49},{2,18},{18,34},{34,5... | collective-permute-start | bytes 1044488 | tf_op jit(solution)/shard_map/ppermute | solution.py:407
  20.7 60.9 %collective-permute-start.18 = (bf16[17,136,128]{2,1,0:T(8,128)(2,1)S(1)}, bf16[17,136,128]{2,1,0:T(8,128)(2,1)S(1)}, u32[]{:S(2)}, u32[]{:S(2)}) collective-permute-start(bf16[17,136,128]{2,1,0:T(8,128)(2,1)S(1)} %get-tuple-element.28), channel_id=1, source_target_pairs={{1,0},{2,1},{3,2},{4,3},{5,4},{6,5},{7,6},{8,7},{9,8},{10,9},{11,1... | collective-permute-start | bytes 1775624 | tf_op jit(solution)/shard_map/ppermute | solution.py:406
  22.0 59.7 %collective-permute-start.17 = (bf16[17,136,128]{2,1,0:T(8,128)(2,1)S(1)}, bf16[17,136,128]{2,1,0:T(8,128)(2,1)S(1)}, u32[]{:S(2)}, u32[]{:S(2)}) collective-permute-start(bf16[17,136,128]{2,1,0:T(8,128)(2,1)S(1)} %get-tuple-element.29), channel_id=1, source_target_pairs={{0,1},{1,2},{2,3},{3,4},{4,5},{5,6},{6,7},{7,8},{8,9},{9,10},{10,1... | collective-permute-start | bytes 1775624 | tf_op jit(solution)/shard_map/ppermute | solution.py:405
  52.2 25.2 %collective-permute-start.2 = (bf16[2,136,128]{2,1,0:T(8,128)(2,1)S(1)}, bf16[2,136,128]{2,1,0:T(8,128)(2,1)S(1)}, u32[]{:S(2)}, u32[]{:S(2)}) collective-permute-start(bf16[2,136,128]{2,1,0:T(8,128)(2,1)S(1)} %get-tuple-element.40), channel_id=1, source_target_pairs={{0,8},{4,12},{8,0},{12,4},{1,9},{5,13},{9,1},{13,5},{2,10},{6,14},... | collective-permute-start | bytes 208904 | tf_op jit(solution)/shard_map/ppermute | solution.py:368
  56.7 22.2 %collective-permute-start.3 = (bf16[2,136,128]{2,1,0:T(8,128)(2,1)S(1)}, bf16[2,136,128]{2,1,0:T(8,128)(2,1)S(1)}, u32[]{:S(2)}, u32[]{:S(2)}) collective-permute-start(bf16[2,136,128]{2,1,0:T(8,128)(2,1)S(1)} %get-tuple-element.41), channel_id=1, source_target_pairs={{0,12},{4,0},{8,4},{12,8},{1,13},{5,1},{9,5},{13,9},{2,14},{6,2},{... | collective-permute-start | bytes 208904 | tf_op jit(solution)/shard_map/ppermute | solution.py:368
  57.5 44.6 %collective-permute-start.1 = (bf16[2,136,128]{2,1,0:T(8,128)(2,1)S(1)}, bf16[2,136,128]{2,1,0:T(8,128)(2,1)S(1)}, u32[]{:S(2)}, u32[]{:S(2)}) collective-permute-start(bf16[2,136,128]{2,1,0:T(8,128)(2,1)S(1)} %get-tuple-element.42), channel_id=1, source_target_pairs={{0,4},{4,8},{8,12},{12,0},{1,5},{5,9},{9,13},{13,1},{2,6},{6,10},{... | collective-permute-start | bytes 208904 | tf_op jit(solution)/shard_map/ppermute | solution.py:368
  77.5 25.5 %collective-permute-start.11 = (bf16[2,136,128]{2,1,0:T(8,128)(2,1)S(1)}, bf16[2,136,128]{2,1,0:T(8,128)(2,1)S(1)}, u32[]{:S(2)}, u32[]{:S(2)}) collective-permute-start(bf16[2,136,128]{2,1,0:T(8,128)(2,1)S(1)} %get-tuple-element.36), channel_id=1, source_target_pairs={{0,8},{4,12},{8,0},{12,4},{1,9},{5,13},{9,1},{13,5},{2,10},{6,14},... | collective-permute-start | bytes 208904 | tf_op jit(solution)/shard_map/ppermute | solution.py:368
  79.0 28.0 %collective-permute-start.12 = (bf16[2,136,128]{2,1,0:T(8,128)(2,1)S(1)}, bf16[2,136,128]{2,1,0:T(8,128)(2,1)S(1)}, u32[]{:S(2)}, u32[]{:S(2)}) collective-permute-start(bf16[2,136,128]{2,1,0:T(8,128)(2,1)S(1)} %get-tuple-element.37), channel_id=1, source_target_pairs={{0,12},{4,0},{8,4},{12,8},{1,13},{5,1},{9,5},{13,9},{2,14},{6,2},{... | collective-permute-start | bytes 208904 | tf_op jit(solution)/shard_map/ppermute | solution.py:368
  81.6 32.4 %collective-permute-start.10 = (bf16[2,136,128]{2,1,0:T(8,128)(2,1)S(1)}, bf16[2,136,128]{2,1,0:T(8,128)(2,1)S(1)}, u32[]{:S(2)}, u32[]{:S(2)}) collective-permute-start(bf16[2,136,128]{2,1,0:T(8,128)(2,1)S(1)} %get-tuple-element.38), channel_id=1, source_target_pairs={{0,4},{4,8},{8,12},{12,0},{1,5},{5,9},{9,13},{13,1},{2,6},{6,10},{... | collective-permute-start | bytes 208904 | tf_op jit(solution)/shard_map/ppermute | solution.py:368
  81.7 44.8 %collective-permute-start.5 = (bf16[2,2,136,128]{3,2,1,0:T(8,128)(2,1)S(1)}, bf16[2,2,136,128]{3,2,1,0:T(8,128)(2,1)S(1)}, u32[]{:S(2)}, u32[]{:S(2)}) collective-permute-start(bf16[2,2,136,128]{3,2,1,0:T(8,128)(2,1)S(1)} %pad_maximum_fusion.9.refs_1_), channel_id=1, source_target_pairs={{3,0},{2,3},{7,4},{6,7},{11,8},{10,11},{15,12},{14,15},{19,16},{18... | collective-permute-start | bytes 417800 | tf_op jit(solution)/shard_map/ppermute | solution.py:372
  102.1 7.7 %collective-permute-start.19 = (bf16[4,136,128]{2,1,0:T(8,128)(2,1)S(1)}, bf16[4,136,128]{2,1,0:T(8,128)(2,1)S(1)}, u32[]{:S(2)}, u32[]{:S(2)}) collective-permute-start(bf16[4,136,128]{2,1,0:T(8,128)(2,1)S(1)} %get-tuple-element.34), channel_id=1, source_target_pairs={{0,4},{4,8},{8,12},{12,0},{1,5},{5,9},{9,13},{13,1},{2,6},{6,10},{... | collective-permute-start | bytes 417800 | tf_op jit(solution)/shard_map/ppermute | solution.py:368
  103.0 8.4 %collective-permute-start.20 = (bf16[4,136,128]{2,1,0:T(8,128)(2,1)S(1)}, bf16[4,136,128]{2,1,0:T(8,128)(2,1)S(1)}, u32[]{:S(2)}, u32[]{:S(2)}) collective-permute-start(bf16[4,136,128]{2,1,0:T(8,128)(2,1)S(1)} %get-tuple-element.32), channel_id=1, source_target_pairs={{0,8},{4,12},{8,0},{12,4},{1,9},{5,13},{9,1},{13,5},{2,10},{6,14},... | collective-permute-start | bytes 417800 | tf_op jit(solution)/shard_map/ppermute | solution.py:368
  107.0 5.7 %collective-permute-start.21 = (bf16[4,136,128]{2,1,0:T(8,128)(2,1)S(1)}, bf16[4,136,128]{2,1,0:T(8,128)(2,1)S(1)}, u32[]{:S(2)}, u32[]{:S(2)}) collective-permute-start(bf16[4,136,128]{2,1,0:T(8,128)(2,1)S(1)} %get-tuple-element.33), channel_id=1, source_target_pairs={{0,12},{4,0},{8,4},{12,8},{1,13},{5,1},{9,5},{13,9},{2,14},{6,2},{... | collective-permute-start | bytes 417800 | tf_op jit(solution)/shard_map/ppermute | solution.py:368
  109.9 8.5 %collective-permute-start.4 = (bf16[2,2,136,128]{3,2,1,0:T(8,128)(2,1)S(1)}, bf16[2,2,136,128]{3,2,1,0:T(8,128)(2,1)S(1)}, u32[]{:S(2)}, u32[]{:S(2)}) collective-permute-start(bf16[2,2,136,128]{3,2,1,0:T(8,128)(2,1)S(1)} %pad_maximum_fusion.8.refs_0_), channel_id=1, source_target_pairs={{1,0},{2,1},{5,4},{6,5},{9,8},{10,9},{13,12},{14,13},{17,16},{18,1... | collective-permute-start | bytes 417800 | tf_op jit(solution)/shard_map/ppermute | solution.py:371
  111.4 17.9 %collective-permute-start.14 = (bf16[2,2,136,128]{3,2,1,0:T(8,128)(2,1)S(1)}, bf16[2,2,136,128]{3,2,1,0:T(8,128)(2,1)S(1)}, u32[]{:S(2)}, u32[]{:S(2)}) collective-permute-start(bf16[2,2,136,128]{3,2,1,0:T(8,128)(2,1)S(1)} %pad_maximum_fusion.11.refs_7_), channel_id=1, source_target_pairs={{3,0},{2,3},{7,4},{6,7},{11,8},{10,11},{15,12},{14,15},{19,16},{18... | collective-permute-start | bytes 417800 | tf_op jit(solution)/shard_map/ppermute | solution.py:372
  112.7 10.4 %collective-permute-start.22 = (bf16[2,4,136,128]{3,2,1,0:T(8,128)(2,1)S(1)}, bf16[2,4,136,128]{3,2,1,0:T(8,128)(2,1)S(1)}, u32[]{:S(2)}, u32[]{:S(2)}) collective-permute-start(bf16[2,4,136,128]{3,2,1,0:T(8,128)(2,1)S(1)} %pad_maximum_fusion.6.refs_12_), channel_id=1, source_target_pairs={{1,0},{2,1},{5,4},{6,5},{9,8},{10,9},{13,12},{14,13},{17,16},{18,1... | collective-permute-start | bytes 835592 | tf_op jit(solution)/shard_map/ppermute | solution.py:371
  114.0 11.1 %collective-permute-start.23 = (bf16[2,4,136,128]{3,2,1,0:T(8,128)(2,1)S(1)}, bf16[2,4,136,128]{3,2,1,0:T(8,128)(2,1)S(1)}, u32[]{:S(2)}, u32[]{:S(2)}) collective-permute-start(bf16[2,4,136,128]{3,2,1,0:T(8,128)(2,1)S(1)} %pad_maximum_fusion.7.refs_13_), channel_id=1, source_target_pairs={{3,0},{2,3},{7,4},{6,7},{11,8},{10,11},{15,12},{14,15},{19,16},{18... | collective-permute-start | bytes 835592 | tf_op jit(solution)/shard_map/ppermute | solution.py:372
  115.3 38.3 %copy-start.12 = (bf16[2,2,136,128]{3,2,1,0:T(8,128)(2,1)}, bf16[2,2,136,128]{3,2,1,0:T(8,128)(2,1)S(1)}, u32[]{:S(2)}) copy-start(bf16[2,2,136,128]{3,2,1,0:T(8,128)(2,1)S(1)} %pad_maximum_fusion.10.refs_6_) | copy-start | bytes 417796
  118.3 35.3 %copy-start.10 = (bf16[2,2,136,128]{3,2,1,0:T(8,128)(2,1)}, bf16[2,2,136,128]{3,2,1,0:T(8,128)(2,1)S(1)}, u32[]{:S(2)}) copy-start(bf16[2,2,136,128]{3,2,1,0:T(8,128)(2,1)S(1)} %collective-permute-done.4.refs_2_) | copy-start | bytes 417796
  118.3 9.5 %collective-permute-start.13 = (bf16[2,2,136,128]{3,2,1,0:T(8,128)(2,1)S(1)}, bf16[2,2,136,128]{3,2,1,0:T(8,128)(2,1)S(1)}, u32[]{:S(2)}, u32[]{:S(2)}) collective-permute-start(bf16[2,2,136,128]{3,2,1,0:T(8,128)(2,1)S(1)} %pad_maximum_fusion.10.refs_6_), channel_id=1, source_target_pairs={{1,0},{2,1},{5,4},{6,5},{9,8},{10,9},{13,12},{14,13},{17,16},{18,1... | collective-permute-start | bytes 417800 | tf_op jit(solution)/shard_map/ppermute | solution.py:371
  123.0 30.6 %copy-start.1 = (bf16[2,4,136,128]{3,2,1,0:T(8,128)(2,1)}, bf16[2,4,136,128]{3,2,1,0:T(8,128)(2,1)S(1)}, u32[]{:S(2)}) copy-start(bf16[2,4,136,128]{3,2,1,0:T(8,128)(2,1)S(1)} %collective-permute-done.22.refs_14_) | copy-start | bytes 835588
  123.0 12.2 %collective-permute-start.6 = (bf16[4,2,136,128]{3,2,1,0:T(8,128)(2,1)S(1)}, bf16[4,2,136,128]{3,2,1,0:T(8,128)(2,1)S(1)}, u32[]{:S(2)}, u32[]{:S(2)}) collective-permute-start(bf16[4,2,136,128]{3,2,1,0:T(8,128)(2,1)S(1)} %pad_maximum_fusion.2), channel_id=1, source_target_pairs={{1,0},{5,4},{9,8},{13,12},{17,16},{21,20},{25,24},{29,28},{33,32},... | collective-permute-start | bytes 835592 | tf_op jit(solution)/shard_map/ppermute | solution.py:373
  125.1 28.6 %copy-start.3 = (bf16[2,4,136,128]{3,2,1,0:T(8,128)(2,1)}, bf16[2,4,136,128]{3,2,1,0:T(8,128)(2,1)S(1)}, u32[]{:S(2)}) copy-start(bf16[2,4,136,128]{3,2,1,0:T(8,128)(2,1)S(1)} %collective-permute-done.23.refs_15_) | copy-start | bytes 835588
  125.1 28.5 %collective-permute-start.24 = (bf16[4,4,136,128]{3,2,1,0:T(8,128)(2,1)S(1)}, bf16[4,4,136,128]{3,2,1,0:T(8,128)(2,1)S(1)}, u32[]{:S(2)}, u32[]{:S(2)}) collective-permute-start(bf16[4,4,136,128]{3,2,1,0:T(8,128)(2,1)S(1)} %pad_maximum_fusion), channel_id=1, source_target_pairs={{1,0},{5,4},{9,8},{13,12},{17,16},{21,20},{25,24},{29,28},{33,32},... | collective-permute-start | bytes 1671176 | tf_op jit(solution)/shard_map/ppermute | solution.py:373
  126.5 27.2 %copy-start.7 = (bf16[2,2,136,128]{3,2,1,0:T(8,128)(2,1)}, bf16[2,2,136,128]{3,2,1,0:T(8,128)(2,1)S(1)}, u32[]{:S(2)}) copy-start(bf16[2,2,136,128]{3,2,1,0:T(8,128)(2,1)S(1)} %collective-permute-done.5.refs_3_) | copy-start | bytes 417796
  126.5 27.1 %collective-permute-start.25 = (bf16[4,4,136,128]{3,2,1,0:T(8,128)(2,1)S(1)}, bf16[4,4,136,128]{3,2,1,0:T(8,128)(2,1)S(1)}, u32[]{:S(2)}, u32[]{:S(2)}) collective-permute-start(bf16[4,4,136,128]{3,2,1,0:T(8,128)(2,1)S(1)} %pad_maximum_fusion.1), channel_id=1, source_target_pairs={{3,0},{7,4},{11,8},{15,12},{19,16},{23,20},{27,24},{31,28},{35,32}... | collective-permute-start | bytes 1671176 | tf_op jit(solution)/shard_map/ppermute | solution.py:374
  127.9 25.8 %copy-start.13 = (bf16[2,2,136,128]{3,2,1,0:T(8,128)(2,1)}, bf16[2,2,136,128]{3,2,1,0:T(8,128)(2,1)S(1)}, u32[]{:S(2)}) copy-start(bf16[2,2,136,128]{3,2,1,0:T(8,128)(2,1)S(1)} %collective-permute-done.13.refs_8_) | copy-start | bytes 417796
  127.9 22.8 %collective-permute-start.7 = (bf16[4,2,136,128]{3,2,1,0:T(8,128)(2,1)S(1)}, bf16[4,2,136,128]{3,2,1,0:T(8,128)(2,1)S(1)}, u32[]{:S(2)}, u32[]{:S(2)}) collective-permute-start(bf16[4,2,136,128]{3,2,1,0:T(8,128)(2,1)S(1)} %pad_maximum_fusion.3), channel_id=1, source_target_pairs={{3,0},{7,4},{11,8},{15,12},{19,16},{23,20},{27,24},{31,28},{35,32}... | collective-permute-start | bytes 835592 | tf_op jit(solution)/shard_map/ppermute | solution.py:374
  129.2 21.4 %collective-permute-start.15 = (bf16[4,2,136,128]{3,2,1,0:T(8,128)(2,1)S(1)}, bf16[4,2,136,128]{3,2,1,0:T(8,128)(2,1)S(1)}, u32[]{:S(2)}, u32[]{:S(2)}) collective-permute-start(bf16[4,2,136,128]{3,2,1,0:T(8,128)(2,1)S(1)} %pad_maximum_fusion.4), channel_id=1, source_target_pairs={{1,0},{5,4},{9,8},{13,12},{17,16},{21,20},{25,24},{29,28},{33,32},... | collective-permute-start | bytes 835592 | tf_op jit(solution)/shard_map/ppermute | solution.py:373
  135.2 18.4 %collective-permute-start.16 = (bf16[4,2,136,128]{3,2,1,0:T(8,128)(2,1)S(1)}, bf16[4,2,136,128]{3,2,1,0:T(8,128)(2,1)S(1)}, u32[]{:S(2)}, u32[]{:S(2)}) collective-permute-start(bf16[4,2,136,128]{3,2,1,0:T(8,128)(2,1)S(1)} %pad_maximum_fusion.5), channel_id=1, source_target_pairs={{3,0},{7,4},{11,8},{15,12},{19,16},{23,20},{27,24},{31,28},{35,32}... | collective-permute-start | bytes 835592 | tf_op jit(solution)/shard_map/ppermute | solution.py:374
  (16 other events, 169.7 us)

commit v2 on v0

v2 whole, which is shorter than its diff:
```python
import functools

import jax
import jax.numpy as jnp
from jax import lax
from jax.experimental import pallas as pl
from jax.experimental.pallas import tpu as pltpu
from jax.sharding import Mesh, PartitionSpec as P

E = 32
W = 135
H = 136
L = 128
R = W - L
PE = 36
PS = 20
BF = jnp.bfloat16
F32 = jnp.float32
VMEM_LIMIT = 56 * 1024 * 1024


def smem():
    return pl.BlockSpec(memory_space=pltpu.SMEM)


def vmem():
    return pl.BlockSpec(memory_space=pltpu.VMEM)


def spread(block, main, rest):
    def step(i, carry):
        for u in range(5):
            row = i * 5 + u
            values = block(row).astype(F32)
            at = pl.ds(row * PE, E)
            main[at, :] = values[:, :L]
            rest[at, 0:R] = values[:, L:]
        return carry

    lax.fori_loop(0, W // 5, step, 0)


def clear(main, rest):
    main[W * PE : H * PE, :] = jnp.zeros((PE, L), F32)
    rest[...] = jnp.zeros((H * PE, L), F32)


def take(ref, element):
    return ref[pl.ds(element, H, stride=PE), :]


def pack_kernel(scal, nbr, agg, own, p_ref, meta, pz0, pz1, xs, ys0, ys1, pt, main, rest):
    pz, ys = (pz0, pz1), (ys0, ys1)
    base = scal[0]

    def place(e, carry):
        def near(direction):
            local = nbr[direction, e] - base
            here = (local >= 0) & (local < E)
            safe = jnp.clip(local, 0, E - 1)
            same = here & (agg[safe] == agg[e])
            return here.astype(jnp.int32), same.astype(jnp.int32)

        here_xm, odd_x = near(0)
        here_xp, _ = near(1)
        here_ym, odd_y = near(2)
        here_yp, _ = near(3)
        _, odd_z = near(4)
        agg_x = jnp.where(odd_x == 1, 1 - here_xp, here_xm)
        agg_y = jnp.where(odd_y == 1, 1 - here_yp, here_ym)
        meta[odd_z * 16 + (2 * agg_x + odd_x) * 4 + 2 * agg_y + odd_y] = e
        owner = own[agg[e] - scal[1]]
        meta[E + agg_x * 2 + agg_y] = owner // 4
        return carry

    lax.fori_loop(0, E, place, 0)
    clear(main, rest)
    spread(lambda row: p_ref[row], main, rest)
    for oz in range(2):
        plane = jnp.zeros((H, L), F32)
        for xy in range(16):
            e = meta[oz * 16 + xy]
            a = take(main, e)
            b = take(rest, e)
            pz[oz][xy] = a.astype(BF)
            plane = plane + (pltpu.roll(b, R * xy, 1) if xy else b)
            pt[oz * 16 + xy] = jnp.concatenate([a.T, b.T[:8]], axis=0).astype(BF)
        pz[oz][16] = plane.astype(BF)
    face = jnp.where(scal[3] == 0, 12, 0)
    for oz in range(2):
        for v in range(4):
            xs[oz * 4 + v] = pz[oz][face + v]
            ys[0][oz * 4 + v] = pz[oz][v * 4]
            ys[1][oz * 4 + v] = pz[oz][v * 4 + 3]
        xs[8 + oz] = pz[oz][16]
        ys[0][8 + oz] = pz[oz][16]
        ys[1][8 + oz] = pz[oz][16]


def pack_call(*operands):
    return pl.pallas_call(
        pack_kernel,
        in_specs=[smem()] * 4 + [vmem()],
        out_specs=[smem()] + [vmem()] * 6,
        out_shape=[
            jax.ShapeDtypeStruct((40,), jnp.int32),
            jax.ShapeDtypeStruct((17, H, L), BF),
            jax.ShapeDtypeStruct((17, H, L), BF),
            jax.ShapeDtypeStruct((10, H, L), BF),
            jax.ShapeDtypeStruct((10, H, L), BF),
            jax.ShapeDtypeStruct((10, H, L), BF),
            jax.ShapeDtypeStruct((E, H, H), BF),
        ],
        scratch_shapes=[pltpu.VMEM((H * PE, L), F32), pltpu.VMEM((H * PE, L), F32)],
        compiler_params=pltpu.CompilerParams(vmem_limit_bytes=VMEM_LIMIT),
        name="pack",
    )(*operands)


def block_kernel(kinds, scal, meta, jac, pz, ghosts, pt, res_t, rem_in, rows, rem_out, scratch):
    main, rest, x0, xs, keep = scratch
    step = pl.program_id(0)
    lane = lax.broadcasted_iota(jnp.int32, (H, L), 1)

    @pl.when(step == 0)
    def _():
        clear(main, rest)

    spread(lambda row: jac[0, row], main, rest)

    def product(c, plane_main, plane_rest, idx):
        e = meta[c]
        left = jnp.concatenate([take(main, e), take(rest, e)[:, :8]], axis=1).astype(BF)
        right = jnp.concatenate([plane_main, plane_rest], axis=1)
        out = jnp.dot(left, right, preferred_element_type=F32)
        low = R * idx
        good = (lane >= low) & (lane < low + R)
        return jnp.concatenate([out[:, :L], jnp.where(good, out[:, L:], 0.0)], axis=1)

    def where_is(q, octant):
        ax, ay = q // 2, lax.rem(q, 2)
        ox, oy, oz = octant // 4, octant // 2 % 2, octant % 2
        return 2 * ax + ox, 2 * ay + oy, oz

    def bits(octant):
        return octant // 4, octant // 2 % 2, octant % 2

    def direct(q):
        for octant in range(8):
            x, y, oz = where_is(q, octant)
            idx = x * 4 + y
            keep[q * 8 + octant] = product(oz * 16 + idx, pz[oz][idx], pz[oz][16], idx)

    def same(k, q):
        axis, shift = (k - 1) // 2, -1 if k % 2 else 1
        for octant in range(8):
            if bits(octant)[axis] != (1 if shift < 0 else 0):
                continue
            x, y, oz = where_is(q, octant)
            near = [x, y, oz]
            near[axis] = near[axis] + shift
            idx = near[0] * 4 + near[1]
            out = product(oz * 16 + x * 4 + y, pz[near[2]][idx], pz[near[2]][16], idx)
            out = out + keep[q * 8 + octant]
            if axis < 2:
                keep[q * 8 + octant] = out
            else:
                e = meta[oz * 16 + x * 4 + y]
                column = pltpu.roll(res_t[...], lax.rem(112 - e + L, L), 1)
                out = jnp.concatenate([out[:, :L], jnp.where(lane == 112, column, out[:, L:])], axis=1)
                x0[q * 8 + octant] = out.astype(BF)

    def outside(k, q):
        axis, shift = (k - 1) // 2, -1 if k % 2 else 1
        ghost = ghosts[k]
        for octant in range(8):
            if bits(octant)[axis] != (0 if shift < 0 else 1):
                continue
            x, y, oz = where_is(q, octant)
            c = oz * 16 + x * 4 + y
            if axis == 2:
                idx = x * 4 + y
                out = product(c, ghost[idx], ghost[16], idx)
                edge = 0 if shift < 0 else 15
                absent = scal[2] * 4 + scal[6] == edge
            else:
                along, other = (x, y) if axis == 0 else (y, x)
                spot = along + shift
                off = (spot < 0) | (spot > 3)
                spot = lax.rem(spot + 4, 4)
                idx = spot * 4 + other if axis == 0 else other * 4 + spot
                plane_main = jnp.where(off, ghost[oz * 4 + other], pz[oz][idx])
                plane_rest = jnp.where(off, ghost[8 + oz], pz[oz][16])
                out = product(c, plane_main, plane_rest, idx)
                edge = 0 if shift < 0 else (1, 3)[axis]
                absent = off & (scal[(3, 5)[axis]] == edge)
            xs[q * 8 + octant] = (out * jnp.where(absent, 0.0, 1.0)).astype(BF)

    def gather(ref, q, octants):
        acc = None
        for octant in octants:
            x, y, oz = where_is(q, octant)
            part = jnp.dot(pt[oz * 16 + x * 4 + y], ref[q * 8 + octant], preferred_element_type=F32)
            acc = part if acc is None else acc + part
        return acc

    def fold(raw, spots, slot):
        total = None
        for spot in spots:
            turned = pltpu.roll(raw, lax.rem(R * slot - R * spot + 2 * L, L), 1)
            total = turned if total is None else total + turned
        good = (lane >= R * slot) & (lane < R * slot + R)
        return jnp.where(good, total, 0.0)

    def finish_sides(axis, q):
        ax, ay = q // 2, lax.rem(q, 2)
        at = meta[E + q]
        remainder = (rem_out if axis == 1 else rem_in)[at]
        for side in range(2):
            acc = gather(xs, q, [o for o in range(8) if bits(o)[axis] == side])
            rows[at, 2 * (axis % 2) + side] = acc[:, :L].astype(BF)
            if axis == 0:
                nx = lax.rem(2 * ax + (-1 if side == 0 else 2) + 4, 4)
                spots = [nx * 4 + 2 * ay + v for v in range(2)]
            elif axis == 1:
                ny = lax.rem(2 * ay + (-1 if side == 0 else 2) + 4, 4)
                spots = [(2 * ax + v) * 4 + ny for v in range(2)]
            else:
                spots = [(2 * ax + v // 2) * 4 + 2 * ay + v % 2 for v in range(4)]
            remainder = remainder + fold(acc[:, L:], spots, 1 + 2 * axis + side)
        if axis == 2:
            rows[at, 2] = remainder.astype(BF)
        else:
            rem_out[at] = remainder

    def finish_centre(q):
        ax, ay = q // 2, lax.rem(q, 2)
        at = meta[E + q]
        acc = gather(x0, q, range(8))
        rows[at, 0] = acc[:, :L].astype(BF)
        raw = acc[:, L:]
        spots = [(2 * ax + v // 2) * 4 + 2 * ay + v % 2 for v in range(4)]
        moved = pltpu.roll(raw, 49 - 112 + L, 1)
        rem_out[at] = jnp.where(lane == 49, moved, fold(raw, spots, 0))

    for at_step, (k, outer) in enumerate(kinds):

        @pl.when(step == at_step)
        def _(k=k, outer=outer):
            def run(q, carry):
                if k == 0:
                    direct(q)
                elif outer:
                    outside(k, q)
                else:
                    same(k, q)
                if outer and k % 2 == 0:
                    finish_sides((k - 1) // 2, q)
                if k == 6 and not outer:
                    finish_centre(q)
                return carry

            lax.fori_loop(0, 4, run, 0)


SCRATCH = [
    pltpu.VMEM((H * PE, L), F32),
    pltpu.VMEM((H * PE, L), F32),
]
HALF = pltpu.VMEM((E, H, 2 * L), BF)
FULL = pltpu.VMEM((E, H, 2 * L), F32)
REST = jax.ShapeDtypeStruct((4, H, L), F32)


def centre_kernel(scal, meta, jac, pz0, pz1, pt, res_t, rows, rem_out, main, rest, x0, keep):
    block_kernel(
        [(k, False) for k in range(7)], scal, meta, jac, (pz0, pz1), {}, pt, res_t, None,
        rows, rem_out, (main, rest, x0, None, keep),
    )


def sides_kernel(
    scal, meta, jac, pz0, pz1, pt, gx, gym, gyp, rem_in, started, rows, rem_out, main, rest, xs
):
    block_kernel(
        [(k, True) for k in range(1, 5)], scal, meta, jac, (pz0, pz1),
        {1: gx, 2: gx, 3: gym, 4: gyp}, pt, None, rem_in,
        rows, rem_out, (main, rest, None, xs, None),
    )


def depth_kernel(scal, meta, jac, pt, gzm, gzp, rem_in, rows, main, rest, xs):
    block_kernel(
        [(k, True) for k in (5, 6)], scal, meta, jac, None,
        {5: gzm, 6: gzp}, pt, None, rem_in,
        rows, None, (main, rest, None, xs, None),
    )


def block_call(kernel, steps, start, operands, out_shape, out_specs, scratch, name, aliases, cost):
    in_specs = [smem(), smem(), pl.BlockSpec((1, W, E, W), lambda s: (start + s, 0, 0, 0))]
    in_specs += [vmem()] * (len(operands) - 3)
    if aliases:
        in_specs[-1] = pl.BlockSpec(memory_space=pl.ANY)
    return pl.pallas_call(
        kernel,
        grid=(steps,),
        in_specs=in_specs,
        out_specs=out_specs,
        out_shape=out_shape,
        scratch_shapes=SCRATCH + scratch,
        input_output_aliases=aliases,
        compiler_params=pltpu.CompilerParams(vmem_limit_bytes=VMEM_LIMIT),
        cost_estimate=pl.CostEstimate(flops=cost, bytes_accessed=1_000_000, transcendentals=0),
        name=name,
    )(*operands)


def final_kernel(scal, *refs):
    parts = [refs[5 * p : 5 * p + 5] for p in range(3)]
    coarse, restricted, s1, s2 = refs[15:]
    step = pl.program_id(0)
    lane = lax.broadcasted_iota(jnp.int32, (H, L), 1)

    def plane_of(part, slot):
        z, y = slot // 4, slot % 4
        which, row = [(0, z), (1, z), (3 + z // 2, z % 2), (2, z)][y]
        return parts[part][which][row, 0].astype(F32)

    @pl.when(scal[4] == 0)
    def _():
        coarse[...] = jnp.zeros_like(coarse)
        restricted[...] = jnp.zeros_like(restricted)

    @pl.when(scal[4] == 1)
    def _():
        @pl.when(step == 0)
        def _():
            acc = jnp.zeros((H, L), F32)
            for slot in range(16):
                turned = pltpu.roll(plane_of(2, slot), (slot - 49 + L) % L, 1)
                acc = jnp.where(lane == slot, turned, acc)
            restricted[...] = acc.T[:16, :W].astype(BF)

        for k in range(7):

            @pl.when(step == k)
            def _(k=k):
                for slot in range(16):
                    s1[pl.ds(slot, H, stride=PS), :] = plane_of(0 if k < 5 else 1, slot)
                    tail = plane_of(2, slot)
                    s2[pl.ds(slot, H, stride=PS), :] = pltpu.roll(tail, L - R * k, 1) if k else tail

        def write(i, carry):
            for u in range(9):
                row = i * 9 + u
                at = pl.ds(row * PS, 16)
                coarse[0, row] = jnp.concatenate([s1[at, :], s2[at, :R]], axis=1).astype(BF)
            return carry

        lax.fori_loop(0, W // 9, write, 0)


def final_call(scal, first, second):
    def plane_spec(array, index):
        return pl.BlockSpec((array.shape[0], 1, H, L), lambda s: (0, index(s), 0, 0))

    specs = [plane_spec(a, lambda s: jnp.where(s == 0, 4, jnp.minimum(s, 4) - 1)) for a in first]
    specs += [plane_spec(a, lambda s: jnp.maximum(s - 5, 0)) for a in second]
    specs += [plane_spec(a, lambda s: 2) for a in second]
    return pl.pallas_call(
        final_kernel,
        grid=(7,),
        in_specs=[smem()] + specs,
        out_specs=[pl.BlockSpec((1, W, 16, W), lambda s: (s, 0, 0, 0)), vmem()],
        out_shape=[jax.ShapeDtypeStruct((7, W, 16, W), BF), jax.ShapeDtypeStruct((16, W), BF)],
        scratch_shapes=[pltpu.VMEM((H * PS, L), F32), pltpu.VMEM((H * PS, L), F32)],
        compiler_params=pltpu.CompilerParams(vmem_limit_bytes=VMEM_LIMIT),
        name="assemble",
    )(scal, *first, *second, *second)


DOWN = [(1, 0), (2, 1), (3, 2), (0, 3)]
UP = [(3, 0), (0, 1), (1, 2), (2, 3)]


def to_owner_row(rows):
    return lax.all_to_all(rows, "zz", split_axis=0, concat_axis=0, tiled=True)


def along_ring(held):
    down = lax.ppermute(held, "yy", DOWN)
    up = lax.ppermute(held, "yy", UP)
    return down, up


def forward(down, up):
    return lax.ppermute(down[:2], "yy", [(1, 0)]), lax.ppermute(up[2:], "yy", [(3, 0)])


def body(jacobian, prolong, residual, neighbours, agg_map, owners):
    gx, gy = lax.axis_index("gx"), lax.axis_index("gy")
    zz, yy = lax.axis_index("zz"), lax.axis_index("yy")
    device = (gx * 4 + gy) * 16 + zz * 4 + yy
    scal = jnp.stack(
        [device * E, device * 4, zz, gx, (yy == 0).astype(jnp.int32), gy, yy]
    ).astype(jnp.int32)
    jac = jnp.transpose(jacobian, (1, 2, 0, 3))
    pro = jnp.transpose(prolong, (1, 0, 2))
    res_t = jnp.pad(residual.T.astype(F32), ((0, 1), (0, L - E)))
    meta, pz0, pz1, xs, ys0, ys1, pt = pack_call(scal, neighbours.T, agg_map, owners, pro)
    gz = ("zz", "yy")
    ghost_x = lax.ppermute(xs, "gx", [(0, 1), (1, 0)])
    ghost_zm = lax.ppermute(pz1, gz, [(i, (i + 1) % 16) for i in range(16)])
    ghost_zp = lax.ppermute(pz0, gz, [((i + 1) % 16, i) for i in range(16)])
    ghost_ym = lax.ppermute(ys1, "gy", [(i, (i + 1) % 4) for i in range(4)])
    ghost_yp = lax.ppermute(ys0, "gy", [((i + 1) % 4, i) for i in range(4)])
    five = jax.ShapeDtypeStruct((4, 5, H, L), BF)
    first, rem = block_call(
        centre_kernel, 7, 0, (scal, meta, jac, pz0, pz1, pt, res_t),
        [five, REST], [pl.BlockSpec((4, 1, H, L), lambda s: (0, 4, 0, 0)), vmem()],
        [HALF, FULL], "centre", {}, 18_000_000_000,
    )
    first, rem = block_call(
        sides_kernel, 4, 1,
        (scal, meta, jac, pz0, pz1, pt, ghost_x, ghost_ym, ghost_yp, rem, first),
        [five, REST], [pl.BlockSpec((4, 4, H, L), lambda s: (0, 0, 0, 0)), vmem()],
        [HALF], "sides", {10: 0}, 12_000_000_000,
    )
    held1 = to_owner_row(first)
    second = block_call(
        depth_kernel, 2, 5, (scal, meta, jac, pt, ghost_zm, ghost_zp, rem),
        jax.ShapeDtypeStruct((4, 3, H, L), BF), vmem(),
        [HALF], "depth", {}, 9_000_000_000,
    )
    held1, second = lax.optimization_barrier((held1, second))
    down1, up1 = along_ring(held1)
    held2 = to_owner_row(second)
    twice1 = forward(down1, up1)
    down2, up2 = along_ring(held2)
    twice2 = forward(down2, up2)
    coarse, restricted = final_call(scal, (held1, down1, up1) + twice1, (held2, down2, up2) + twice2)
    return jnp.transpose(coarse, (2, 0, 1, 3)), restricted


def solution(mesh):
    fine = Mesh(mesh.devices.reshape(2, 4, 4, 4), ("gx", "gy", "zz", "yy"))
    every = ("gx", "gy", "zz", "yy")
    return jax.shard_map(
        body,
        mesh=fine,
        in_specs=(P(every), P(every), P(every), P(every), P(every), P(every)),
        out_specs=(P(every), P(every)),
        check_vma=False,
    )
```

time: 371 us -> 114 us (0.31)
  waiting for transfers between devices: 139 us -> 18.2 us
  matrix products: 107 us -> 0 us
  local copies, waits for them, and re-layouts: 89.2 us -> 5.07 us
  Pallas kernels: 0 us -> 52.7 us
  blocking collectives: 0 us -> 10.9 us
  starting transfers between devices: 31.8 us -> 25.1 us
    all_to_all x2 -> x1, waiting for transfers between devices: 116 us -> 2.58 us  [to_owner_row(): return lax.all_to_all(rows, 'zz', split_axis=0, concat_axis=0, tiled=True)]
    dot_general x8 -> x0, matrix products: 107 us -> none  [the longest x2 67.3 us: body(): jnp.einsum('ea,eds,edik->asik', agg_hot, slot_hot, triple, precision=lax....]
    pallas_call x0 -> x5, Pallas kernels: none -> 52.7 us  [the longest x3 36.3 us: block_call(): pl.pallas_call(kernel, grid=(steps,), in_specs=in_specs, out_specs=out_sp...]
    transpose x1 -> x0, local copies, waits for them, and re-layouts: 38.8 us -> none  [body(): jnp.einsum('eji,edjk->edik', prolong, products, preferred_element_type=jn...]
    reshape x2 -> x0, local copies, waits for them, and re-layouts: 23.9 us -> none  [the longest x1 21.9 us: body(): gathered = gathered.reshape(elems, 7, width, width)]
    all_to_all x2 -> x1, starting transfers between devices: 17.1 us -> 3.49 us  [to_owner_row(): return lax.all_to_all(rows, 'zz', split_axis=0, concat_axis=0, tiled=True)]
    unnamed x20 -> x31, local copies, waits for them, and re-layouts: 17.5 us -> 4.36 us
    all_to_all x0 -> x1, blocking collectives: none -> 10.9 us  [to_owner_row(): return lax.all_to_all(rows, 'zz', split_axis=0, concat_axis=0, tiled=True)]
  transfers between devices with their start and end apart: 8 -> 14, of which waited for: 3 -> 4; matrix products, arithmetic and copies ran while one was open for 50% -> 1% of each run, Pallas kernels for 0% -> 32%
where the time goes in v2:
time: 114 us; the launch traced here: 113 us
  Pallas kernels  52.7 us (46%)
  starting transfers between devices  25.1 us (22%)
  waiting for transfers between devices  18.2 us (16%)
  blocking collectives  10.9 us (10%)
  local copies, waits for them, and re-layouts  5.07 us (4%)
    pallas_call x3, Pallas kernels, block_call(): pl.pallas_call(kernel, grid=(steps,), in_specs=in_specs, out_specs=out_sp...  36.3 us
    all_to_all x1, blocking collectives, to_owner_row(): return lax.all_to_all(rows, 'zz', split_axis=0, concat_axis=0, tiled=True)  10.9 us
    pallas_call x1, Pallas kernels, final_call(): pl.pallas_call(final_kernel, grid=(7,), in_specs=[smem()] + specs, out_sp...  9.35 us
    ppermute x2, waiting for transfers between devices, along_ring(): up = lax.ppermute(held, 'yy', UP)  8.61 us
    pallas_call x1, Pallas kernels, pack_call(): pl.pallas_call(pack_kernel, in_specs=[smem()] * 4 + [vmem()], out_specs=[...  6.97 us
    ppermute x2, waiting for transfers between devices, forward(): lax.ppermute(up[2:], 'yy', [(3, 0)])  6.94 us
    ppermute x1, starting transfers between devices, body(): ghost_zp = lax.ppermute(pz0, gz, [((i + 1) % 16, i) for i in range(16)])  6.57 us
    ppermute x2, starting transfers between devices, along_ring(): down = lax.ppermute(held, 'yy', DOWN)  6.47 us
  transfers between devices with their start and end apart: 14, of which 4 were waited for; matrix products, arithmetic and copies ran while one was open for 1% of the time, Pallas kernels for 32%

profile of v2, /device:TPU:0, one launch (start us, length us, event | category | flops | bytes accessed | tf_op | source)
XLA Modules:
  0.0 113.5 jit_solution(3562446131869919099)
XLA Ops:
  0.6 0.6 stack.35.scal
  1.3 7.0 %pack.1 = (s32[40]{0:T(128)}, bf16[17,136,128]{2,1,0:T(8,128)(2,1)}, bf16[17,136,128]{2,1,0:T(8,128)(2,1)}, bf16[10,136,128]{2,1,0:T(8,128)(2,1)}, bf16[10,136,1...) custom-call(s32[7]{0:T(128)} %stack.35.scal, s32[6,32]{1,0:T(8,128)} %bitcast.14, ...), custom_call_target="tpu_custom_call" | custom-call | tf_op jit(solution)/shard_map/pack/pallas_call | solution.py:101
  8.3 1.6 %collective-permute-start.1 = (bf16[10,136,128]{2,1,0:T(8,128)(2,1)}, bf16[10,136,128]{2,1,0:T(8,128)(2,1)S(1)}, u32[]{:S(2)}, u32[]{:S(2)}) collective-permute-start(bf16[10,136,128]{2,1,0:T(8,128)(2,1)} %get-tuple-element.22), channel_id=1, source_target_pairs={{0,16},{16,32},{32,48},{48,0},{1,17},{17,33},{33,49},{49,1},{2,18}... | collective-permute-start | bytes 1044488 | tf_op jit(solution)/shard_map/ppermute | solution.py:416
  10.0 1.7 %collective-permute-start.2 = (bf16[10,136,128]{2,1,0:T(8,128)(2,1)}, bf16[10,136,128]{2,1,0:T(8,128)(2,1)S(1)}, u32[]{:S(2)}, u32[]{:S(2)}) collective-permute-start(bf16[10,136,128]{2,1,0:T(8,128)(2,1)} %get-tuple-element.23), channel_id=1, source_target_pairs={{16,0},{32,16},{48,32},{0,48},{17,1},{33,17},{49,33},{1,49},{18,2}... | collective-permute-start | bytes 1044488 | tf_op jit(solution)/shard_map/ppermute | solution.py:417
  11.6 6.6 %collective-permute-start.4 = (bf16[17,136,128]{2,1,0:T(8,128)(2,1)}, bf16[17,136,128]{2,1,0:T(8,128)(2,1)S(1)}, u32[]{:S(2)}, u32[]{:S(2)}) collective-permute-start(bf16[17,136,128]{2,1,0:T(8,128)(2,1)} %get-tuple-element.18.pz0), channel_id=1, source_target_pairs={{1,0},{2,1},{3,2},{4,3},{5,4},{6,5},{7,6},{8,7},{9,8},{10,9},{11,1... | collective-permute-start | bytes 1775624 | tf_op jit(solution)/shard_map/ppermute | solution.py:415
  18.2 0.8 copy.9
  19.1 0.6 pad_convert_fusion.res_t
  19.7 16.2 %centre.1 = (bf16[4,5,136,128]{3,2,1,0:T(8,128)(2,1)}, f32[4,136,128]{2,1,0:T(8,128)}) custom-call(s32[7]{0:T(128)} %stack.35.scal, s32[40]{0:T(128)} %get-tuple-element.17.meta, bf16[7,135,32,135]{3,2,1,0:T(8,128)(2,1)} %bitcast.15, bf16[17,136,128]{2,1,0:T(8,128)(2,1)} %get-tuple-element.18.pz0, bf16[17,136,128]{2,1,0:T(8,128)(2,1)} %get-tuple-element.19.pz1, ...), custom_call_target="tpu_custom_call" | custom-call | flops 17999998976 | bytes 1000000 | tf_op jit(solution)/shard_map/centre/pallas_call | solution.py:305
  35.9 0.7 copy-done.12
  36.6 0.1 copy-done.13
  36.8 0.1 copy-done.14
  36.9 12.5 %sides.1 = (bf16[4,5,136,128]{3,2,1,0:T(8,128)(2,1)}, f32[4,136,128]{2,1,0:T(8,128)}) custom-call(s32[7]{0:T(128)} %stack.35.scal, s32[40]{0:T(128)} %get-tuple-element.17.meta, bf16[7,135,32,135]{3,2,1,0:T(8,128)(2,1)} %bitcast.16, bf16[17,136,128]{2,1,0:T(8,128)(2,1)} %get-tuple-element.18.pz0, ...), custom_call_target="tpu_custom_call", output_to_operand_aliasing={{0}: (10, {})} | custom-call | flops 12000000000 | bytes 1000000 | tf_op jit(solution)/shard_map/sides/pallas_call | solution.py:305
  49.4 3.5 %all-to-all-start = ((bf16[4,5,136,128]{3,2,1,0:T(8,128)(2,1)}), bf16[4,5,136,128]{3,2,1,0:T(8,128)(2,1)S(1)}, u32[]{:S(2)}, u32[]{:S(2)}) async-start(bf16[4,5,136,128]{3,2,1,0:T(8,128)(2,1)} %get-tuple-element.26), calls=%async_computation | async-start | bytes 1392640 | tf_op jit(solution)/shard_map/all_to_all | solution.py:388
  52.9 0.8 copy-done.10
  53.7 0.2 copy-done.11
  53.9 7.7 %depth.1 = bf16[4,3,136,128]{3,2,1,0:T(8,128)(2,1)} custom-call(s32[7]{0:T(128)} %stack.35.scal, s32[40]{0:T(128)} %get-tuple-element.17.meta, bf16[7,135,32,135]{3,2,1,0:T(8,128)(2,1)} %bitcast.17, bf16[32,136,136]{2,1,0:T(8,128)(2,1)} %get-tuple-element.20.pt, bf16[17,136,128]{2,1,0:T(8,128)(2,1)} %copy-done.11, bf16[17,136,128]{2,1,0:T(8,128)(2,1)} %copy-done.10, ...), custom_call_target="tpu_custom_call" | custom-call | flops 8999999488 | bytes 1000000 | tf_op jit(solution)/shard_map/depth/pallas_call | solution.py:305
  61.6 2.6 %all-to-all-done.refs_0_ = bf16[4,5,136,128]{3,2,1,0:T(8,128)(2,1)S(1)} async-done(((bf16[4,5,136,128]{3,2,1,0:T(8,128)(2,1)}), bf16[4,5,136,128]{3,2,1,0:T(8,128)(2,1)S(1)}, u32[]{:S(2)}, u32[]{:S(2)}) %all-to-all-start) | async-done | bytes 696352 | tf_op jit(solution)/shard_map/all_to_all | solution.py:388
  64.2 3.2 %collective-permute-start.5 = (bf16[4,5,136,128]{3,2,1,0:T(8,128)(2,1)S(1)}, bf16[4,5,136,128]{3,2,1,0:T(8,128)(2,1)S(1)}, u32[]{:S(2)}, u32[]{:S(2)}) collective-permute-start(bf16[4,5,136,128]{3,2,1,0:T(8,128)(2,1)S(1)} %all-to-all-done.refs_0_), channel_id=1, source_target_pairs={{1,0},{2,1},{3,2},{0,3},{5,4},{6,5},{7,6},{4,7},{9,8},{10,9},{11,1... | collective-permute-start | bytes 2088968 | tf_op jit(solution)/shard_map/ppermute | solution.py:392
  67.4 10.9 %all_to_all.10.refs_5_.refs_10_ = bf16[4,3,136,128]{3,2,1,0:T(8,128)(2,1)S(1)} all-to-all(bf16[4,3,136,128]{3,2,1,0:T(8,128)(2,1)} %depth.1), channel_id=1, replica_groups=mesh['gx'=2,'gy'=4,'zz'=4,'yy'=4] {'zz'}, dimensions={0} | all-to-all | bytes 835584 | tf_op jit(solution)/shard_map/all_to_all | solution.py:388
  78.4 3.2 %collective-permute-start.9 = (bf16[4,3,136,128]{3,2,1,0:T(8,128)(2,1)S(1)}, bf16[4,3,136,128]{3,2,1,0:T(8,128)(2,1)S(1)}, u32[]{:S(2)}, u32[]{:S(2)}) collective-permute-start(bf16[4,3,136,128]{3,2,1,0:T(8,128)(2,1)S(1)} %all_to_all.10.refs_5_.refs_10_), channel_id=1, source_target_pairs={{1,0},{2,1},{3,2},{0,3},{5,4},{6,5},{7,6},{4,7},{9,8},{10,9},{11,1... | collective-permute-start | bytes 1253384 | tf_op jit(solution)/shard_map/ppermute | solution.py:392
  81.6 2.3 %collective-permute-done.6.refs_2_ = bf16[4,5,136,128]{3,2,1,0:T(8,128)(2,1)S(1)} collective-permute-done((bf16[4,5,136,128]{3,2,1,0:T(8,128)(2,1)S(1)}, bf16[4,5,136,128]{3,2,1,0:T(8,128)(2,1)S(1)}, u32[]{:S(2)}, u32[]{:S(2)}) %collective-permute-start.6) | collective-permute-done | bytes 696352 | tf_op jit(solution)/shard_map/ppermute | solution.py:393
  84.0 1.3 %collective-permute-start.8 = (bf16[2,5,136,128]{3,2,1,0:T(8,128)(2,1)S(1)}, bf16[2,5,136,128]{3,2,1,0:T(8,128)(2,1)S(1)}, u32[]{:S(2)}, u32[]{:S(2)}) collective-permute-start(bf16[2,5,136,128]{3,2,1,0:T(8,128)(2,1)S(1)} %slice.17), channel_id=1, source_target_pairs={{3,0},{7,4},{11,8},{15,12},{19,16},{23,20},{27,24},{31,28},{35,32}... | collective-permute-start | bytes 1044488 | tf_op jit(solution)/shard_map/ppermute | solution.py:398
  85.3 1.3 %collective-permute-start.7 = (bf16[2,5,136,128]{3,2,1,0:T(8,128)(2,1)S(1)}, bf16[2,5,136,128]{3,2,1,0:T(8,128)(2,1)S(1)}, u32[]{:S(2)}, u32[]{:S(2)}) collective-permute-start(bf16[2,5,136,128]{3,2,1,0:T(8,128)(2,1)S(1)} %slice.16), channel_id=1, source_target_pairs={{1,0},{5,4},{9,8},{13,12},{17,16},{21,20},{25,24},{29,28},{33,32},... | collective-permute-start | bytes 1044488 | tf_op jit(solution)/shard_map/ppermute | solution.py:398
  86.6 6.3 %collective-permute-done.10.refs_7_.refs_12_ = bf16[4,3,136,128]{3,2,1,0:T(8,128)(2,1)S(1)} collective-permute-done((bf16[4,3,136,128]{3,2,1,0:T(8,128)(2,1)S(1)}, bf16[4,3,136,128]{3,2,1,0:T(8,128)(2,1)S(1)}, u32[]{:S(2)}, u32[]{:S(2)}) %collective-permute-start.10) | collective-permute-done | bytes 417824 | tf_op jit(solution)/shard_map/ppermute | solution.py:393
  92.9 1.3 %collective-permute-start.12 = (bf16[2,3,136,128]{3,2,1,0:T(8,128)(2,1)S(1)}, bf16[2,3,136,128]{3,2,1,0:T(8,128)(2,1)S(1)}, u32[]{:S(2)}, u32[]{:S(2)}) collective-permute-start(bf16[2,3,136,128]{3,2,1,0:T(8,128)(2,1)S(1)} %slice.19), channel_id=1, source_target_pairs={{3,0},{7,4},{11,8},{15,12},{19,16},{23,20},{27,24},{31,28},{35,32}... | collective-permute-start | bytes 626696 | tf_op jit(solution)/shard_map/ppermute | solution.py:398
  94.3 1.3 %collective-permute-start.11 = (bf16[2,3,136,128]{3,2,1,0:T(8,128)(2,1)S(1)}, bf16[2,3,136,128]{3,2,1,0:T(8,128)(2,1)S(1)}, u32[]{:S(2)}, u32[]{:S(2)}) collective-permute-start(bf16[2,3,136,128]{3,2,1,0:T(8,128)(2,1)S(1)} %slice.18), channel_id=1, source_target_pairs={{1,0},{5,4},{9,8},{13,12},{17,16},{21,20},{25,24},{29,28},{33,32},... | collective-permute-start | bytes 626696 | tf_op jit(solution)/shard_map/ppermute | solution.py:398
  95.6 6.9 %collective-permute-done.12.refs_9_.refs_14_ = bf16[2,3,136,128]{3,2,1,0:T(8,128)(2,1)S(1)} collective-permute-done((bf16[2,3,136,128]{3,2,1,0:T(8,128)(2,1)S(1)}, bf16[2,3,136,128]{3,2,1,0:T(8,128)(2,1)S(1)}, u32[]{:S(2)}, u32[]{:S(2)}) %collective-permute-start.12) | collective-permute-done | bytes 208928 | tf_op jit(solution)/shard_map/ppermute | solution.py:398
  102.6 0.6 copy-done.6
  103.2 0.1 copy-done.7
  103.3 0.1 copy-done.8
  103.4 0.7 copy-done.9
  104.1 9.3 %assemble.1 = (bf16[7,135,16,135]{3,2,1,0:T(8,128)(2,1)}, bf16[16,135]{1,0:T(8,128)(2,1)}) custom-call(s32[7]{0:T(128)} %stack.35.scal, bf16[4,5,136,128]{3,2,1,0:T(8,128)(2,1)} %copy-done.1, bf16[4,5,136,128]{3,2,1,0:T(8,128)(2,1)} %copy-done.5, bf16[4,5,136,128]{3,2,1,0:T(8,128)(2,1)} %copy-done.4, bf16[2,5,136,128]{3,2,1,0:T(8,128)(2,1)} %copy-done.9, ...), custom_call_target="tpu_custom_call" | custom-call | tf_op jit(solution)/shard_map/assemble/pallas_call | solution.py:371
  (39 shorter events, 0.2 us)
Async XLA Ops:
  8.2 27.6 %collective-permute-start = (bf16[10,136,128]{2,1,0:T(8,128)(2,1)}, bf16[10,136,128]{2,1,0:T(8,128)(2,1)S(1)}, u32[]{:S(2)}, u32[]{:S(2)}) collective-permute-start(bf16[10,136,128]{2,1,0:T(8,128)(2,1)} %get-tuple-element.21), channel_id=1, source_target_pairs={{0,64},{64,0},{1,65},{65,1},{2,66},{66,2},{3,67},{67,3},{4,68},{68... | collective-permute-start | bytes 1044488 | tf_op jit(solution)/shard_map/ppermute | solution.py:413
  8.3 27.6 %collective-permute-start.1 = (bf16[10,136,128]{2,1,0:T(8,128)(2,1)}, bf16[10,136,128]{2,1,0:T(8,128)(2,1)S(1)}, u32[]{:S(2)}, u32[]{:S(2)}) collective-permute-start(bf16[10,136,128]{2,1,0:T(8,128)(2,1)} %get-tuple-element.22), channel_id=1, source_target_pairs={{0,16},{16,32},{32,48},{48,0},{1,17},{17,33},{33,49},{49,1},{2,18}... | collective-permute-start | bytes 1044488 | tf_op jit(solution)/shard_map/ppermute | solution.py:416
  10.0 25.9 %collective-permute-start.2 = (bf16[10,136,128]{2,1,0:T(8,128)(2,1)}, bf16[10,136,128]{2,1,0:T(8,128)(2,1)S(1)}, u32[]{:S(2)}, u32[]{:S(2)}) collective-permute-start(bf16[10,136,128]{2,1,0:T(8,128)(2,1)} %get-tuple-element.23), channel_id=1, source_target_pairs={{16,0},{32,16},{48,32},{0,48},{17,1},{33,17},{49,33},{1,49},{18,2}... | collective-permute-start | bytes 1044488 | tf_op jit(solution)/shard_map/ppermute | solution.py:417
  11.6 41.2 %collective-permute-start.4 = (bf16[17,136,128]{2,1,0:T(8,128)(2,1)}, bf16[17,136,128]{2,1,0:T(8,128)(2,1)S(1)}, u32[]{:S(2)}, u32[]{:S(2)}) collective-permute-start(bf16[17,136,128]{2,1,0:T(8,128)(2,1)} %get-tuple-element.18.pz0), channel_id=1, source_target_pairs={{1,0},{2,1},{3,2},{4,3},{5,4},{6,5},{7,6},{8,7},{9,8},{10,9},{11,1... | collective-permute-start | bytes 1775624 | tf_op jit(solution)/shard_map/ppermute | solution.py:415
  18.2 34.7 %collective-permute-start.3 = (bf16[17,136,128]{2,1,0:T(8,128)(2,1)}, bf16[17,136,128]{2,1,0:T(8,128)(2,1)S(1)}, u32[]{:S(2)}, u32[]{:S(2)}) collective-permute-start(bf16[17,136,128]{2,1,0:T(8,128)(2,1)} %get-tuple-element.19.pz1), channel_id=1, source_target_pairs={{0,1},{1,2},{2,3},{3,4},{4,5},{5,6},{6,7},{7,8},{8,9},{9,10},{10,1... | collective-permute-start | bytes 1775624 | tf_op jit(solution)/shard_map/ppermute | solution.py:414
  35.9 0.7 copy-start.12
  35.9 0.9 copy-start.13
  35.9 1.0 copy-start.14
  49.4 14.8 %all-to-all-start = ((bf16[4,5,136,128]{3,2,1,0:T(8,128)(2,1)}), bf16[4,5,136,128]{3,2,1,0:T(8,128)(2,1)S(1)}, u32[]{:S(2)}, u32[]{:S(2)}) async-start(bf16[4,5,136,128]{3,2,1,0:T(8,128)(2,1)} %get-tuple-element.26), calls=%async_computation | async-start | bytes 1392640 | tf_op jit(solution)/shard_map/all_to_all | solution.py:388
  52.9 0.8 copy-start.10
  52.9 1.0 copy-start.11
  64.2 38.4 %copy-start.1 = (bf16[4,5,136,128]{3,2,1,0:T(8,128)(2,1)}, bf16[4,5,136,128]{3,2,1,0:T(8,128)(2,1)S(1)}, u32[]{:S(2)}) copy-start(bf16[4,5,136,128]{3,2,1,0:T(8,128)(2,1)S(1)} %all-to-all-done.refs_0_) | copy-start | bytes 2088964
  64.2 19.8 %collective-permute-start.6 = (bf16[4,5,136,128]{3,2,1,0:T(8,128)(2,1)S(1)}, bf16[4,5,136,128]{3,2,1,0:T(8,128)(2,1)S(1)}, u32[]{:S(2)}, u32[]{:S(2)}) collective-permute-start(bf16[4,5,136,128]{3,2,1,0:T(8,128)(2,1)S(1)} %all-to-all-done.refs_0_), channel_id=1, source_target_pairs={{3,0},{0,1},{1,2},{2,3},{7,4},{4,5},{5,6},{6,7},{11,8},{8,9},{9,10... | collective-permute-start | bytes 2088968 | tf_op jit(solution)/shard_map/ppermute | solution.py:393
  64.2 21.1 %collective-permute-start.5 = (bf16[4,5,136,128]{3,2,1,0:T(8,128)(2,1)S(1)}, bf16[4,5,136,128]{3,2,1,0:T(8,128)(2,1)S(1)}, u32[]{:S(2)}, u32[]{:S(2)}) collective-permute-start(bf16[4,5,136,128]{3,2,1,0:T(8,128)(2,1)S(1)} %all-to-all-done.refs_0_), channel_id=1, source_target_pairs={{1,0},{2,1},{3,2},{0,3},{5,4},{6,5},{7,6},{4,7},{9,8},{10,9},{11,1... | collective-permute-start | bytes 2088968 | tf_op jit(solution)/shard_map/ppermute | solution.py:392
  78.4 24.2 %copy-start = (bf16[4,3,136,128]{3,2,1,0:T(8,128)(2,1)}, bf16[4,3,136,128]{3,2,1,0:T(8,128)(2,1)S(1)}, u32[]{:S(2)}) copy-start(bf16[4,3,136,128]{3,2,1,0:T(8,128)(2,1)S(1)} %all_to_all.10.refs_5_.refs_10_) | copy-start | bytes 1253380
  78.4 14.5 %collective-permute-start.10 = (bf16[4,3,136,128]{3,2,1,0:T(8,128)(2,1)S(1)}, bf16[4,3,136,128]{3,2,1,0:T(8,128)(2,1)S(1)}, u32[]{:S(2)}, u32[]{:S(2)}) collective-permute-start(bf16[4,3,136,128]{3,2,1,0:T(8,128)(2,1)S(1)} %all_to_all.10.refs_5_.refs_10_), channel_id=1, source_target_pairs={{3,0},{0,1},{1,2},{2,3},{7,4},{4,5},{5,6},{6,7},{11,8},{8,9},{9,10... | collective-permute-start | bytes 1253384 | tf_op jit(solution)/shard_map/ppermute | solution.py:393
  78.4 15.9 %collective-permute-start.9 = (bf16[4,3,136,128]{3,2,1,0:T(8,128)(2,1)S(1)}, bf16[4,3,136,128]{3,2,1,0:T(8,128)(2,1)S(1)}, u32[]{:S(2)}, u32[]{:S(2)}) collective-permute-start(bf16[4,3,136,128]{3,2,1,0:T(8,128)(2,1)S(1)} %all_to_all.10.refs_5_.refs_10_), channel_id=1, source_target_pairs={{1,0},{2,1},{3,2},{0,3},{5,4},{6,5},{7,6},{4,7},{9,8},{10,9},{11,1... | collective-permute-start | bytes 1253384 | tf_op jit(solution)/shard_map/ppermute | solution.py:392
  83.9 18.6 %copy-start.4 = (bf16[4,5,136,128]{3,2,1,0:T(8,128)(2,1)}, bf16[4,5,136,128]{3,2,1,0:T(8,128)(2,1)S(1)}, u32[]{:S(2)}) copy-start(bf16[4,5,136,128]{3,2,1,0:T(8,128)(2,1)S(1)} %collective-permute-done.6.refs_2_) | copy-start | bytes 2088964
  84.0 18.5 %collective-permute-start.8 = (bf16[2,5,136,128]{3,2,1,0:T(8,128)(2,1)S(1)}, bf16[2,5,136,128]{3,2,1,0:T(8,128)(2,1)S(1)}, u32[]{:S(2)}, u32[]{:S(2)}) collective-permute-start(bf16[2,5,136,128]{3,2,1,0:T(8,128)(2,1)S(1)} %slice.17), channel_id=1, source_target_pairs={{3,0},{7,4},{11,8},{15,12},{19,16},{23,20},{27,24},{31,28},{35,32}... | collective-permute-start | bytes 1044488 | tf_op jit(solution)/shard_map/ppermute | solution.py:398
  85.3 17.3 %copy-start.5 = (bf16[4,5,136,128]{3,2,1,0:T(8,128)(2,1)}, bf16[4,5,136,128]{3,2,1,0:T(8,128)(2,1)S(1)}, u32[]{:S(2)}) copy-start(bf16[4,5,136,128]{3,2,1,0:T(8,128)(2,1)S(1)} %collective-permute-done.5.refs_1_) | copy-start | bytes 2088964
  85.3 17.2 %collective-permute-start.7 = (bf16[2,5,136,128]{3,2,1,0:T(8,128)(2,1)S(1)}, bf16[2,5,136,128]{3,2,1,0:T(8,128)(2,1)S(1)}, u32[]{:S(2)}, u32[]{:S(2)}) collective-permute-start(bf16[2,5,136,128]{3,2,1,0:T(8,128)(2,1)S(1)} %slice.16), channel_id=1, source_target_pairs={{1,0},{5,4},{9,8},{13,12},{17,16},{21,20},{25,24},{29,28},{33,32},... | collective-permute-start | bytes 1044488 | tf_op jit(solution)/shard_map/ppermute | solution.py:398
  92.9 9.7 %copy-start.2 = (bf16[4,3,136,128]{3,2,1,0:T(8,128)(2,1)}, bf16[4,3,136,128]{3,2,1,0:T(8,128)(2,1)S(1)}, u32[]{:S(2)}) copy-start(bf16[4,3,136,128]{3,2,1,0:T(8,128)(2,1)S(1)} %collective-permute-done.10.refs_7_.refs_12_) | copy-start | bytes 1253380
  92.9 9.6 %collective-permute-start.12 = (bf16[2,3,136,128]{3,2,1,0:T(8,128)(2,1)S(1)}, bf16[2,3,136,128]{3,2,1,0:T(8,128)(2,1)S(1)}, u32[]{:S(2)}, u32[]{:S(2)}) collective-permute-start(bf16[2,3,136,128]{3,2,1,0:T(8,128)(2,1)S(1)} %slice.19), channel_id=1, source_target_pairs={{3,0},{7,4},{11,8},{15,12},{19,16},{23,20},{27,24},{31,28},{35,32}... | collective-permute-start | bytes 626696 | tf_op jit(solution)/shard_map/ppermute | solution.py:398
  94.2 8.4 %copy-start.3 = (bf16[4,3,136,128]{3,2,1,0:T(8,128)(2,1)}, bf16[4,3,136,128]{3,2,1,0:T(8,128)(2,1)S(1)}, u32[]{:S(2)}) copy-start(bf16[4,3,136,128]{3,2,1,0:T(8,128)(2,1)S(1)} %collective-permute-done.9.refs_6_.refs_11_) | copy-start | bytes 1253380
  94.3 8.2 %collective-permute-start.11 = (bf16[2,3,136,128]{3,2,1,0:T(8,128)(2,1)S(1)}, bf16[2,3,136,128]{3,2,1,0:T(8,128)(2,1)S(1)}, u32[]{:S(2)}, u32[]{:S(2)}) collective-permute-start(bf16[2,3,136,128]{3,2,1,0:T(8,128)(2,1)S(1)} %slice.18), channel_id=1, source_target_pairs={{1,0},{5,4},{9,8},{13,12},{17,16},{21,20},{25,24},{29,28},{33,32},... | collective-permute-start | bytes 626696 | tf_op jit(solution)/shard_map/ppermute | solution.py:398
  102.5 0.7 copy-start.6
  102.5 0.8 copy-start.7
  102.5 0.9 copy-start.8
  103.4 0.7 copy-start.9

commit v3 on v2

--- a/solution.py
+++ b/solution.py
@@ -16,7 +16,11 @@
 PS = 20
 BF = jnp.bfloat16
 F32 = jnp.float32
-VMEM_LIMIT = 56 * 1024 * 1024
+VMEM_LIMIT = 40 * 1024 * 1024
+
+
+def anywhere():
+    return pl.BlockSpec(memory_space=pl.ANY)
 
 
 def smem():
@@ -117,16 +121,28 @@
     )(*operands)
 
 
-def block_kernel(kinds, scal, meta, jac, pz, ghosts, pt, res_t, rem_in, rows, rem_out, scratch):
-    main, rest, x0, xs, keep = scratch
-    step = pl.program_id(0)
+DEPTH = 3
+
+
+def block_kernel(kinds, scal, meta, jac, early, late, views, rows, rows_out, rem_out, rem_to, buffers):
+    jbuf, main, rest, x0, xs, keep, jac_sems, early_sems, late_sems, out_sems = buffers
+    pz, ghosts, pt, res_t, rem_in = views
     lane = lax.broadcasted_iota(jnp.int32, (H, L), 1)
 
-    @pl.when(step == 0)
-    def _():
-        clear(main, rest)
-
-    spread(lambda row: jac[0, row], main, rest)
+    def jac_copy(i):
+        return pltpu.make_async_copy(jac.at[kinds[i][0]], jbuf.at[i % DEPTH], jac_sems.at[i % DEPTH])
+
+    early_copies = [pltpu.make_async_copy(a, b, early_sems.at[i]) for i, (a, b) in enumerate(early)]
+    late_copies = [pltpu.make_async_copy(a, b, late_sems.at[i]) for i, (a, b) in enumerate(late)]
+    jac_copy(0).start()
+    for copy in early_copies:
+        copy.start()
+    jac_copy(1).start()
+    for copy in late_copies:
+        copy.start()
+    if len(kinds) > 2:
+        jac_copy(2).start()
+    clear(main, rest)
 
     def product(c, plane_main, plane_rest, idx):
         e = meta[c]
@@ -243,72 +259,97 @@
         moved = pltpu.roll(raw, 49 - 112 + L, 1)
         rem_out[at] = jnp.where(lane == 49, moved, fold(raw, spots, 0))
 
-    for at_step, (k, outer) in enumerate(kinds):
-
-        @pl.when(step == at_step)
-        def _(k=k, outer=outer):
-            def run(q, carry):
-                if k == 0:
-                    direct(q)
-                elif outer:
-                    outside(k, q)
-                else:
-                    same(k, q)
-                if outer and k % 2 == 0:
-                    finish_sides((k - 1) // 2, q)
-                if k == 6 and not outer:
-                    finish_centre(q)
-                return carry
-
-            lax.fori_loop(0, 4, run, 0)
-
-
-SCRATCH = [
+    for i, (k, outer) in enumerate(kinds):
+        jac_copy(i).wait()
+        spread(lambda row, i=i: jbuf[i % DEPTH, row], main, rest)
+        if i + DEPTH < len(kinds):
+            jac_copy(i + DEPTH).start()
+        if i == 0:
+            for copy in early_copies:
+                copy.wait()
+        if i == 1:
+            for copy in late_copies:
+                copy.wait()
+
+        def run(q, carry, k=k, outer=outer):
+            if k == 0:
+                direct(q)
+            elif outer:
+                outside(k, q)
+            else:
+                same(k, q)
+            if outer and k % 2 == 0:
+                finish_sides((k - 1) // 2, q)
+            if k == 6 and not outer:
+                finish_centre(q)
+            return carry
+
+        lax.fori_loop(0, 4, run, 0)
+    copies = [pltpu.make_async_copy(rows, rows_out, out_sems.at[0])]
+    if rem_out is not None:
+        copies.append(pltpu.make_async_copy(rem_out, rem_to, out_sems.at[1]))
+    for copy in copies:
+        copy.start()
+    for copy in copies:
+        copy.wait()
+
+
+COMMON = [
+    pltpu.VMEM((DEPTH, W, E, W), BF),
     pltpu.VMEM((H * PE, L), F32),
     pltpu.VMEM((H * PE, L), F32),
+    pltpu.SemaphoreType.DMA((DEPTH,)),
+    pltpu.SemaphoreType.DMA((6,)),
+    pltpu.SemaphoreType.DMA((6,)),
+    pltpu.SemaphoreType.DMA((2,)),
 ]
 HALF = pltpu.VMEM((E, H, 2 * L), BF)
 FULL = pltpu.VMEM((E, H, 2 * L), F32)
+REM = pltpu.VMEM((4, H, L), F32)
 REST = jax.ShapeDtypeStruct((4, H, L), F32)
 
 
-def centre_kernel(scal, meta, jac, pz0, pz1, pt, res_t, rows, rem_out, main, rest, x0, keep):
+def centre_kernel(scal, meta, jac, pz0, pz1, pt, res_t, rows_out, rem_to, *scratch):
+    jbuf, main, rest, j_sems, e_sems, l_sems, o_sems, x0, keep, vz0, vz1, vpt, vres, rows, rem_out = scratch
     block_kernel(
-        [(k, False) for k in range(7)], scal, meta, jac, (pz0, pz1), {}, pt, res_t, None,
-        rows, rem_out, (main, rest, x0, None, keep),
-    )
-
-
-def sides_kernel(
-    scal, meta, jac, pz0, pz1, pt, gx, gym, gyp, rem_in, started, rows, rem_out, main, rest, xs
-):
+        [(k, False) for k in range(7)], scal, meta, jac,
+        [(pz0, vz0), (pz1, vz1)], [(pt, vpt), (res_t, vres)],
+        ((vz0, vz1), {}, vpt, vres, None),
+        rows, rows_out.at[:, pl.ds(4, 1)], rem_out, rem_to,
+        (jbuf, main, rest, x0, None, keep, j_sems, e_sems, l_sems, o_sems),
+    )
+
+
+def sides_kernel(scal, meta, jac, pz0, pz1, pt, gx, gym, gyp, rem_in, started, rows_out, rem_to, *scratch):
+    jbuf, main, rest, j_sems, e_sems, l_sems, o_sems = scratch[:7]
+    xs, vz0, vz1, vpt, vx, vym, vyp, vrem, rows, rem_out = scratch[7:]
     block_kernel(
-        [(k, True) for k in range(1, 5)], scal, meta, jac, (pz0, pz1),
-        {1: gx, 2: gx, 3: gym, 4: gyp}, pt, None, rem_in,
-        rows, rem_out, (main, rest, None, xs, None),
-    )
-
-
-def depth_kernel(scal, meta, jac, pt, gzm, gzp, rem_in, rows, main, rest, xs):
+        [(k, True) for k in range(1, 5)], scal, meta, jac,
+        [(pz0, vz0), (pz1, vz1), (gx, vx)], [(pt, vpt), (rem_in, vrem), (gym, vym), (gyp, vyp)],
+        ((vz0, vz1), {1: vx, 2: vx, 3: vym, 4: vyp}, vpt, None, vrem),
+        rows, rows_out.at[:, pl.ds(0, 4)], rem_out, rem_to,
+        (jbuf, main, rest, None, xs, None, j_sems, e_sems, l_sems, o_sems),
+    )
+
+
+def depth_kernel(scal, meta, jac, pt, gzm, gzp, rem_in, rows_out, *scratch):
+    jbuf, main, rest, j_sems, e_sems, l_sems, o_sems, xs, vpt, vzm, vzp, vrem, rows = scratch
     block_kernel(
-        [(k, True) for k in (5, 6)], scal, meta, jac, None,
-        {5: gzm, 6: gzp}, pt, None, rem_in,
-        rows, None, (main, rest, None, xs, None),
-    )
-
-
-def block_call(kernel, steps, start, operands, out_shape, out_specs, scratch, name, aliases, cost):
-    in_specs = [smem(), smem(), pl.BlockSpec((1, W, E, W), lambda s: (start + s, 0, 0, 0))]
-    in_specs += [vmem()] * (len(operands) - 3)
-    if aliases:
-        in_specs[-1] = pl.BlockSpec(memory_space=pl.ANY)
+        [(k, True) for k in (5, 6)], scal, meta, jac,
+        [(gzm, vzm)], [(pt, vpt), (gzp, vzp), (rem_in, vrem)],
+        (None, {5: vzm, 6: vzp}, vpt, None, vrem),
+        rows, rows_out, None, None,
+        (jbuf, main, rest, None, xs, None, j_sems, e_sems, l_sems, o_sems),
+    )
+
+
+def block_call(kernel, operands, out_shape, scratch, name, aliases, cost):
     return pl.pallas_call(
         kernel,
-        grid=(steps,),
-        in_specs=in_specs,
-        out_specs=out_specs,
+        in_specs=[smem(), smem()] + [anywhere()] * (len(operands) - 2),
+        out_specs=jax.tree.map(lambda _: anywhere(), out_shape),
         out_shape=out_shape,
-        scratch_shapes=SCRATCH + scratch,
+        scratch_shapes=COMMON + scratch,
         input_output_aliases=aliases,
         compiler_params=pltpu.CompilerParams(vmem_limit_bytes=VMEM_LIMIT),
         cost_estimate=pl.CostEstimate(flops=cost, bytes_accessed=1_000_000, transcendentals=0),
@@ -317,67 +358,94 @@
 
 
 def final_kernel(scal, *refs):
-    parts = [refs[5 * p : 5 * p + 5] for p in range(3)]
-    coarse, restricted, s1, s2 = refs[15:]
-    step = pl.program_id(0)
+    sources = refs[:10]
+    coarse, restricted = refs[10:12]
+    held = refs[12:22]
+    out, s1, s2, in_sems, out_sems = refs[22:]
     lane = lax.broadcasted_iota(jnp.int32, (H, L), 1)
 
-    def plane_of(part, slot):
+    def copies(n):
+        part, plane = (0, n) if n < 5 else (1, n - 5)
+        return [
+            pltpu.make_async_copy(
+                sources[5 * part + i].at[:, plane], held[5 * part + i].at[:, plane], in_sems.at[n, i]
+            )
+            for i in range(5)
+        ]
+
+    def plane_of(n, slot):
+        part, plane = (0, n) if n < 5 else (1, n - 5)
         z, y = slot // 4, slot % 4
         which, row = [(0, z), (1, z), (3 + z // 2, z % 2), (2, z)][y]
-        return parts[part][which][row, 0].astype(F32)
+        return held[5 * part + which][row, plane].astype(F32)
+
+    def out_copy(k):
+        return pltpu.make_async_copy(out.at[k % 2], coarse.at[k], out_sems.at[k])
 
     @pl.when(scal[4] == 0)
     def _():
-        coarse[...] = jnp.zeros_like(coarse)
+        out[0] = jnp.zeros((W, 16, W), BF)
         restricted[...] = jnp.zeros_like(restricted)
+        zero_copies = [pltpu.make_async_copy(out.at[0], coarse.at[k], out_sems.at[k]) for k in range(7)]
+        for copy in zero_copies:
+            copy.start()
+        for copy in zero_copies:
+            copy.wait()
 
     @pl.when(scal[4] == 1)
     def _():
-        @pl.when(step == 0)
-        def _():
-            acc = jnp.zeros((H, L), F32)
+        order = [4, 0, 1, 2, 3, 5, 6]
+        for n in [7] + order:
+            for copy in copies(n):
+                copy.start()
+        for copy in copies(7):
+            copy.wait()
+        acc = jnp.zeros((H, L), F32)
+        for slot in range(16):
+            turned = pltpu.roll(plane_of(7, slot), (slot - 49 + L) % L, 1)
+            acc = jnp.where(lane == slot, turned, acc)
+        restricted[...] = acc.T[:16, :W].astype(BF)
+        for k in range(7):
+            for copy in copies(order[k]):
+                copy.wait()
             for slot in range(16):
-                turned = pltpu.roll(plane_of(2, slot), (slot - 49 + L) % L, 1)
-                acc = jnp.where(lane == slot, turned, acc)
-            restricted[...] = acc.T[:16, :W].astype(BF)
-
-        for k in range(7):
-
-            @pl.when(step == k)
-            def _(k=k):
-                for slot in range(16):
-                    s1[pl.ds(slot, H, stride=PS), :] = plane_of(0 if k < 5 else 1, slot)
-                    tail = plane_of(2, slot)
-                    s2[pl.ds(slot, H, stride=PS), :] = pltpu.roll(tail, L - R * k, 1) if k else tail
-
-        def write(i, carry):
-            for u in range(9):
-                row = i * 9 + u
-                at = pl.ds(row * PS, 16)
-                coarse[0, row] = jnp.concatenate([s1[at, :], s2[at, :R]], axis=1).astype(BF)
-            return carry
-
-        lax.fori_loop(0, W // 9, write, 0)
+                s1[pl.ds(slot, H, stride=PS), :] = plane_of(order[k], slot)
+                tail = plane_of(7, slot)
+                s2[pl.ds(slot, H, stride=PS), :] = pltpu.roll(tail, L - R * k, 1) if k else tail
+            if k >= 2:
+                out_copy(k - 2).wait()
+
+            def write(i, carry, k=k):
+                for u in range(9):
+                    row = i * 9 + u
+                    at = pl.ds(row * PS, 16)
+                    out[k % 2, row] = jnp.concatenate([s1[at, :], s2[at, :R]], axis=1).astype(BF)
+                return carry
+
+            lax.fori_loop(0, W // 9, write, 0)
+            out_copy(k).start()
+        out_copy(5).wait()
+        out_copy(6).wait()
 
 
 def final_call(scal, first, second):
-    def plane_spec(array, index):
-        return pl.BlockSpec((array.shape[0], 1, H, L), lambda s: (0, index(s), 0, 0))
-
-    specs = [plane_spec(a, lambda s: jnp.where(s == 0, 4, jnp.minimum(s, 4) - 1)) for a in first]
-    specs += [plane_spec(a, lambda s: jnp.maximum(s - 5, 0)) for a in second]
-    specs += [plane_spec(a, lambda s: 2) for a in second]
+    operands = [scal, *first, *second]
     return pl.pallas_call(
         final_kernel,
-        grid=(7,),
-        in_specs=[smem()] + specs,
-        out_specs=[pl.BlockSpec((1, W, 16, W), lambda s: (s, 0, 0, 0)), vmem()],
+        in_specs=[smem()] + [anywhere()] * 10,
+        out_specs=[anywhere(), vmem()],
         out_shape=[jax.ShapeDtypeStruct((7, W, 16, W), BF), jax.ShapeDtypeStruct((16, W), BF)],
-        scratch_shapes=[pltpu.VMEM((H * PS, L), F32), pltpu.VMEM((H * PS, L), F32)],
+        scratch_shapes=[pltpu.VMEM(a.shape, BF) for a in operands[1:]]
+        + [
+            pltpu.VMEM((2, W, 16, W), BF),
+            pltpu.VMEM((H * PS, L), F32),
+            pltpu.VMEM((H * PS, L), F32),
+            pltpu.SemaphoreType.DMA((8, 5)),
+            pltpu.SemaphoreType.DMA((7,)),
+        ],
         compiler_params=pltpu.CompilerParams(vmem_limit_bytes=VMEM_LIMIT),
         name="assemble",
-    )(scal, *first, *second, *second)
+    )(*operands)
 
 
 DOWN = [(1, 0), (2, 1), (3, 2), (0, 3)]
@@ -416,22 +484,24 @@
     ghost_ym = lax.ppermute(ys1, "gy", [(i, (i + 1) % 4) for i in range(4)])
     ghost_yp = lax.ppermute(ys0, "gy", [((i + 1) % 4, i) for i in range(4)])
     five = jax.ShapeDtypeStruct((4, 5, H, L), BF)
+    z_face, side_face = [pltpu.VMEM((n, H, L), BF) for n in (17, 10)]
+    turned = pltpu.VMEM((E, H, H), BF)
     first, rem = block_call(
-        centre_kernel, 7, 0, (scal, meta, jac, pz0, pz1, pt, res_t),
-        [five, REST], [pl.BlockSpec((4, 1, H, L), lambda s: (0, 4, 0, 0)), vmem()],
-        [HALF, FULL], "centre", {}, 18_000_000_000,
+        centre_kernel, (scal, meta, jac, pz0, pz1, pt, res_t), [five, REST],
+        [HALF, FULL, z_face, z_face, turned, pltpu.VMEM((H, L), F32), pltpu.VMEM((4, 1, H, L), BF), REM],
+        "centre", {}, 18_000_000_000,
     )
     first, rem = block_call(
-        sides_kernel, 4, 1,
-        (scal, meta, jac, pz0, pz1, pt, ghost_x, ghost_ym, ghost_yp, rem, first),
-        [five, REST], [pl.BlockSpec((4, 4, H, L), lambda s: (0, 0, 0, 0)), vmem()],
-        [HALF], "sides", {10: 0}, 12_000_000_000,
+        sides_kernel, (scal, meta, jac, pz0, pz1, pt, ghost_x, ghost_ym, ghost_yp, rem, first), [five, REST],
+        [HALF, z_face, z_face, turned, side_face, side_face, side_face, REM, pltpu.VMEM((4, 4, H, L), BF), REM],
+        "sides", {10: 0}, 12_000_000_000,
     )
     held1 = to_owner_row(first)
-    second = block_call(
-        depth_kernel, 2, 5, (scal, meta, jac, pt, ghost_zm, ghost_zp, rem),
-        jax.ShapeDtypeStruct((4, 3, H, L), BF), vmem(),
-        [HALF], "depth", {}, 9_000_000_000,
+    (second,) = block_call(
+        depth_kernel, (scal, meta, jac, pt, ghost_zm, ghost_zp, rem),
+        [jax.ShapeDtypeStruct((4, 3, H, L), BF)],
+        [HALF, turned, z_face, z_face, REM, pltpu.VMEM((4, 3, H, L), BF)],
+        "depth", {}, 9_000_000_000,
     )
     held1, second = lax.optimization_barrier((held1, second))
     down1, up1 = along_ring(held1)

time: 114 us -> 109 us (0.956)
  Pallas kernels: 52.7 us -> 45.7 us
  waiting for transfers between devices: 18.2 us -> 20.5 us
  local copies, waits for them, and re-layouts: 5.07 us -> 6.29 us
    pallas_call x4, Pallas kernels: 45.7 us -> 40.6 us  [the longest x3 32.1 us: block_call(): pl.pallas_call(kernel, in_specs=[smem(), smem()] + [anywhere()] * (len(op...]
    pallas_call x1, Pallas kernels: 6.97 us -> 5.07 us  [pack_call(): pl.pallas_call(pack_kernel, in_specs=[smem()] * 4 + [vmem()], out_specs=[...]
    unnamed x31 -> x13, local copies, waits for them, and re-layouts: 4.36 us -> 6.12 us
    all_to_all x1, waiting for transfers between devices: 2.58 us -> 3.82 us  [to_owner_row(): return lax.all_to_all(rows, 'zz', split_axis=0, concat_axis=0, tiled=True)]
  transfers between devices with their start and end apart: 14 -> 14, of which waited for: 4 -> 4; matrix products, arithmetic and copies ran while one was open for 1% -> 1% of each run, Pallas kernels for 32% -> 30%
where the time goes in v3:
time: 109 us; the launch traced here: 108 us
  Pallas kernels  45.7 us (42%)
  starting transfers between devices  25.1 us (23%)
  waiting for transfers between devices  20.5 us (19%)
  blocking collectives  9.86 us (9%)
  local copies, waits for them, and re-layouts  6.29 us (6%)
    pallas_call x3, Pallas kernels, block_call(): pl.pallas_call(kernel, in_specs=[smem(), smem()] + [anywhere()] * (len(op...  32.1 us
    all_to_all x1, blocking collectives, to_owner_row(): return lax.all_to_all(rows, 'zz', split_axis=0, concat_axis=0, tiled=True)  9.86 us
    ppermute x2, waiting for transfers between devices, along_ring(): up = lax.ppermute(held, 'yy', UP)  9.7 us
    pallas_call x1, Pallas kernels, final_call(): pl.pallas_call(final_kernel, in_specs=[smem()] + [anywhere()] * 10, out_s...  8.45 us
    ppermute x2, waiting for transfers between devices, forward(): lax.ppermute(up[2:], 'yy', [(3, 0)])  6.95 us
    ppermute x1, starting transfers between devices, body(): ghost_zp = lax.ppermute(pz0, gz, [((i + 1) % 16, i) for i in range(16)])  6.57 us
    ppermute x2, starting transfers between devices, along_ring(): down = lax.ppermute(held, 'yy', DOWN)  6.47 us
    unnamed x13, local copies, waits for them, and re-layouts  6.12 us
  transfers between devices with their start and end apart: 14, of which 4 were waited for; matrix products, arithmetic and copies ran while one was open for 1% of the time, Pallas kernels for 30%

profile of v3, /device:TPU:0, one launch (start us, length us, event | category | flops | bytes accessed | tf_op | source)
XLA Modules:
  0.0 108.3 jit_solution(2620203721862725387)
XLA Ops:
  0.6 0.1 stack.35.scal
  0.7 1.6 %copy-done = bf16[32,135,135]{2,0,1:T(8,128)(2,1)S(1)} copy-done((bf16[32,135,135]{2,0,1:T(8,128)(2,1)S(1)}, bf16[32,135,135]{2,0,1:T(8,128)(2,1)}, u32[]{:S(2)}) %copy-start) | copy-done | bytes 1166424
  2.4 0.7 copy-done.1
  3.0 0.7 copy-done.2
  3.7 0.7 copy-done.3
  4.4 5.1 %pack.1 = (s32[40]{0:T(128)S(1)}, bf16[17,136,128]{2,1,0:T(8,128)(2,1)}, bf16[17,136,128]{2,1,0:T(8,128)(2,1)}, bf16[10,136,128]{2,1,0:T(8,128)(2,1)}, bf16[10,1...) custom-call(s32[7]{0:T(128)S(1)} %stack.35.scal, ...), custom_call_target="tpu_custom_call" | custom-call | tf_op jit(solution)/shard_map/pack/pallas_call | solution.py:105
  9.4 0.1 collective-permute-start
  9.5 1.6 %collective-permute-start.1 = (bf16[10,136,128]{2,1,0:T(8,128)(2,1)S(1)}, bf16[10,136,128]{2,1,0:T(8,128)(2,1)}, u32[]{:S(2)}, u32[]{:S(2)}) collective-permute-start(bf16[10,136,128]{2,1,0:T(8,128)(2,1)S(1)} %get-tuple-element.22), channel_id=1, source_target_pairs={{0,16},{16,32},{32,48},{48,0},{1,17},{17,33},{33,49},{49,1},{2,18}... | collective-permute-start | bytes 1044488 | tf_op jit(solution)/shard_map/ppermute | solution.py:484
  11.2 1.7 %collective-permute-start.2 = (bf16[10,136,128]{2,1,0:T(8,128)(2,1)S(1)}, bf16[10,136,128]{2,1,0:T(8,128)(2,1)}, u32[]{:S(2)}, u32[]{:S(2)}) collective-permute-start(bf16[10,136,128]{2,1,0:T(8,128)(2,1)S(1)} %get-tuple-element.23), channel_id=1, source_target_pairs={{16,0},{32,16},{48,32},{0,48},{17,1},{33,17},{49,33},{1,49},{18,2}... | collective-permute-start | bytes 1044488 | tf_op jit(solution)/shard_map/ppermute | solution.py:485
  12.8 6.6 %collective-permute-start.4 = (bf16[17,136,128]{2,1,0:T(8,128)(2,1)}, bf16[17,136,128]{2,1,0:T(8,128)(2,1)}, u32[]{:S(2)}, u32[]{:S(2)}) collective-permute-start(bf16[17,136,128]{2,1,0:T(8,128)(2,1)} %get-tuple-element.18.pz0), channel_id=1, source_target_pairs={{1,0},{2,1},{3,2},{4,3},{5,4},{6,5},{7,6},{8,7},{9,8},{10,9},{11,1... | collective-permute-start | bytes 1775624 | tf_op jit(solution)/shard_map/ppermute | solution.py:483
  19.4 0.0 collective-permute-start.3
  19.4 0.8 copy.9
  20.3 14.3 %centre.1 = (bf16[4,5,136,128]{3,2,1,0:T(8,128)(2,1)}, f32[4,136,128]{2,1,0:T(8,128)S(1)}) custom-call(s32[7]{0:T(128)S(1)} %stack.35.scal, s32[40]{0:T(128)S(1)} %get-tuple-element.17.meta, bf16[7,135,32,135]{3,2,1,0:T(8,128)(2,1)} %bitcast.15, bf16[17,136,128]{2,1,0:T(8,128)(2,1)} %get-tuple-element.18.pz0, bf16[17,136,128]{2,1,0:T(8,128)(2,1)} %get-tuple-element.19.pz1, ...), custom_call_target="tpu_custom_call" | custom-call | flops 17999998976 | bytes 1000000 | tf_op jit(solution)/shard_map/centre/pallas_call | solution.py:347
  34.5 0.0 collective-permute-done.1.gym
  34.5 0.0 collective-permute-done.2.gyp
  34.6 11.3 %sides.1 = (bf16[4,5,136,128]{3,2,1,0:T(8,128)(2,1)}, f32[4,136,128]{2,1,0:T(8,128)S(1)}) custom-call(s32[7]{0:T(128)S(1)} %stack.35.scal, s32[40]{0:T(128)S(1)} %get-tuple-element.17.meta, bf16[7,135,32,135]{3,2,1,0:T(8,128)(2,1)} %bitcast.16, bf16[17,136,128]{2,1,0:T(8,128)(2,1)} %get-tuple-element.18.pz0, ...), custom_call_target="tpu_custom_call", output_to_operand_aliasing={{0}: (10, {})} | custom-call | flops 12000000000 | bytes 1000000 | tf_op jit(solution)/shard_map/sides/pallas_call | solution.py:347
  45.9 0.7 copy-done.4
  46.6 3.5 %all-to-all-start = ((bf16[4,5,136,128]{3,2,1,0:T(8,128)(2,1)}), bf16[4,5,136,128]{3,2,1,0:T(8,128)(2,1)S(1)}, u32[]{:S(2)}, u32[]{:S(2)}) async-start(bf16[4,5,136,128]{3,2,1,0:T(8,128)(2,1)} %get-tuple-element.26), calls=%async_computation | async-start | bytes 1392640 | tf_op jit(solution)/shard_map/all_to_all | solution.py:456
  50.2 0.9 copy-done.5
  51.1 6.5 %depth.1 = bf16[4,3,136,128]{3,2,1,0:T(8,128)(2,1)S(1)} custom-call(s32[7]{0:T(128)S(1)} %stack.35.scal, s32[40]{0:T(128)S(1)} %get-tuple-element.17.meta, bf16[7,135,32,135]{3,2,1,0:T(8,128)(2,1)} %bitcast.17, bf16[32,136,136]{2,1,0:T(8,128)(2,1)S(1)} %get-tuple-element.20.pt, bf16[17,136,128]{2,1,0:T(8,128)(2,1)} %collective-permute-done.3.gzm, ...), custom_call_target="tpu_custom_call" | custom-call | flops 8999999488 | bytes 1000000 | tf_op jit(solution)/shard_map/depth/pallas_call | solution.py:347
  57.7 3.8 %all-to-all-done.refs_0_ = bf16[4,5,136,128]{3,2,1,0:T(8,128)(2,1)S(1)} async-done(((bf16[4,5,136,128]{3,2,1,0:T(8,128)(2,1)}), bf16[4,5,136,128]{3,2,1,0:T(8,128)(2,1)S(1)}, u32[]{:S(2)}, u32[]{:S(2)}) %all-to-all-start) | async-done | bytes 696352 | tf_op jit(solution)/shard_map/all_to_all | solution.py:456
  61.5 3.2 %collective-permute-start.5 = (bf16[4,5,136,128]{3,2,1,0:T(8,128)(2,1)S(1)}, bf16[4,5,136,128]{3,2,1,0:T(8,128)(2,1)S(1)}, u32[]{:S(2)}, u32[]{:S(2)}) collective-permute-start(bf16[4,5,136,128]{3,2,1,0:T(8,128)(2,1)S(1)} %all-to-all-done.refs_0_), channel_id=1, source_target_pairs={{1,0},{2,1},{3,2},{0,3},{5,4},{6,5},{7,6},{4,7},{9,8},{10,9},{11,1... | collective-permute-start | bytes 2088968 | tf_op jit(solution)/shard_map/ppermute | solution.py:460
  64.7 9.9 %all_to_all.10.refs_5_ = bf16[4,3,136,128]{3,2,1,0:T(8,128)(2,1)S(1)} all-to-all(bf16[4,3,136,128]{3,2,1,0:T(8,128)(2,1)S(1)} %depth.1), channel_id=1, replica_groups=mesh['gx'=2,'gy'=4,'zz'=4,'yy'=4] {'zz'}, dimensions={0} | all-to-all | bytes 835584 | tf_op jit(solution)/shard_map/all_to_all | solution.py:456
  74.6 3.2 %collective-permute-start.9 = (bf16[4,3,136,128]{3,2,1,0:T(8,128)(2,1)S(1)}, bf16[4,3,136,128]{3,2,1,0:T(8,128)(2,1)S(1)}, u32[]{:S(2)}, u32[]{:S(2)}) collective-permute-start(bf16[4,3,136,128]{3,2,1,0:T(8,128)(2,1)S(1)} %all_to_all.10.refs_5_), channel_id=1, source_target_pairs={{1,0},{2,1},{3,2},{0,3},{5,4},{6,5},{7,6},{4,7},{9,8},{10,9},{11,1... | collective-permute-start | bytes 1253384 | tf_op jit(solution)/shard_map/ppermute | solution.py:460
  77.8 3.4 %collective-permute-done.6.refs_2_ = bf16[4,5,136,128]{3,2,1,0:T(8,128)(2,1)S(1)} collective-permute-done((bf16[4,5,136,128]{3,2,1,0:T(8,128)(2,1)S(1)}, bf16[4,5,136,128]{3,2,1,0:T(8,128)(2,1)S(1)}, u32[]{:S(2)}, u32[]{:S(2)}) %collective-permute-start.6) | collective-permute-done | bytes 696352 | tf_op jit(solution)/shard_map/ppermute | solution.py:461
  81.3 1.3 %collective-permute-start.8 = (bf16[2,5,136,128]{3,2,1,0:T(8,128)(2,1)S(1)}, bf16[2,5,136,128]{3,2,1,0:T(8,128)(2,1)S(1)}, u32[]{:S(2)}, u32[]{:S(2)}) collective-permute-start(bf16[2,5,136,128]{3,2,1,0:T(8,128)(2,1)S(1)} %slice.17), channel_id=1, source_target_pairs={{3,0},{7,4},{11,8},{15,12},{19,16},{23,20},{27,24},{31,28},{35,32}... | collective-permute-start | bytes 1044488 | tf_op jit(solution)/shard_map/ppermute | solution.py:466
  82.6 1.3 %collective-permute-start.7 = (bf16[2,5,136,128]{3,2,1,0:T(8,128)(2,1)S(1)}, bf16[2,5,136,128]{3,2,1,0:T(8,128)(2,1)S(1)}, u32[]{:S(2)}, u32[]{:S(2)}) collective-permute-start(bf16[2,5,136,128]{3,2,1,0:T(8,128)(2,1)S(1)} %slice.16), channel_id=1, source_target_pairs={{1,0},{5,4},{9,8},{13,12},{17,16},{21,20},{25,24},{29,28},{33,32},... | collective-permute-start | bytes 1044488 | tf_op jit(solution)/shard_map/ppermute | solution.py:466
  83.9 6.3 %collective-permute-done.10.refs_7_ = bf16[4,3,136,128]{3,2,1,0:T(8,128)(2,1)S(1)} collective-permute-done((bf16[4,3,136,128]{3,2,1,0:T(8,128)(2,1)S(1)}, bf16[4,3,136,128]{3,2,1,0:T(8,128)(2,1)S(1)}, u32[]{:S(2)}, u32[]{:S(2)}) %collective-permute-start.10) | collective-permute-done | bytes 417824 | tf_op jit(solution)/shard_map/ppermute | solution.py:461
  90.2 1.3 %collective-permute-start.12 = (bf16[2,3,136,128]{3,2,1,0:T(8,128)(2,1)S(1)}, bf16[2,3,136,128]{3,2,1,0:T(8,128)(2,1)S(1)}, u32[]{:S(2)}, u32[]{:S(2)}) collective-permute-start(bf16[2,3,136,128]{3,2,1,0:T(8,128)(2,1)S(1)} %slice.19), channel_id=1, source_target_pairs={{3,0},{7,4},{11,8},{15,12},{19,16},{23,20},{27,24},{31,28},{35,32}... | collective-permute-start | bytes 626696 | tf_op jit(solution)/shard_map/ppermute | solution.py:466
  91.5 1.3 %collective-permute-start.11 = (bf16[2,3,136,128]{3,2,1,0:T(8,128)(2,1)S(1)}, bf16[2,3,136,128]{3,2,1,0:T(8,128)(2,1)S(1)}, u32[]{:S(2)}, u32[]{:S(2)}) collective-permute-start(bf16[2,3,136,128]{3,2,1,0:T(8,128)(2,1)S(1)} %slice.18), channel_id=1, source_target_pairs={{1,0},{5,4},{9,8},{13,12},{17,16},{21,20},{25,24},{29,28},{33,32},... | collective-permute-start | bytes 626696 | tf_op jit(solution)/shard_map/ppermute | solution.py:466
  92.8 7.0 %collective-permute-done.12.refs_9_ = bf16[2,3,136,128]{3,2,1,0:T(8,128)(2,1)S(1)} collective-permute-done((bf16[2,3,136,128]{3,2,1,0:T(8,128)(2,1)S(1)}, bf16[2,3,136,128]{3,2,1,0:T(8,128)(2,1)S(1)}, u32[]{:S(2)}, u32[]{:S(2)}) %collective-permute-start.12) | collective-permute-done | bytes 208928 | tf_op jit(solution)/shard_map/ppermute | solution.py:466
  99.8 8.4 %assemble.1 = (bf16[7,135,16,135]{3,2,1,0:T(8,128)(2,1)}, bf16[16,135]{1,0:T(8,128)(2,1)}) custom-call(s32[7]{0:T(128)S(1)} %stack.35.scal, bf16[4,5,136,128]{3,2,1,0:T(8,128)(2,1)S(1)} %all-to-all-done.refs_0_, bf16[4,5,136,128]{3,2,1,0:T(8,128)(2,1)S(1)} %collective-permute-done.5.refs_1_, bf16[4,5,136,128]{3,2,1,0:T(8,128)(2,1)S(1)} %collective-permute-done.6.refs_2_, ...), custom_call_target="tpu_custom_call" | custom-call | tf_op jit(solution)/shard_map/assemble/pallas_call | solution.py:433
  (21 shorter events, 0.1 us)
Async XLA Ops:
  0.7 1.6 %copy-start = (bf16[32,135,135]{2,0,1:T(8,128)(2,1)S(1)}, bf16[32,135,135]{2,0,1:T(8,128)(2,1)}, u32[]{:S(2)}) copy-start(bf16[32,135,135]{2,0,1:T(8,128)(2,1)} %param.7) | copy-start | bytes 3499204
  2.4 0.7 copy-start.1
  3.0 0.7 copy-start.2
  3.7 0.7 copy-start.3
  9.4 25.1 %collective-permute-start = (bf16[10,136,128]{2,1,0:T(8,128)(2,1)}, bf16[10,136,128]{2,1,0:T(8,128)(2,1)S(1)}, u32[]{:S(2)}, u32[]{:S(2)}) collective-permute-start(bf16[10,136,128]{2,1,0:T(8,128)(2,1)} %get-tuple-element.21), channel_id=1, source_target_pairs={{0,64},{64,0},{1,65},{65,1},{2,66},{66,2},{3,67},{67,3},{4,68},{68... | collective-permute-start | bytes 1044488 | tf_op jit(solution)/shard_map/ppermute | solution.py:481
  9.5 25.0 %collective-permute-start.1 = (bf16[10,136,128]{2,1,0:T(8,128)(2,1)S(1)}, bf16[10,136,128]{2,1,0:T(8,128)(2,1)}, u32[]{:S(2)}, u32[]{:S(2)}) collective-permute-start(bf16[10,136,128]{2,1,0:T(8,128)(2,1)S(1)} %get-tuple-element.22), channel_id=1, source_target_pairs={{0,16},{16,32},{32,48},{48,0},{1,17},{17,33},{33,49},{49,1},{2,18}... | collective-permute-start | bytes 1044488 | tf_op jit(solution)/shard_map/ppermute | solution.py:484
  11.2 23.4 %collective-permute-start.2 = (bf16[10,136,128]{2,1,0:T(8,128)(2,1)S(1)}, bf16[10,136,128]{2,1,0:T(8,128)(2,1)}, u32[]{:S(2)}, u32[]{:S(2)}) collective-permute-start(bf16[10,136,128]{2,1,0:T(8,128)(2,1)S(1)} %get-tuple-element.23), channel_id=1, source_target_pairs={{16,0},{32,16},{48,32},{0,48},{17,1},{33,17},{49,33},{1,49},{18,2}... | collective-permute-start | bytes 1044488 | tf_op jit(solution)/shard_map/ppermute | solution.py:485
  12.8 37.3 %collective-permute-start.4 = (bf16[17,136,128]{2,1,0:T(8,128)(2,1)}, bf16[17,136,128]{2,1,0:T(8,128)(2,1)}, u32[]{:S(2)}, u32[]{:S(2)}) collective-permute-start(bf16[17,136,128]{2,1,0:T(8,128)(2,1)} %get-tuple-element.18.pz0), channel_id=1, source_target_pairs={{1,0},{2,1},{3,2},{4,3},{5,4},{6,5},{7,6},{8,7},{9,8},{10,9},{11,1... | collective-permute-start | bytes 1775624 | tf_op jit(solution)/shard_map/ppermute | solution.py:483
  19.4 30.7 %collective-permute-start.3 = (bf16[17,136,128]{2,1,0:T(8,128)(2,1)}, bf16[17,136,128]{2,1,0:T(8,128)(2,1)}, u32[]{:S(2)}, u32[]{:S(2)}) collective-permute-start(bf16[17,136,128]{2,1,0:T(8,128)(2,1)} %get-tuple-element.19.pz1), channel_id=1, source_target_pairs={{0,1},{1,2},{2,3},{3,4},{4,5},{5,6},{6,7},{7,8},{8,9},{9,10},{10,1... | collective-permute-start | bytes 1775624 | tf_op jit(solution)/shard_map/ppermute | solution.py:482
  45.9 0.7 copy-start.4
  46.6 14.8 %all-to-all-start = ((bf16[4,5,136,128]{3,2,1,0:T(8,128)(2,1)}), bf16[4,5,136,128]{3,2,1,0:T(8,128)(2,1)S(1)}, u32[]{:S(2)}, u32[]{:S(2)}) async-start(bf16[4,5,136,128]{3,2,1,0:T(8,128)(2,1)} %get-tuple-element.26), calls=%async_computation | async-start | bytes 1392640 | tf_op jit(solution)/shard_map/all_to_all | solution.py:456
  50.2 1.0 copy-start.5
  61.5 19.8 %collective-permute-start.6 = (bf16[4,5,136,128]{3,2,1,0:T(8,128)(2,1)S(1)}, bf16[4,5,136,128]{3,2,1,0:T(8,128)(2,1)S(1)}, u32[]{:S(2)}, u32[]{:S(2)}) collective-permute-start(bf16[4,5,136,128]{3,2,1,0:T(8,128)(2,1)S(1)} %all-to-all-done.refs_0_), channel_id=1, source_target_pairs={{3,0},{0,1},{1,2},{2,3},{7,4},{4,5},{5,6},{6,7},{11,8},{8,9},{9,10... | collective-permute-start | bytes 2088968 | tf_op jit(solution)/shard_map/ppermute | solution.py:461
  61.5 21.1 %collective-permute-start.5 = (bf16[4,5,136,128]{3,2,1,0:T(8,128)(2,1)S(1)}, bf16[4,5,136,128]{3,2,1,0:T(8,128)(2,1)S(1)}, u32[]{:S(2)}, u32[]{:S(2)}) collective-permute-start(bf16[4,5,136,128]{3,2,1,0:T(8,128)(2,1)S(1)} %all-to-all-done.refs_0_), channel_id=1, source_target_pairs={{1,0},{2,1},{3,2},{0,3},{5,4},{6,5},{7,6},{4,7},{9,8},{10,9},{11,1... | collective-permute-start | bytes 2088968 | tf_op jit(solution)/shard_map/ppermute | solution.py:460
  74.6 15.6 %collective-permute-start.10 = (bf16[4,3,136,128]{3,2,1,0:T(8,128)(2,1)S(1)}, bf16[4,3,136,128]{3,2,1,0:T(8,128)(2,1)S(1)}, u32[]{:S(2)}, u32[]{:S(2)}) collective-permute-start(bf16[4,3,136,128]{3,2,1,0:T(8,128)(2,1)S(1)} %all_to_all.10.refs_5_), channel_id=1, source_target_pairs={{3,0},{0,1},{1,2},{2,3},{7,4},{4,5},{5,6},{6,7},{11,8},{8,9},{9,10... | collective-permute-start | bytes 1253384 | tf_op jit(solution)/shard_map/ppermute | solution.py:461
  74.6 16.9 %collective-permute-start.9 = (bf16[4,3,136,128]{3,2,1,0:T(8,128)(2,1)S(1)}, bf16[4,3,136,128]{3,2,1,0:T(8,128)(2,1)S(1)}, u32[]{:S(2)}, u32[]{:S(2)}) collective-permute-start(bf16[4,3,136,128]{3,2,1,0:T(8,128)(2,1)S(1)} %all_to_all.10.refs_5_), channel_id=1, source_target_pairs={{1,0},{2,1},{3,2},{0,3},{5,4},{6,5},{7,6},{4,7},{9,8},{10,9},{11,1... | collective-permute-start | bytes 1253384 | tf_op jit(solution)/shard_map/ppermute | solution.py:460
  81.3 18.5 %collective-permute-start.8 = (bf16[2,5,136,128]{3,2,1,0:T(8,128)(2,1)S(1)}, bf16[2,5,136,128]{3,2,1,0:T(8,128)(2,1)S(1)}, u32[]{:S(2)}, u32[]{:S(2)}) collective-permute-start(bf16[2,5,136,128]{3,2,1,0:T(8,128)(2,1)S(1)} %slice.17), channel_id=1, source_target_pairs={{3,0},{7,4},{11,8},{15,12},{19,16},{23,20},{27,24},{31,28},{35,32}... | collective-permute-start | bytes 1044488 | tf_op jit(solution)/shard_map/ppermute | solution.py:466
  82.6 17.2 %collective-permute-start.7 = (bf16[2,5,136,128]{3,2,1,0:T(8,128)(2,1)S(1)}, bf16[2,5,136,128]{3,2,1,0:T(8,128)(2,1)S(1)}, u32[]{:S(2)}, u32[]{:S(2)}) collective-permute-start(bf16[2,5,136,128]{3,2,1,0:T(8,128)(2,1)S(1)} %slice.16), channel_id=1, source_target_pairs={{1,0},{5,4},{9,8},{13,12},{17,16},{21,20},{25,24},{29,28},{33,32},... | collective-permute-start | bytes 1044488 | tf_op jit(solution)/shard_map/ppermute | solution.py:466
  90.2 9.6 %collective-permute-start.12 = (bf16[2,3,136,128]{3,2,1,0:T(8,128)(2,1)S(1)}, bf16[2,3,136,128]{3,2,1,0:T(8,128)(2,1)S(1)}, u32[]{:S(2)}, u32[]{:S(2)}) collective-permute-start(bf16[2,3,136,128]{3,2,1,0:T(8,128)(2,1)S(1)} %slice.19), channel_id=1, source_target_pairs={{3,0},{7,4},{11,8},{15,12},{19,16},{23,20},{27,24},{31,28},{35,32}... | collective-permute-start | bytes 626696 | tf_op jit(solution)/shard_map/ppermute | solution.py:466
  91.5 8.3 %collective-permute-start.11 = (bf16[2,3,136,128]{3,2,1,0:T(8,128)(2,1)S(1)}, bf16[2,3,136,128]{3,2,1,0:T(8,128)(2,1)S(1)}, u32[]{:S(2)}, u32[]{:S(2)}) collective-permute-start(bf16[2,3,136,128]{3,2,1,0:T(8,128)(2,1)S(1)} %slice.18), channel_id=1, source_target_pairs={{1,0},{5,4},{9,8},{13,12},{17,16},{21,20},{25,24},{29,28},{33,32},... | collective-permute-start | bytes 626696 | tf_op jit(solution)/shard_map/ppermute | solution.py:466

commit v4 on v3

--- a/solution.py
+++ b/solution.py
@@ -17,6 +17,7 @@
 BF = jnp.bfloat16
 F32 = jnp.float32
 VMEM_LIMIT = 40 * 1024 * 1024
+PACK_LIMIT = 40 * 1024 * 1024
 
 
 def anywhere():
@@ -116,7 +117,7 @@
             jax.ShapeDtypeStruct((E, H, H), BF),
         ],
         scratch_shapes=[pltpu.VMEM((H * PE, L), F32), pltpu.VMEM((H * PE, L), F32)],
-        compiler_params=pltpu.CompilerParams(vmem_limit_bytes=VMEM_LIMIT),
+        compiler_params=pltpu.CompilerParams(vmem_limit_bytes=PACK_LIMIT),
         name="pack",
     )(*operands)
 
@@ -126,7 +127,7 @@
 
 def block_kernel(kinds, scal, meta, jac, early, late, views, rows, rows_out, rem_out, rem_to, buffers):
     jbuf, main, rest, x0, xs, keep, jac_sems, early_sems, late_sems, out_sems = buffers
-    pz, ghosts, pt, res_t, rem_in = views
+    pz, ghosts, pt, (res, res_t), rem_in = views
     lane = lax.broadcasted_iota(jnp.int32, (H, L), 1)
 
     def jac_copy(i):
@@ -270,6 +271,11 @@
         if i == 1:
             for copy in late_copies:
                 copy.wait()
+            if res is not None:
+                values = res[...].astype(F32)
+                tail = jnp.concatenate([values[:, L:], jnp.zeros((E, L - R), F32)], axis=1)
+                res_t[0:L, 0:E] = values[:, :L].T
+                res_t[L:H, 0:E] = tail.T[: H - L]
 
         def run(q, carry, k=k, outer=outer):
             if k == 0:
@@ -309,12 +315,12 @@
 REST = jax.ShapeDtypeStruct((4, H, L), F32)
 
 
-def centre_kernel(scal, meta, jac, pz0, pz1, pt, res_t, rows_out, rem_to, *scratch):
-    jbuf, main, rest, j_sems, e_sems, l_sems, o_sems, x0, keep, vz0, vz1, vpt, vres, rows, rem_out = scratch
+def centre_kernel(scal, meta, jac, pz0, pz1, pt, res, rows_out, rem_to, *scratch):
+    jbuf, main, rest, j_sems, e_sems, l_sems, o_sems, x0, keep, vz0, vz1, vpt, vres, res_t, rows, rem_out = scratch
     block_kernel(
         [(k, False) for k in range(7)], scal, meta, jac,
-        [(pz0, vz0), (pz1, vz1)], [(pt, vpt), (res_t, vres)],
-        ((vz0, vz1), {}, vpt, vres, None),
+        [(pz0, vz0), (pz1, vz1)], [(pt, vpt), (res, vres)],
+        ((vz0, vz1), {}, vpt, (vres, res_t), None),
         rows, rows_out.at[:, pl.ds(4, 1)], rem_out, rem_to,
         (jbuf, main, rest, x0, None, keep, j_sems, e_sems, l_sems, o_sems),
     )
@@ -326,7 +332,7 @@
     block_kernel(
         [(k, True) for k in range(1, 5)], scal, meta, jac,
         [(pz0, vz0), (pz1, vz1), (gx, vx)], [(pt, vpt), (rem_in, vrem), (gym, vym), (gyp, vyp)],
-        ((vz0, vz1), {1: vx, 2: vx, 3: vym, 4: vyp}, vpt, None, vrem),
+        ((vz0, vz1), {1: vx, 2: vx, 3: vym, 4: vyp}, vpt, (None, None), vrem),
         rows, rows_out.at[:, pl.ds(0, 4)], rem_out, rem_to,
         (jbuf, main, rest, None, xs, None, j_sems, e_sems, l_sems, o_sems),
     )
@@ -337,7 +343,7 @@
     block_kernel(
         [(k, True) for k in (5, 6)], scal, meta, jac,
         [(gzm, vzm)], [(pt, vpt), (gzp, vzp), (rem_in, vrem)],
-        (None, {5: vzm, 6: vzp}, vpt, None, vrem),
+        (None, {5: vzm, 6: vzp}, vpt, (None, None), vrem),
         rows, rows_out, None, None,
         (jbuf, main, rest, None, xs, None, j_sems, e_sems, l_sems, o_sems),
     )
@@ -358,20 +364,9 @@
 
 
 def final_kernel(scal, *refs):
-    sources = refs[:10]
-    coarse, restricted = refs[10:12]
-    held = refs[12:22]
-    out, s1, s2, in_sems, out_sems = refs[22:]
+    held = refs[:10]
+    coarse, restricted, out, s1, s2, out_sems = refs[10:]
     lane = lax.broadcasted_iota(jnp.int32, (H, L), 1)
-
-    def copies(n):
-        part, plane = (0, n) if n < 5 else (1, n - 5)
-        return [
-            pltpu.make_async_copy(
-                sources[5 * part + i].at[:, plane], held[5 * part + i].at[:, plane], in_sems.at[n, i]
-            )
-            for i in range(5)
-        ]
 
     def plane_of(n, slot):
         part, plane = (0, n) if n < 5 else (1, n - 5)
@@ -394,58 +389,48 @@
 
     @pl.when(scal[4] == 1)
     def _():
-        order = [4, 0, 1, 2, 3, 5, 6]
-        for n in [7] + order:
-            for copy in copies(n):
-                copy.start()
-        for copy in copies(7):
-            copy.wait()
+        for k in range(7):
+            for slot in range(16):
+                s1[pl.ds(slot, H, stride=PS), :] = plane_of([4, 0, 1, 2, 3, 5, 6][k], slot)
+                tail = plane_of(7, slot)
+                s2[pl.ds(slot, H, stride=PS), :] = pltpu.roll(tail, L - R * k, 1) if k else tail
+            if k >= 2:
+                out_copy(k - 2).wait()
+
+            def write(i, carry, k=k):
+                for u in range(27):
+                    row = i * 27 + u
+                    at = pl.ds(row * PS, 16)
+                    out[k % 2, row] = jnp.concatenate([s1[at, :], s2[at, :R]], axis=1).astype(BF)
+                return carry
+
+            lax.fori_loop(0, W // 27, write, 0)
+            out_copy(k).start()
         acc = jnp.zeros((H, L), F32)
         for slot in range(16):
             turned = pltpu.roll(plane_of(7, slot), (slot - 49 + L) % L, 1)
             acc = jnp.where(lane == slot, turned, acc)
         restricted[...] = acc.T[:16, :W].astype(BF)
-        for k in range(7):
-            for copy in copies(order[k]):
-                copy.wait()
-            for slot in range(16):
-                s1[pl.ds(slot, H, stride=PS), :] = plane_of(order[k], slot)
-                tail = plane_of(7, slot)
-                s2[pl.ds(slot, H, stride=PS), :] = pltpu.roll(tail, L - R * k, 1) if k else tail
-            if k >= 2:
-                out_copy(k - 2).wait()
-
-            def write(i, carry, k=k):
-                for u in range(9):
-                    row = i * 9 + u
-                    at = pl.ds(row * PS, 16)
-                    out[k % 2, row] = jnp.concatenate([s1[at, :], s2[at, :R]], axis=1).astype(BF)
-                return carry
-
-            lax.fori_loop(0, W // 9, write, 0)
-            out_copy(k).start()
         out_copy(5).wait()
         out_copy(6).wait()
 
 
-def final_call(scal, first, second):
-    operands = [scal, *first, *second]
+def final_call(scal, rows):
+    rows = [pltpu.with_memory_space_constraint(a, pltpu.VMEM) for a in rows]
     return pl.pallas_call(
         final_kernel,
-        in_specs=[smem()] + [anywhere()] * 10,
+        in_specs=[smem()] + [vmem()] * 10,
         out_specs=[anywhere(), vmem()],
         out_shape=[jax.ShapeDtypeStruct((7, W, 16, W), BF), jax.ShapeDtypeStruct((16, W), BF)],
-        scratch_shapes=[pltpu.VMEM(a.shape, BF) for a in operands[1:]]
-        + [
+        scratch_shapes=[
             pltpu.VMEM((2, W, 16, W), BF),
             pltpu.VMEM((H * PS, L), F32),
             pltpu.VMEM((H * PS, L), F32),
-            pltpu.SemaphoreType.DMA((8, 5)),
             pltpu.SemaphoreType.DMA((7,)),
         ],
         compiler_params=pltpu.CompilerParams(vmem_limit_bytes=VMEM_LIMIT),
         name="assemble",
-    )(*operands)
+    )(scal, *rows)
 
 
 DOWN = [(1, 0), (2, 1), (3, 2), (0, 3)]
@@ -475,7 +460,6 @@
     ).astype(jnp.int32)
     jac = jnp.transpose(jacobian, (1, 2, 0, 3))
     pro = jnp.transpose(prolong, (1, 0, 2))
-    res_t = jnp.pad(residual.T.astype(F32), ((0, 1), (0, L - E)))
     meta, pz0, pz1, xs, ys0, ys1, pt = pack_call(scal, neighbours.T, agg_map, owners, pro)
     gz = ("zz", "yy")
     ghost_x = lax.ppermute(xs, "gx", [(0, 1), (1, 0)])
@@ -487,8 +471,8 @@
     z_face, side_face = [pltpu.VMEM((n, H, L), BF) for n in (17, 10)]
     turned = pltpu.VMEM((E, H, H), BF)
     first, rem = block_call(
-        centre_kernel, (scal, meta, jac, pz0, pz1, pt, res_t), [five, REST],
-        [HALF, FULL, z_face, z_face, turned, pltpu.VMEM((H, L), F32), pltpu.VMEM((4, 1, H, L), BF), REM],
+        centre_kernel, (scal, meta, jac, pz0, pz1, pt, residual), [five, REST],
+        [HALF, FULL, z_face, z_face, turned, pltpu.VMEM((E, W), BF), pltpu.VMEM((H, L), F32), pltpu.VMEM((4, 1, H, L), BF), REM],
         "centre", {}, 18_000_000_000,
     )
     first, rem = block_call(
@@ -509,7 +493,7 @@
     twice1 = forward(down1, up1)
     down2, up2 = along_ring(held2)
     twice2 = forward(down2, up2)
-    coarse, restricted = final_call(scal, (held1, down1, up1) + twice1, (held2, down2, up2) + twice2)
+    coarse, restricted = final_call(scal, (held1, down1, up1) + twice1 + (held2, down2, up2) + twice2)
     return jnp.transpose(coarse, (2, 0, 1, 3)), restricted
 
 

time: 109 us -> 106 us (0.972)
  Pallas kernels: 45.7 us -> 43.1 us
    pallas_call x1, Pallas kernels: 8.45 us -> 5.93 us  [final_call(): pl.pallas_call(final_kernel, in_specs=[smem()] + [vmem()] * 10, out_specs...]
    unnamed x13 -> x14, local copies, waits for them, and re-layouts: 6.12 us -> 6 us
  transfers between devices with their start and end apart: 14 -> 14, of which waited for: 4 -> 4; matrix products, arithmetic and copies ran while one was open for 1% -> 0% of each run, Pallas kernels for 30% -> 31%
where the time goes in v4:
time: 106 us
  Pallas kernels  43.1 us (41%)
  starting transfers between devices  25.1 us (24%)
  waiting for transfers between devices  20.5 us (19%)
  blocking collectives  9.86 us (9%)
  local copies, waits for them, and re-layouts  6.17 us (6%)
    pallas_call x3, Pallas kernels, block_call(): pl.pallas_call(kernel, in_specs=[smem(), smem()] + [anywhere()] * (len(op...  32.2 us
    all_to_all x1, blocking collectives, to_owner_row(): return lax.all_to_all(rows, 'zz', split_axis=0, concat_axis=0, tiled=True)  9.86 us
    ppermute x2, waiting for transfers between devices, along_ring(): up = lax.ppermute(held, 'yy', UP)  9.7 us
    ppermute x2, waiting for transfers between devices, forward(): lax.ppermute(up[2:], 'yy', [(3, 0)])  6.95 us
    ppermute x1, starting transfers between devices, body(): ghost_zp = lax.ppermute(pz0, gz, [((i + 1) % 16, i) for i in range(16)])  6.57 us
    ppermute x2, starting transfers between devices, along_ring(): down = lax.ppermute(held, 'yy', DOWN)  6.47 us
    unnamed x14, local copies, waits for them, and re-layouts  6 us
    pallas_call x1, Pallas kernels, final_call(): pl.pallas_call(final_kernel, in_specs=[smem()] + [vmem()] * 10, out_specs...  5.93 us
  transfers between devices with their start and end apart: 14, of which 4 were waited for; matrix products, arithmetic and copies ran while one was open for 0% of the time, Pallas kernels for 31%

profile of v4, /device:TPU:0, one launch (start us, length us, event | category | flops | bytes accessed | tf_op | source)
XLA Modules:
  0.0 105.6 jit_solution(16155397905093289447)
XLA Ops:
  0.6 0.1 stack.35.scal
  0.7 1.6 %copy-done = bf16[32,135,135]{2,0,1:T(8,128)(2,1)S(1)} copy-done((bf16[32,135,135]{2,0,1:T(8,128)(2,1)S(1)}, bf16[32,135,135]{2,0,1:T(8,128)(2,1)}, u32[]{:S(2)}) %copy-start) | copy-done | bytes 1166424
  2.4 0.7 copy-done.1
  3.0 0.7 copy-done.2
  3.7 0.7 copy-done.3
  4.4 5.0 %pack.1 = (s32[40]{0:T(128)S(1)}, bf16[17,136,128]{2,1,0:T(8,128)(2,1)}, bf16[17,136,128]{2,1,0:T(8,128)(2,1)}, bf16[10,136,128]{2,1,0:T(8,128)(2,1)S(1)}, bf16[...) custom-call(s32[7]{0:T(128)S(1)} %stack.35.scal, ...), custom_call_target="tpu_custom_call" | custom-call | tf_op jit(solution)/shard_map/pack/pallas_call | solution.py:106
  9.3 0.1 collective-permute-start
  9.4 1.6 %collective-permute-start.1 = (bf16[10,136,128]{2,1,0:T(8,128)(2,1)S(1)}, bf16[10,136,128]{2,1,0:T(8,128)(2,1)S(1)}, u32[]{:S(2)}, u32[]{:S(2)}) collective-permute-start(bf16[10,136,128]{2,1,0:T(8,128)(2,1)S(1)} %get-tuple-element.22), channel_id=1, source_target_pairs={{0,16},{16,32},{32,48},{48,0},{1,17},{17,33},{33,49},{49,1},{2,18}... | collective-permute-start | bytes 1044488 | tf_op jit(solution)/shard_map/ppermute | solution.py:468
  11.1 1.7 %collective-permute-start.2 = (bf16[10,136,128]{2,1,0:T(8,128)(2,1)S(1)}, bf16[10,136,128]{2,1,0:T(8,128)(2,1)S(1)}, u32[]{:S(2)}, u32[]{:S(2)}) collective-permute-start(bf16[10,136,128]{2,1,0:T(8,128)(2,1)S(1)} %get-tuple-element.23), channel_id=1, source_target_pairs={{16,0},{32,16},{48,32},{0,48},{17,1},{33,17},{49,33},{1,49},{18,2}... | collective-permute-start | bytes 1044488 | tf_op jit(solution)/shard_map/ppermute | solution.py:469
  12.7 6.6 %collective-permute-start.4 = (bf16[17,136,128]{2,1,0:T(8,128)(2,1)}, bf16[17,136,128]{2,1,0:T(8,128)(2,1)}, u32[]{:S(2)}, u32[]{:S(2)}) collective-permute-start(bf16[17,136,128]{2,1,0:T(8,128)(2,1)} %get-tuple-element.18.pz0), channel_id=1, source_target_pairs={{1,0},{2,1},{3,2},{4,3},{5,4},{6,5},{7,6},{8,7},{9,8},{10,9},{11,1... | collective-permute-start | bytes 1775624 | tf_op jit(solution)/shard_map/ppermute | solution.py:467
  19.3 0.7 copy-done.4
  20.0 14.4 %centre.1 = (bf16[4,5,136,128]{3,2,1,0:T(8,128)(2,1)}, f32[4,136,128]{2,1,0:T(8,128)S(1)}) custom-call(s32[7]{0:T(128)S(1)} %stack.35.scal, s32[40]{0:T(128)S(1)} %get-tuple-element.17.meta, bf16[7,135,32,135]{3,2,1,0:T(8,128)(2,1)} %bitcast.13, bf16[17,136,128]{2,1,0:T(8,128)(2,1)} %get-tuple-element.18.pz0, bf16[17,136,128]{2,1,0:T(8,128)(2,1)} %get-tuple-element.19.pz1, ...), custom_call_target="tpu_custom_call" | custom-call | flops 17999998976 | bytes 1000000 | tf_op jit(solution)/shard_map/centre/pallas_call | solution.py:353
  34.4 0.0 collective-permute-done.gx
  34.4 0.0 collective-permute-done.1.gym
  34.4 11.4 %sides.1 = (bf16[4,5,136,128]{3,2,1,0:T(8,128)(2,1)}, f32[4,136,128]{2,1,0:T(8,128)S(1)}) custom-call(s32[7]{0:T(128)S(1)} %stack.35.scal, s32[40]{0:T(128)S(1)} %get-tuple-element.17.meta, bf16[7,135,32,135]{3,2,1,0:T(8,128)(2,1)} %bitcast.14, bf16[17,136,128]{2,1,0:T(8,128)(2,1)} %get-tuple-element.18.pz0, ...), custom_call_target="tpu_custom_call", output_to_operand_aliasing={{0}: (10, {})} | custom-call | flops 12000000000 | bytes 1000000 | tf_op jit(solution)/shard_map/sides/pallas_call | solution.py:353
  45.8 0.7 copy-done.5
  46.5 3.5 %all-to-all-start = ((bf16[4,5,136,128]{3,2,1,0:T(8,128)(2,1)}), bf16[4,5,136,128]{3,2,1,0:T(8,128)(2,1)S(1)}, u32[]{:S(2)}, u32[]{:S(2)}) async-start(bf16[4,5,136,128]{3,2,1,0:T(8,128)(2,1)} %get-tuple-element.26), calls=%async_computation | async-start | bytes 1392640 | tf_op jit(solution)/shard_map/all_to_all | solution.py:441
  50.0 0.0 collective-permute-done.4.gzp
  50.0 0.9 copy-done.6
  50.9 6.5 %depth.1 = bf16[4,3,136,128]{3,2,1,0:T(8,128)(2,1)S(1)} custom-call(s32[7]{0:T(128)S(1)} %stack.35.scal, s32[40]{0:T(128)S(1)} %get-tuple-element.17.meta, bf16[7,135,32,135]{3,2,1,0:T(8,128)(2,1)} %bitcast.15, bf16[32,136,136]{2,1,0:T(8,128)(2,1)S(1)} %get-tuple-element.20.pt, bf16[17,136,128]{2,1,0:T(8,128)(2,1)} %collective-permute-done.3.gzm, ...), custom_call_target="tpu_custom_call" | custom-call | flops 8999999488 | bytes 1000000 | tf_op jit(solution)/shard_map/depth/pallas_call | solution.py:353
  57.5 3.8 %all-to-all-done.refs_0_ = bf16[4,5,136,128]{3,2,1,0:T(8,128)(2,1)S(1)} async-done(((bf16[4,5,136,128]{3,2,1,0:T(8,128)(2,1)}), bf16[4,5,136,128]{3,2,1,0:T(8,128)(2,1)S(1)}, u32[]{:S(2)}, u32[]{:S(2)}) %all-to-all-start) | async-done | bytes 696352 | tf_op jit(solution)/shard_map/all_to_all | solution.py:441
  61.3 3.2 %collective-permute-start.5 = (bf16[4,5,136,128]{3,2,1,0:T(8,128)(2,1)S(1)}, bf16[4,5,136,128]{3,2,1,0:T(8,128)(2,1)S(1)}, u32[]{:S(2)}, u32[]{:S(2)}) collective-permute-start(bf16[4,5,136,128]{3,2,1,0:T(8,128)(2,1)S(1)} %all-to-all-done.refs_0_), channel_id=1, source_target_pairs={{1,0},{2,1},{3,2},{0,3},{5,4},{6,5},{7,6},{4,7},{9,8},{10,9},{11,1... | collective-permute-start | bytes 2088968 | tf_op jit(solution)/shard_map/ppermute | solution.py:445
  64.5 9.9 %all_to_all.10.refs_5_ = bf16[4,3,136,128]{3,2,1,0:T(8,128)(2,1)S(1)} all-to-all(bf16[4,3,136,128]{3,2,1,0:T(8,128)(2,1)S(1)} %depth.1), channel_id=1, replica_groups=mesh['gx'=2,'gy'=4,'zz'=4,'yy'=4] {'zz'}, dimensions={0} | all-to-all | bytes 835584 | tf_op jit(solution)/shard_map/all_to_all | solution.py:441
  74.4 3.2 %collective-permute-start.9 = (bf16[4,3,136,128]{3,2,1,0:T(8,128)(2,1)S(1)}, bf16[4,3,136,128]{3,2,1,0:T(8,128)(2,1)S(1)}, u32[]{:S(2)}, u32[]{:S(2)}) collective-permute-start(bf16[4,3,136,128]{3,2,1,0:T(8,128)(2,1)S(1)} %all_to_all.10.refs_5_), channel_id=1, source_target_pairs={{1,0},{2,1},{3,2},{0,3},{5,4},{6,5},{7,6},{4,7},{9,8},{10,9},{11,1... | collective-permute-start | bytes 1253384 | tf_op jit(solution)/shard_map/ppermute | solution.py:445
  77.6 3.4 %collective-permute-done.6.refs_2_ = bf16[4,5,136,128]{3,2,1,0:T(8,128)(2,1)S(1)} collective-permute-done((bf16[4,5,136,128]{3,2,1,0:T(8,128)(2,1)S(1)}, bf16[4,5,136,128]{3,2,1,0:T(8,128)(2,1)S(1)}, u32[]{:S(2)}, u32[]{:S(2)}) %collective-permute-start.6) | collective-permute-done | bytes 696352 | tf_op jit(solution)/shard_map/ppermute | solution.py:446
  81.1 1.3 %collective-permute-start.8 = (bf16[2,5,136,128]{3,2,1,0:T(8,128)(2,1)S(1)}, bf16[2,5,136,128]{3,2,1,0:T(8,128)(2,1)S(1)}, u32[]{:S(2)}, u32[]{:S(2)}) collective-permute-start(bf16[2,5,136,128]{3,2,1,0:T(8,128)(2,1)S(1)} %slice.17), channel_id=1, source_target_pairs={{3,0},{7,4},{11,8},{15,12},{19,16},{23,20},{27,24},{31,28},{35,32}... | collective-permute-start | bytes 1044488 | tf_op jit(solution)/shard_map/ppermute | solution.py:451
  82.4 1.3 %collective-permute-start.7 = (bf16[2,5,136,128]{3,2,1,0:T(8,128)(2,1)S(1)}, bf16[2,5,136,128]{3,2,1,0:T(8,128)(2,1)S(1)}, u32[]{:S(2)}, u32[]{:S(2)}) collective-permute-start(bf16[2,5,136,128]{3,2,1,0:T(8,128)(2,1)S(1)} %slice.16), channel_id=1, source_target_pairs={{1,0},{5,4},{9,8},{13,12},{17,16},{21,20},{25,24},{29,28},{33,32},... | collective-permute-start | bytes 1044488 | tf_op jit(solution)/shard_map/ppermute | solution.py:451
  83.7 6.3 %collective-permute-done.10.refs_7_ = bf16[4,3,136,128]{3,2,1,0:T(8,128)(2,1)S(1)} collective-permute-done((bf16[4,3,136,128]{3,2,1,0:T(8,128)(2,1)S(1)}, bf16[4,3,136,128]{3,2,1,0:T(8,128)(2,1)S(1)}, u32[]{:S(2)}, u32[]{:S(2)}) %collective-permute-start.10) | collective-permute-done | bytes 417824 | tf_op jit(solution)/shard_map/ppermute | solution.py:446
  90.0 1.3 %collective-permute-start.12 = (bf16[2,3,136,128]{3,2,1,0:T(8,128)(2,1)S(1)}, bf16[2,3,136,128]{3,2,1,0:T(8,128)(2,1)S(1)}, u32[]{:S(2)}, u32[]{:S(2)}) collective-permute-start(bf16[2,3,136,128]{3,2,1,0:T(8,128)(2,1)S(1)} %slice.19), channel_id=1, source_target_pairs={{3,0},{7,4},{11,8},{15,12},{19,16},{23,20},{27,24},{31,28},{35,32}... | collective-permute-start | bytes 626696 | tf_op jit(solution)/shard_map/ppermute | solution.py:451
  91.4 1.3 %collective-permute-start.11 = (bf16[2,3,136,128]{3,2,1,0:T(8,128)(2,1)S(1)}, bf16[2,3,136,128]{3,2,1,0:T(8,128)(2,1)S(1)}, u32[]{:S(2)}, u32[]{:S(2)}) collective-permute-start(bf16[2,3,136,128]{3,2,1,0:T(8,128)(2,1)S(1)} %slice.18), channel_id=1, source_target_pairs={{1,0},{5,4},{9,8},{13,12},{17,16},{21,20},{25,24},{29,28},{33,32},... | collective-permute-start | bytes 626696 | tf_op jit(solution)/shard_map/ppermute | solution.py:451
  92.7 6.9 %collective-permute-done.12.refs_9_ = bf16[2,3,136,128]{3,2,1,0:T(8,128)(2,1)S(1)} collective-permute-done((bf16[2,3,136,128]{3,2,1,0:T(8,128)(2,1)S(1)}, bf16[2,3,136,128]{3,2,1,0:T(8,128)(2,1)S(1)}, u32[]{:S(2)}, u32[]{:S(2)}) %collective-permute-start.12) | collective-permute-done | bytes 208928 | tf_op jit(solution)/shard_map/ppermute | solution.py:451
  99.6 5.9 %assemble.1 = (bf16[7,135,16,135]{3,2,1,0:T(8,128)(2,1)}, bf16[16,135]{1,0:T(8,128)(2,1)}) custom-call(s32[7]{0:T(128)S(1)} %stack.35.scal, bf16[4,5,136,128]{3,2,1,0:T(8,128)(2,1)S(1)} %all-to-all-done.refs_0_, bf16[4,5,136,128]{3,2,1,0:T(8,128)(2,1)S(1)} %collective-permute-done.5.refs_1_, bf16[4,5,136,128]{3,2,1,0:T(8,128)(2,1)S(1)} %collective-permute-done.6.refs_2_, ...), custom_call_target="tpu_custom_call" | custom-call | tf_op jit(solution)/shard_map/assemble/pallas_call | solution.py:420
  (21 shorter events, 0.1 us)
Async XLA Ops:
  0.7 1.6 %copy-start = (bf16[32,135,135]{2,0,1:T(8,128)(2,1)S(1)}, bf16[32,135,135]{2,0,1:T(8,128)(2,1)}, u32[]{:S(2)}) copy-start(bf16[32,135,135]{2,0,1:T(8,128)(2,1)} %param.7) | copy-start | bytes 3499204
  2.4 0.7 copy-start.1
  3.0 0.7 copy-start.2
  3.7 0.7 copy-start.3
  9.3 25.1 %collective-permute-start = (bf16[10,136,128]{2,1,0:T(8,128)(2,1)S(1)}, bf16[10,136,128]{2,1,0:T(8,128)(2,1)S(1)}, u32[]{:S(2)}, u32[]{:S(2)}) collective-permute-start(bf16[10,136,128]{2,1,0:T(8,128)(2,1)S(1)} %get-tuple-element.21), channel_id=1, source_target_pairs={{0,64},{64,0},{1,65},{65,1},{2,66},{66,2},{3,67},{67,3},{4,68},{68... | collective-permute-start | bytes 1044488 | tf_op jit(solution)/shard_map/ppermute | solution.py:465
  9.4 25.0 %collective-permute-start.1 = (bf16[10,136,128]{2,1,0:T(8,128)(2,1)S(1)}, bf16[10,136,128]{2,1,0:T(8,128)(2,1)S(1)}, u32[]{:S(2)}, u32[]{:S(2)}) collective-permute-start(bf16[10,136,128]{2,1,0:T(8,128)(2,1)S(1)} %get-tuple-element.22), channel_id=1, source_target_pairs={{0,16},{16,32},{32,48},{48,0},{1,17},{17,33},{33,49},{49,1},{2,18}... | collective-permute-start | bytes 1044488 | tf_op jit(solution)/shard_map/ppermute | solution.py:468
  11.1 23.3 %collective-permute-start.2 = (bf16[10,136,128]{2,1,0:T(8,128)(2,1)S(1)}, bf16[10,136,128]{2,1,0:T(8,128)(2,1)S(1)}, u32[]{:S(2)}, u32[]{:S(2)}) collective-permute-start(bf16[10,136,128]{2,1,0:T(8,128)(2,1)S(1)} %get-tuple-element.23), channel_id=1, source_target_pairs={{16,0},{32,16},{48,32},{0,48},{17,1},{33,17},{49,33},{1,49},{18,2}... | collective-permute-start | bytes 1044488 | tf_op jit(solution)/shard_map/ppermute | solution.py:469
  12.7 37.3 %collective-permute-start.4 = (bf16[17,136,128]{2,1,0:T(8,128)(2,1)}, bf16[17,136,128]{2,1,0:T(8,128)(2,1)}, u32[]{:S(2)}, u32[]{:S(2)}) collective-permute-start(bf16[17,136,128]{2,1,0:T(8,128)(2,1)} %get-tuple-element.18.pz0), channel_id=1, source_target_pairs={{1,0},{2,1},{3,2},{4,3},{5,4},{6,5},{7,6},{8,7},{9,8},{10,9},{11,1... | collective-permute-start | bytes 1775624 | tf_op jit(solution)/shard_map/ppermute | solution.py:467
  19.3 30.7 %collective-permute-start.3 = (bf16[17,136,128]{2,1,0:T(8,128)(2,1)}, bf16[17,136,128]{2,1,0:T(8,128)(2,1)}, u32[]{:S(2)}, u32[]{:S(2)}) collective-permute-start(bf16[17,136,128]{2,1,0:T(8,128)(2,1)} %get-tuple-element.19.pz1), channel_id=1, source_target_pairs={{0,1},{1,2},{2,3},{3,4},{4,5},{5,6},{6,7},{7,8},{8,9},{9,10},{10,1... | collective-permute-start | bytes 1775624 | tf_op jit(solution)/shard_map/ppermute | solution.py:466
  19.3 0.7 copy-start.4
  45.8 0.7 copy-start.5
  46.5 14.8 %all-to-all-start = ((bf16[4,5,136,128]{3,2,1,0:T(8,128)(2,1)}), bf16[4,5,136,128]{3,2,1,0:T(8,128)(2,1)S(1)}, u32[]{:S(2)}, u32[]{:S(2)}) async-start(bf16[4,5,136,128]{3,2,1,0:T(8,128)(2,1)} %get-tuple-element.26), calls=%async_computation | async-start | bytes 1392640 | tf_op jit(solution)/shard_map/all_to_all | solution.py:441
  50.0 1.0 copy-start.6
  61.3 19.8 %collective-permute-start.6 = (bf16[4,5,136,128]{3,2,1,0:T(8,128)(2,1)S(1)}, bf16[4,5,136,128]{3,2,1,0:T(8,128)(2,1)S(1)}, u32[]{:S(2)}, u32[]{:S(2)}) collective-permute-start(bf16[4,5,136,128]{3,2,1,0:T(8,128)(2,1)S(1)} %all-to-all-done.refs_0_), channel_id=1, source_target_pairs={{3,0},{0,1},{1,2},{2,3},{7,4},{4,5},{5,6},{6,7},{11,8},{8,9},{9,10... | collective-permute-start | bytes 2088968 | tf_op jit(solution)/shard_map/ppermute | solution.py:446
  61.3 21.1 %collective-permute-start.5 = (bf16[4,5,136,128]{3,2,1,0:T(8,128)(2,1)S(1)}, bf16[4,5,136,128]{3,2,1,0:T(8,128)(2,1)S(1)}, u32[]{:S(2)}, u32[]{:S(2)}) collective-permute-start(bf16[4,5,136,128]{3,2,1,0:T(8,128)(2,1)S(1)} %all-to-all-done.refs_0_), channel_id=1, source_target_pairs={{1,0},{2,1},{3,2},{0,3},{5,4},{6,5},{7,6},{4,7},{9,8},{10,9},{11,1... | collective-permute-start | bytes 2088968 | tf_op jit(solution)/shard_map/ppermute | solution.py:445
  74.4 15.6 %collective-permute-start.10 = (bf16[4,3,136,128]{3,2,1,0:T(8,128)(2,1)S(1)}, bf16[4,3,136,128]{3,2,1,0:T(8,128)(2,1)S(1)}, u32[]{:S(2)}, u32[]{:S(2)}) collective-permute-start(bf16[4,3,136,128]{3,2,1,0:T(8,128)(2,1)S(1)} %all_to_all.10.refs_5_), channel_id=1, source_target_pairs={{3,0},{0,1},{1,2},{2,3},{7,4},{4,5},{5,6},{6,7},{11,8},{8,9},{9,10... | collective-permute-start | bytes 1253384 | tf_op jit(solution)/shard_map/ppermute | solution.py:446
  74.4 16.9 %collective-permute-start.9 = (bf16[4,3,136,128]{3,2,1,0:T(8,128)(2,1)S(1)}, bf16[4,3,136,128]{3,2,1,0:T(8,128)(2,1)S(1)}, u32[]{:S(2)}, u32[]{:S(2)}) collective-permute-start(bf16[4,3,136,128]{3,2,1,0:T(8,128)(2,1)S(1)} %all_to_all.10.refs_5_), channel_id=1, source_target_pairs={{1,0},{2,1},{3,2},{0,3},{5,4},{6,5},{7,6},{4,7},{9,8},{10,9},{11,1... | collective-permute-start | bytes 1253384 | tf_op jit(solution)/shard_map/ppermute | solution.py:445
  81.1 18.5 %collective-permute-start.8 = (bf16[2,5,136,128]{3,2,1,0:T(8,128)(2,1)S(1)}, bf16[2,5,136,128]{3,2,1,0:T(8,128)(2,1)S(1)}, u32[]{:S(2)}, u32[]{:S(2)}) collective-permute-start(bf16[2,5,136,128]{3,2,1,0:T(8,128)(2,1)S(1)} %slice.17), channel_id=1, source_target_pairs={{3,0},{7,4},{11,8},{15,12},{19,16},{23,20},{27,24},{31,28},{35,32}... | collective-permute-start | bytes 1044488 | tf_op jit(solution)/shard_map/ppermute | solution.py:451
  82.4 17.2 %collective-permute-start.7 = (bf16[2,5,136,128]{3,2,1,0:T(8,128)(2,1)S(1)}, bf16[2,5,136,128]{3,2,1,0:T(8,128)(2,1)S(1)}, u32[]{:S(2)}, u32[]{:S(2)}) collective-permute-start(bf16[2,5,136,128]{3,2,1,0:T(8,128)(2,1)S(1)} %slice.16), channel_id=1, source_target_pairs={{1,0},{5,4},{9,8},{13,12},{17,16},{21,20},{25,24},{29,28},{33,32},... | collective-permute-start | bytes 1044488 | tf_op jit(solution)/shard_map/ppermute | solution.py:451
  90.0 9.6 %collective-permute-start.12 = (bf16[2,3,136,128]{3,2,1,0:T(8,128)(2,1)S(1)}, bf16[2,3,136,128]{3,2,1,0:T(8,128)(2,1)S(1)}, u32[]{:S(2)}, u32[]{:S(2)}) collective-permute-start(bf16[2,3,136,128]{3,2,1,0:T(8,128)(2,1)S(1)} %slice.19), channel_id=1, source_target_pairs={{3,0},{7,4},{11,8},{15,12},{19,16},{23,20},{27,24},{31,28},{35,32}... | collective-permute-start | bytes 626696 | tf_op jit(solution)/shard_map/ppermute | solution.py:451
  91.4 8.2 %collective-permute-start.11 = (bf16[2,3,136,128]{3,2,1,0:T(8,128)(2,1)S(1)}, bf16[2,3,136,128]{3,2,1,0:T(8,128)(2,1)S(1)}, u32[]{:S(2)}, u32[]{:S(2)}) collective-permute-start(bf16[2,3,136,128]{3,2,1,0:T(8,128)(2,1)S(1)} %slice.18), channel_id=1, source_target_pairs={{1,0},{5,4},{9,8},{13,12},{17,16},{21,20},{25,24},{29,28},{33,32},... | collective-permute-start | bytes 626696 | tf_op jit(solution)/shard_map/ppermute | solution.py:451

commit v5 on v4

--- a/solution.py
+++ b/solution.py
@@ -24,6 +24,10 @@
     return pl.BlockSpec(memory_space=pl.ANY)
 
 
+def stay(array):
+    return pltpu.with_memory_space_constraint(array, pltpu.HBM)
+
+
 def smem():
     return pl.BlockSpec(memory_space=pltpu.SMEM)
 
@@ -54,9 +58,21 @@
     return ref[pl.ds(element, H, stride=PE), :]
 
 
-def pack_kernel(scal, nbr, agg, own, p_ref, meta, pz0, pz1, xs, ys0, ys1, pt, main, rest):
+def pack_kernel(
+    scal, nbr_in, agg_in, own_in, p_ref, meta, pz0, pz1, xs, ys0, ys1, pt, main, rest, nbr, agg, own, sems
+):
     pz, ys = (pz0, pz1), (ys0, ys1)
     base = scal[0]
+    copies = [
+        pltpu.make_async_copy(a, b, sems.at[i])
+        for i, (a, b) in enumerate([(nbr_in, nbr), (agg_in, agg), (own_in, own)])
+    ]
+    for copy in copies:
+        copy.start()
+    clear(main, rest)
+    spread(lambda row: p_ref[row], main, rest)
+    for copy in copies:
+        copy.wait()
 
     def place(e, carry):
         def near(direction):
@@ -79,8 +95,6 @@
         return carry
 
     lax.fori_loop(0, E, place, 0)
-    clear(main, rest)
-    spread(lambda row: p_ref[row], main, rest)
     for oz in range(2):
         plane = jnp.zeros((H, L), F32)
         for xy in range(16):
@@ -105,7 +119,7 @@
 def pack_call(*operands):
     return pl.pallas_call(
         pack_kernel,
-        in_specs=[smem()] * 4 + [vmem()],
+        in_specs=[smem()] + [anywhere()] * 3 + [vmem()],
         out_specs=[smem()] + [vmem()] * 6,
         out_shape=[
             jax.ShapeDtypeStruct((40,), jnp.int32),
@@ -116,7 +130,14 @@
             jax.ShapeDtypeStruct((10, H, L), BF),
             jax.ShapeDtypeStruct((E, H, H), BF),
         ],
-        scratch_shapes=[pltpu.VMEM((H * PE, L), F32), pltpu.VMEM((H * PE, L), F32)],
+        scratch_shapes=[
+            pltpu.VMEM((H * PE, L), F32),
+            pltpu.VMEM((H * PE, L), F32),
+            pltpu.SMEM((6, E), jnp.int32),
+            pltpu.SMEM((E,), jnp.int32),
+            pltpu.SMEM((4,), jnp.int32),
+            pltpu.SemaphoreType.DMA((3,)),
+        ],
         compiler_params=pltpu.CompilerParams(vmem_limit_bytes=PACK_LIMIT),
         name="pack",
     )(*operands)
@@ -312,7 +333,7 @@
 HALF = pltpu.VMEM((E, H, 2 * L), BF)
 FULL = pltpu.VMEM((E, H, 2 * L), F32)
 REM = pltpu.VMEM((4, H, L), F32)
-REST = jax.ShapeDtypeStruct((4, H, L), F32)
+REST = pltpu.HBM((4, H, L), F32)
 
 
 def centre_kernel(scal, meta, jac, pz0, pz1, pt, res, rows_out, rem_to, *scratch):
@@ -353,7 +374,7 @@
     return pl.pallas_call(
         kernel,
         in_specs=[smem(), smem()] + [anywhere()] * (len(operands) - 2),
-        out_specs=jax.tree.map(lambda _: anywhere(), out_shape),
+        out_specs=[anywhere()] * len(out_shape),
         out_shape=out_shape,
         scratch_shapes=COMMON + scratch,
         input_output_aliases=aliases,
@@ -460,7 +481,9 @@
     ).astype(jnp.int32)
     jac = jnp.transpose(jacobian, (1, 2, 0, 3))
     pro = jnp.transpose(prolong, (1, 0, 2))
-    meta, pz0, pz1, xs, ys0, ys1, pt = pack_call(scal, neighbours.T, agg_map, owners, pro)
+    meta, pz0, pz1, xs, ys0, ys1, pt = pack_call(
+        scal, stay(neighbours.T), stay(agg_map), stay(owners), pro
+    )
     gz = ("zz", "yy")
     ghost_x = lax.ppermute(xs, "gx", [(0, 1), (1, 0)])
     ghost_zm = lax.ppermute(pz1, gz, [(i, (i + 1) % 16) for i in range(16)])
@@ -471,18 +494,18 @@
     z_face, side_face = [pltpu.VMEM((n, H, L), BF) for n in (17, 10)]
     turned = pltpu.VMEM((E, H, H), BF)
     first, rem = block_call(
-        centre_kernel, (scal, meta, jac, pz0, pz1, pt, residual), [five, REST],
+        centre_kernel, (scal, meta, jac, pz0, pz1, pt, stay(residual)), [five, REST],
         [HALF, FULL, z_face, z_face, turned, pltpu.VMEM((E, W), BF), pltpu.VMEM((H, L), F32), pltpu.VMEM((4, 1, H, L), BF), REM],
         "centre", {}, 18_000_000_000,
     )
     first, rem = block_call(
-        sides_kernel, (scal, meta, jac, pz0, pz1, pt, ghost_x, ghost_ym, ghost_yp, rem, first), [five, REST],
+        sides_kernel, (scal, meta, jac, pz0, pz1, pt, ghost_x, ghost_ym, ghost_yp, stay(rem), first), [five, REST],
         [HALF, z_face, z_face, turned, side_face, side_face, side_face, REM, pltpu.VMEM((4, 4, H, L), BF), REM],
         "sides", {10: 0}, 12_000_000_000,
     )
     held1 = to_owner_row(first)
     (second,) = block_call(
-        depth_kernel, (scal, meta, jac, pt, ghost_zm, ghost_zp, rem),
+        depth_kernel, (scal, meta, jac, pt, ghost_zm, ghost_zp, stay(rem)),
         [jax.ShapeDtypeStruct((4, 3, H, L), BF)],
         [HALF, turned, z_face, z_face, REM, pltpu.VMEM((4, 3, H, L), BF)],
         "depth", {}, 9_000_000_000,

time: 106 us -> 103 us (0.972)
  local copies, waits for them, and re-layouts: 6.17 us -> 1.8 us
    unnamed x14 -> x2, local copies, waits for them, and re-layouts: 6 us -> 1.63 us
  transfers between devices with their start and end apart: 14 -> 14, of which waited for: 4 -> 4; matrix products, arithmetic and copies ran while one was open for 0% -> 0% of each run, Pallas kernels for 31% -> 32%
where the time goes in v5:
time: 103 us
  Pallas kernels  43.6 us (42%)
  starting transfers between devices  25.1 us (24%)
  waiting for transfers between devices  21.4 us (21%)
  blocking collectives  9.86 us (10%)
  local copies, waits for them, and re-layouts  1.8 us (2%)
    pallas_call x3, Pallas kernels, block_call(): pl.pallas_call(kernel, in_specs=[smem(), smem()] + [anywhere()] * (len(op...  32.5 us
    all_to_all x1, blocking collectives, to_owner_row(): return lax.all_to_all(rows, 'zz', split_axis=0, concat_axis=0, tiled=True)  9.86 us
    ppermute x2, waiting for transfers between devices, along_ring(): up = lax.ppermute(held, 'yy', UP)  9.7 us
    ppermute x2, waiting for transfers between devices, forward(): lax.ppermute(up[2:], 'yy', [(3, 0)])  6.95 us
    ppermute x1, starting transfers between devices, body(): ghost_zp = lax.ppermute(pz0, gz, [((i + 1) % 16, i) for i in range(16)])  6.57 us
    ppermute x2, starting transfers between devices, along_ring(): down = lax.ppermute(held, 'yy', DOWN)  6.47 us
    pallas_call x1, Pallas kernels, final_call(): pl.pallas_call(final_kernel, in_specs=[smem()] + [vmem()] * 10, out_specs...  5.93 us
    pallas_call x1, Pallas kernels, pack_call(): pl.pallas_call(pack_kernel, in_specs=[smem()] + [anywhere()] * 3 + [vmem(...  5.11 us
  transfers between devices with their start and end apart: 14, of which 4 were waited for; matrix products, arithmetic and copies ran while one was open for 0% of the time, Pallas kernels for 32%

profile of v5, /device:TPU:0, one launch (start us, length us, event | category | flops | bytes accessed | tf_op | source)
XLA Modules:
  0.0 102.6 jit_solution(2654037715207177891)
XLA Ops:
  0.6 0.1 stack.35.scal
  0.7 1.6 %copy-done = bf16[32,135,135]{2,0,1:T(8,128)(2,1)S(1)} copy-done((bf16[32,135,135]{2,0,1:T(8,128)(2,1)S(1)}, bf16[32,135,135]{2,0,1:T(8,128)(2,1)}, u32[]{:S(2)}) %copy-start) | copy-done | bytes 1166424
  2.4 5.1 %pack.1 = (s32[40]{0:T(128)S(1)}, bf16[17,136,128]{2,1,0:T(8,128)(2,1)}, bf16[17,136,128]{2,1,0:T(8,128)(2,1)}, bf16[10,136,128]{2,1,0:T(8,128)(2,1)S(1)}, bf16[...) custom-call(s32[7]{0:T(128)S(1)} %stack.35.scal, ...), custom_call_target="tpu_custom_call" | custom-call | tf_op jit(solution)/shard_map/pack/pallas_call | solution.py:120
  7.5 0.1 collective-permute-start
  7.6 1.6 %collective-permute-start.1 = (bf16[10,136,128]{2,1,0:T(8,128)(2,1)S(1)}, bf16[10,136,128]{2,1,0:T(8,128)(2,1)S(1)}, u32[]{:S(2)}, u32[]{:S(2)}) collective-permute-start(bf16[10,136,128]{2,1,0:T(8,128)(2,1)S(1)} %get-tuple-element.22), channel_id=1, source_target_pairs={{0,16},{16,32},{32,48},{48,0},{1,17},{17,33},{33,49},{49,1},{2,18}... | collective-permute-start | bytes 1044488 | tf_op jit(solution)/shard_map/ppermute | solution.py:491
  9.2 1.7 %collective-permute-start.2 = (bf16[10,136,128]{2,1,0:T(8,128)(2,1)S(1)}, bf16[10,136,128]{2,1,0:T(8,128)(2,1)S(1)}, u32[]{:S(2)}, u32[]{:S(2)}) collective-permute-start(bf16[10,136,128]{2,1,0:T(8,128)(2,1)S(1)} %get-tuple-element.23), channel_id=1, source_target_pairs={{16,0},{32,16},{48,32},{0,48},{17,1},{33,17},{49,33},{1,49},{18,2}... | collective-permute-start | bytes 1044488 | tf_op jit(solution)/shard_map/ppermute | solution.py:492
  10.9 6.6 %collective-permute-start.4 = (bf16[17,136,128]{2,1,0:T(8,128)(2,1)}, bf16[17,136,128]{2,1,0:T(8,128)(2,1)}, u32[]{:S(2)}, u32[]{:S(2)}) collective-permute-start(bf16[17,136,128]{2,1,0:T(8,128)(2,1)} %get-tuple-element.18.pz0), channel_id=1, source_target_pairs={{1,0},{2,1},{3,2},{4,3},{5,4},{6,5},{7,6},{8,7},{9,8},{10,9},{11,1... | collective-permute-start | bytes 1775624 | tf_op jit(solution)/shard_map/ppermute | solution.py:490
  17.4 0.0 collective-permute-start.3
  17.4 14.5 %centre.1 = (bf16[4,5,136,128]{3,2,1,0:T(8,128)(2,1)}, f32[4,136,128]{2,1,0:T(8,128)}) custom-call(s32[7]{0:T(128)S(1)} %stack.35.scal, s32[40]{0:T(128)S(1)} %get-tuple-element.17.meta, bf16[7,135,32,135]{3,2,1,0:T(8,128)(2,1)} %bitcast.13, bf16[17,136,128]{2,1,0:T(8,128)(2,1)} %get-tuple-element.18.pz0, bf16[17,136,128]{2,1,0:T(8,128)(2,1)} %get-tuple-element.19.pz1, ...), custom_call_target="tpu_custom_call" | custom-call | flops 17999998976 | bytes 1000000 | tf_op jit(solution)/shard_map/centre/pallas_call | solution.py:374
  32.0 0.0 collective-permute-done.gx
  32.0 0.0 collective-permute-done.1.gym
  32.0 0.0 collective-permute-done.2.gyp
  32.0 11.4 %sides.1 = (bf16[4,5,136,128]{3,2,1,0:T(8,128)(2,1)}, f32[4,136,128]{2,1,0:T(8,128)}) custom-call(s32[7]{0:T(128)S(1)} %stack.35.scal, s32[40]{0:T(128)S(1)} %get-tuple-element.17.meta, bf16[7,135,32,135]{3,2,1,0:T(8,128)(2,1)} %bitcast.14, bf16[17,136,128]{2,1,0:T(8,128)(2,1)} %get-tuple-element.18.pz0, ...), custom_call_target="tpu_custom_call", output_to_operand_aliasing={{0}: (10, {})} | custom-call | flops 12000000000 | bytes 1000000 | tf_op jit(solution)/shard_map/sides/pallas_call | solution.py:374
  43.5 3.5 %all-to-all-start = ((bf16[4,5,136,128]{3,2,1,0:T(8,128)(2,1)}), bf16[4,5,136,128]{3,2,1,0:T(8,128)(2,1)S(1)}, u32[]{:S(2)}, u32[]{:S(2)}) async-start(bf16[4,5,136,128]{3,2,1,0:T(8,128)(2,1)} %get-tuple-element.26), calls=%async_computation | async-start | bytes 1392640 | tf_op jit(solution)/shard_map/all_to_all | solution.py:462
  47.0 0.0 collective-permute-done.4.gzp
  47.0 0.0 collective-permute-done.3.gzm
  47.0 6.5 %depth.1 = bf16[4,3,136,128]{3,2,1,0:T(8,128)(2,1)S(1)} custom-call(s32[7]{0:T(128)S(1)} %stack.35.scal, s32[40]{0:T(128)S(1)} %get-tuple-element.17.meta, bf16[7,135,32,135]{3,2,1,0:T(8,128)(2,1)} %bitcast.15, bf16[32,136,136]{2,1,0:T(8,128)(2,1)S(1)} %get-tuple-element.20.pt, bf16[17,136,128]{2,1,0:T(8,128)(2,1)} %collective-permute-done.3.gzm, ...), custom_call_target="tpu_custom_call" | custom-call | flops 8999999488 | bytes 1000000 | tf_op jit(solution)/shard_map/depth/pallas_call | solution.py:374
  53.5 4.8 %all-to-all-done.refs_0_ = bf16[4,5,136,128]{3,2,1,0:T(8,128)(2,1)S(1)} async-done(((bf16[4,5,136,128]{3,2,1,0:T(8,128)(2,1)}), bf16[4,5,136,128]{3,2,1,0:T(8,128)(2,1)S(1)}, u32[]{:S(2)}, u32[]{:S(2)}) %all-to-all-start) | async-done | bytes 696352 | tf_op jit(solution)/shard_map/all_to_all | solution.py:462
  58.3 0.0 collective-permute-start.6
  58.3 3.2 %collective-permute-start.5 = (bf16[4,5,136,128]{3,2,1,0:T(8,128)(2,1)S(1)}, bf16[4,5,136,128]{3,2,1,0:T(8,128)(2,1)S(1)}, u32[]{:S(2)}, u32[]{:S(2)}) collective-permute-start(bf16[4,5,136,128]{3,2,1,0:T(8,128)(2,1)S(1)} %all-to-all-done.refs_0_), channel_id=1, source_target_pairs={{1,0},{2,1},{3,2},{0,3},{5,4},{6,5},{7,6},{4,7},{9,8},{10,9},{11,1... | collective-permute-start | bytes 2088968 | tf_op jit(solution)/shard_map/ppermute | solution.py:466
  61.5 9.9 %all_to_all.10.refs_5_ = bf16[4,3,136,128]{3,2,1,0:T(8,128)(2,1)S(1)} all-to-all(bf16[4,3,136,128]{3,2,1,0:T(8,128)(2,1)S(1)} %depth.1), channel_id=1, replica_groups=mesh['gx'=2,'gy'=4,'zz'=4,'yy'=4] {'zz'}, dimensions={0} | all-to-all | bytes 835584 | tf_op jit(solution)/shard_map/all_to_all | solution.py:462
  71.4 3.2 %collective-permute-start.9 = (bf16[4,3,136,128]{3,2,1,0:T(8,128)(2,1)S(1)}, bf16[4,3,136,128]{3,2,1,0:T(8,128)(2,1)S(1)}, u32[]{:S(2)}, u32[]{:S(2)}) collective-permute-start(bf16[4,3,136,128]{3,2,1,0:T(8,128)(2,1)S(1)} %all_to_all.10.refs_5_), channel_id=1, source_target_pairs={{1,0},{2,1},{3,2},{0,3},{5,4},{6,5},{7,6},{4,7},{9,8},{10,9},{11,1... | collective-permute-start | bytes 1253384 | tf_op jit(solution)/shard_map/ppermute | solution.py:466
  74.6 3.4 %collective-permute-done.6.refs_2_ = bf16[4,5,136,128]{3,2,1,0:T(8,128)(2,1)S(1)} collective-permute-done((bf16[4,5,136,128]{3,2,1,0:T(8,128)(2,1)S(1)}, bf16[4,5,136,128]{3,2,1,0:T(8,128)(2,1)S(1)}, u32[]{:S(2)}, u32[]{:S(2)}) %collective-permute-start.6) | collective-permute-done | bytes 696352 | tf_op jit(solution)/shard_map/ppermute | solution.py:467
  78.1 1.3 %collective-permute-start.8 = (bf16[2,5,136,128]{3,2,1,0:T(8,128)(2,1)S(1)}, bf16[2,5,136,128]{3,2,1,0:T(8,128)(2,1)S(1)}, u32[]{:S(2)}, u32[]{:S(2)}) collective-permute-start(bf16[2,5,136,128]{3,2,1,0:T(8,128)(2,1)S(1)} %slice.17), channel_id=1, source_target_pairs={{3,0},{7,4},{11,8},{15,12},{19,16},{23,20},{27,24},{31,28},{35,32}... | collective-permute-start | bytes 1044488 | tf_op jit(solution)/shard_map/ppermute | solution.py:472
  79.4 0.0 collective-permute-done.5.refs_1_
  79.4 1.3 %collective-permute-start.7 = (bf16[2,5,136,128]{3,2,1,0:T(8,128)(2,1)S(1)}, bf16[2,5,136,128]{3,2,1,0:T(8,128)(2,1)S(1)}, u32[]{:S(2)}, u32[]{:S(2)}) collective-permute-start(bf16[2,5,136,128]{3,2,1,0:T(8,128)(2,1)S(1)} %slice.16), channel_id=1, source_target_pairs={{1,0},{5,4},{9,8},{13,12},{17,16},{21,20},{25,24},{29,28},{33,32},... | collective-permute-start | bytes 1044488 | tf_op jit(solution)/shard_map/ppermute | solution.py:472
  80.7 6.3 %collective-permute-done.10.refs_7_ = bf16[4,3,136,128]{3,2,1,0:T(8,128)(2,1)S(1)} collective-permute-done((bf16[4,3,136,128]{3,2,1,0:T(8,128)(2,1)S(1)}, bf16[4,3,136,128]{3,2,1,0:T(8,128)(2,1)S(1)}, u32[]{:S(2)}, u32[]{:S(2)}) %collective-permute-start.10) | collective-permute-done | bytes 417824 | tf_op jit(solution)/shard_map/ppermute | solution.py:467
  87.0 1.3 %collective-permute-start.12 = (bf16[2,3,136,128]{3,2,1,0:T(8,128)(2,1)S(1)}, bf16[2,3,136,128]{3,2,1,0:T(8,128)(2,1)S(1)}, u32[]{:S(2)}, u32[]{:S(2)}) collective-permute-start(bf16[2,3,136,128]{3,2,1,0:T(8,128)(2,1)S(1)} %slice.19), channel_id=1, source_target_pairs={{3,0},{7,4},{11,8},{15,12},{19,16},{23,20},{27,24},{31,28},{35,32}... | collective-permute-start | bytes 626696 | tf_op jit(solution)/shard_map/ppermute | solution.py:472
  88.3 0.0 collective-permute-done.9.refs_6_
  88.4 1.3 %collective-permute-start.11 = (bf16[2,3,136,128]{3,2,1,0:T(8,128)(2,1)S(1)}, bf16[2,3,136,128]{3,2,1,0:T(8,128)(2,1)S(1)}, u32[]{:S(2)}, u32[]{:S(2)}) collective-permute-start(bf16[2,3,136,128]{3,2,1,0:T(8,128)(2,1)S(1)} %slice.18), channel_id=1, source_target_pairs={{1,0},{5,4},{9,8},{13,12},{17,16},{21,20},{25,24},{29,28},{33,32},... | collective-permute-start | bytes 626696 | tf_op jit(solution)/shard_map/ppermute | solution.py:472
  89.7 6.9 %collective-permute-done.12.refs_9_ = bf16[2,3,136,128]{3,2,1,0:T(8,128)(2,1)S(1)} collective-permute-done((bf16[2,3,136,128]{3,2,1,0:T(8,128)(2,1)S(1)}, bf16[2,3,136,128]{3,2,1,0:T(8,128)(2,1)S(1)}, u32[]{:S(2)}, u32[]{:S(2)}) %collective-permute-start.12) | collective-permute-done | bytes 208928 | tf_op jit(solution)/shard_map/ppermute | solution.py:472
  96.6 5.9 %assemble.1 = (bf16[7,135,16,135]{3,2,1,0:T(8,128)(2,1)}, bf16[16,135]{1,0:T(8,128)(2,1)}) custom-call(s32[7]{0:T(128)S(1)} %stack.35.scal, bf16[4,5,136,128]{3,2,1,0:T(8,128)(2,1)S(1)} %all-to-all-done.refs_0_, bf16[4,5,136,128]{3,2,1,0:T(8,128)(2,1)S(1)} %collective-permute-done.5.refs_1_, bf16[4,5,136,128]{3,2,1,0:T(8,128)(2,1)S(1)} %collective-permute-done.6.refs_2_, ...), custom_call_target="tpu_custom_call" | custom-call | tf_op jit(solution)/shard_map/assemble/pallas_call | solution.py:441
  (9 shorter events, 0.1 us)
Async XLA Ops:
  0.7 1.6 %copy-start = (bf16[32,135,135]{2,0,1:T(8,128)(2,1)S(1)}, bf16[32,135,135]{2,0,1:T(8,128)(2,1)}, u32[]{:S(2)}) copy-start(bf16[32,135,135]{2,0,1:T(8,128)(2,1)} %param.7) | copy-start | bytes 3499204
  7.5 24.5 %collective-permute-start = (bf16[10,136,128]{2,1,0:T(8,128)(2,1)S(1)}, bf16[10,136,128]{2,1,0:T(8,128)(2,1)S(1)}, u32[]{:S(2)}, u32[]{:S(2)}) collective-permute-start(bf16[10,136,128]{2,1,0:T(8,128)(2,1)S(1)} %get-tuple-element.21), channel_id=1, source_target_pairs={{0,64},{64,0},{1,65},{65,1},{2,66},{66,2},{3,67},{67,3},{4,68},{68... | collective-permute-start | bytes 1044488 | tf_op jit(solution)/shard_map/ppermute | solution.py:488
  7.6 24.4 %collective-permute-start.1 = (bf16[10,136,128]{2,1,0:T(8,128)(2,1)S(1)}, bf16[10,136,128]{2,1,0:T(8,128)(2,1)S(1)}, u32[]{:S(2)}, u32[]{:S(2)}) collective-permute-start(bf16[10,136,128]{2,1,0:T(8,128)(2,1)S(1)} %get-tuple-element.22), channel_id=1, source_target_pairs={{0,16},{16,32},{32,48},{48,0},{1,17},{17,33},{33,49},{49,1},{2,18}... | collective-permute-start | bytes 1044488 | tf_op jit(solution)/shard_map/ppermute | solution.py:491
  9.2 22.8 %collective-permute-start.2 = (bf16[10,136,128]{2,1,0:T(8,128)(2,1)S(1)}, bf16[10,136,128]{2,1,0:T(8,128)(2,1)S(1)}, u32[]{:S(2)}, u32[]{:S(2)}) collective-permute-start(bf16[10,136,128]{2,1,0:T(8,128)(2,1)S(1)} %get-tuple-element.23), channel_id=1, source_target_pairs={{16,0},{32,16},{48,32},{0,48},{17,1},{33,17},{49,33},{1,49},{18,2}... | collective-permute-start | bytes 1044488 | tf_op jit(solution)/shard_map/ppermute | solution.py:492
  10.9 36.1 %collective-permute-start.4 = (bf16[17,136,128]{2,1,0:T(8,128)(2,1)}, bf16[17,136,128]{2,1,0:T(8,128)(2,1)}, u32[]{:S(2)}, u32[]{:S(2)}) collective-permute-start(bf16[17,136,128]{2,1,0:T(8,128)(2,1)} %get-tuple-element.18.pz0), channel_id=1, source_target_pairs={{1,0},{2,1},{3,2},{4,3},{5,4},{6,5},{7,6},{8,7},{9,8},{10,9},{11,1... | collective-permute-start | bytes 1775624 | tf_op jit(solution)/shard_map/ppermute | solution.py:490
  17.4 29.5 %collective-permute-start.3 = (bf16[17,136,128]{2,1,0:T(8,128)(2,1)}, bf16[17,136,128]{2,1,0:T(8,128)(2,1)}, u32[]{:S(2)}, u32[]{:S(2)}) collective-permute-start(bf16[17,136,128]{2,1,0:T(8,128)(2,1)} %get-tuple-element.19.pz1), channel_id=1, source_target_pairs={{0,1},{1,2},{2,3},{3,4},{4,5},{5,6},{6,7},{7,8},{8,9},{9,10},{10,1... | collective-permute-start | bytes 1775624 | tf_op jit(solution)/shard_map/ppermute | solution.py:489
  43.5 14.8 %all-to-all-start = ((bf16[4,5,136,128]{3,2,1,0:T(8,128)(2,1)}), bf16[4,5,136,128]{3,2,1,0:T(8,128)(2,1)S(1)}, u32[]{:S(2)}, u32[]{:S(2)}) async-start(bf16[4,5,136,128]{3,2,1,0:T(8,128)(2,1)} %get-tuple-element.26), calls=%async_computation | async-start | bytes 1392640 | tf_op jit(solution)/shard_map/all_to_all | solution.py:462
  58.3 19.8 %collective-permute-start.6 = (bf16[4,5,136,128]{3,2,1,0:T(8,128)(2,1)S(1)}, bf16[4,5,136,128]{3,2,1,0:T(8,128)(2,1)S(1)}, u32[]{:S(2)}, u32[]{:S(2)}) collective-permute-start(bf16[4,5,136,128]{3,2,1,0:T(8,128)(2,1)S(1)} %all-to-all-done.refs_0_), channel_id=1, source_target_pairs={{3,0},{0,1},{1,2},{2,3},{7,4},{4,5},{5,6},{6,7},{11,8},{8,9},{9,10... | collective-permute-start | bytes 2088968 | tf_op jit(solution)/shard_map/ppermute | solution.py:467
  58.3 21.1 %collective-permute-start.5 = (bf16[4,5,136,128]{3,2,1,0:T(8,128)(2,1)S(1)}, bf16[4,5,136,128]{3,2,1,0:T(8,128)(2,1)S(1)}, u32[]{:S(2)}, u32[]{:S(2)}) collective-permute-start(bf16[4,5,136,128]{3,2,1,0:T(8,128)(2,1)S(1)} %all-to-all-done.refs_0_), channel_id=1, source_target_pairs={{1,0},{2,1},{3,2},{0,3},{5,4},{6,5},{7,6},{4,7},{9,8},{10,9},{11,1... | collective-permute-start | bytes 2088968 | tf_op jit(solution)/shard_map/ppermute | solution.py:466
  71.4 15.6 %collective-permute-start.10 = (bf16[4,3,136,128]{3,2,1,0:T(8,128)(2,1)S(1)}, bf16[4,3,136,128]{3,2,1,0:T(8,128)(2,1)S(1)}, u32[]{:S(2)}, u32[]{:S(2)}) collective-permute-start(bf16[4,3,136,128]{3,2,1,0:T(8,128)(2,1)S(1)} %all_to_all.10.refs_5_), channel_id=1, source_target_pairs={{3,0},{0,1},{1,2},{2,3},{7,4},{4,5},{5,6},{6,7},{11,8},{8,9},{9,10... | collective-permute-start | bytes 1253384 | tf_op jit(solution)/shard_map/ppermute | solution.py:467
  71.4 16.9 %collective-permute-start.9 = (bf16[4,3,136,128]{3,2,1,0:T(8,128)(2,1)S(1)}, bf16[4,3,136,128]{3,2,1,0:T(8,128)(2,1)S(1)}, u32[]{:S(2)}, u32[]{:S(2)}) collective-permute-start(bf16[4,3,136,128]{3,2,1,0:T(8,128)(2,1)S(1)} %all_to_all.10.refs_5_), channel_id=1, source_target_pairs={{1,0},{2,1},{3,2},{0,3},{5,4},{6,5},{7,6},{4,7},{9,8},{10,9},{11,1... | collective-permute-start | bytes 1253384 | tf_op jit(solution)/shard_map/ppermute | solution.py:466
  78.1 18.5 %collective-permute-start.8 = (bf16[2,5,136,128]{3,2,1,0:T(8,128)(2,1)S(1)}, bf16[2,5,136,128]{3,2,1,0:T(8,128)(2,1)S(1)}, u32[]{:S(2)}, u32[]{:S(2)}) collective-permute-start(bf16[2,5,136,128]{3,2,1,0:T(8,128)(2,1)S(1)} %slice.17), channel_id=1, source_target_pairs={{3,0},{7,4},{11,8},{15,12},{19,16},{23,20},{27,24},{31,28},{35,32}... | collective-permute-start | bytes 1044488 | tf_op jit(solution)/shard_map/ppermute | solution.py:472
  79.4 17.2 %collective-permute-start.7 = (bf16[2,5,136,128]{3,2,1,0:T(8,128)(2,1)S(1)}, bf16[2,5,136,128]{3,2,1,0:T(8,128)(2,1)S(1)}, u32[]{:S(2)}, u32[]{:S(2)}) collective-permute-start(bf16[2,5,136,128]{3,2,1,0:T(8,128)(2,1)S(1)} %slice.16), channel_id=1, source_target_pairs={{1,0},{5,4},{9,8},{13,12},{17,16},{21,20},{25,24},{29,28},{33,32},... | collective-permute-start | bytes 1044488 | tf_op jit(solution)/shard_map/ppermute | solution.py:472
  87.0 9.6 %collective-permute-start.12 = (bf16[2,3,136,128]{3,2,1,0:T(8,128)(2,1)S(1)}, bf16[2,3,136,128]{3,2,1,0:T(8,128)(2,1)S(1)}, u32[]{:S(2)}, u32[]{:S(2)}) collective-permute-start(bf16[2,3,136,128]{3,2,1,0:T(8,128)(2,1)S(1)} %slice.19), channel_id=1, source_target_pairs={{3,0},{7,4},{11,8},{15,12},{19,16},{23,20},{27,24},{31,28},{35,32}... | collective-permute-start | bytes 626696 | tf_op jit(solution)/shard_map/ppermute | solution.py:472
  88.4 8.2 %collective-permute-start.11 = (bf16[2,3,136,128]{3,2,1,0:T(8,128)(2,1)S(1)}, bf16[2,3,136,128]{3,2,1,0:T(8,128)(2,1)S(1)}, u32[]{:S(2)}, u32[]{:S(2)}) collective-permute-start(bf16[2,3,136,128]{3,2,1,0:T(8,128)(2,1)S(1)} %slice.18), channel_id=1, source_target_pairs={{1,0},{5,4},{9,8},{13,12},{17,16},{21,20},{25,24},{29,28},{33,32},... | collective-permute-start | bytes 626696 | tf_op jit(solution)/shard_map/ppermute | solution.py:472

commit v6 on v5

--- a/solution.py
+++ b/solution.py
@@ -36,17 +36,17 @@
     return pl.BlockSpec(memory_space=pltpu.VMEM)
 
 
-def spread(block, main, rest):
+def spread(block, main, rest, base=0, count=W):
     def step(i, carry):
-        for u in range(5):
-            row = i * 5 + u
+        for u in range(9):
+            row = base + i * 9 + u
             values = block(row).astype(F32)
             at = pl.ds(row * PE, E)
             main[at, :] = values[:, :L]
             rest[at, 0:R] = values[:, L:]
         return carry
 
-    lax.fori_loop(0, W // 5, step, 0)
+    lax.fori_loop(0, count // 9, step, 0)
 
 
 def clear(main, rest):
@@ -59,9 +59,33 @@
 
 
 def pack_kernel(
-    scal, nbr_in, agg_in, own_in, p_ref, meta, pz0, pz1, xs, ys0, ys1, pt, main, rest, nbr, agg, own, sems
+    scal, nbr_in, agg_in, own_in, p_in, meta, pz0_out, pz1_out, xs_out, ys0_out, ys1_out, pt_out,
+    main, rest, nbr, agg, own, p_ref, pz0, pz1, xs, ys0, ys1, pt, sems, p_sems, out_sems,
 ):
     pz, ys = (pz0, pz1), (ys0, ys1)
+    chunk = W // 5
+    p_copies = [
+        pltpu.make_async_copy(
+            p_in.at[pl.ds(i * chunk, chunk)], p_ref.at[pl.ds(i * chunk, chunk)], p_sems.at[i]
+        )
+        for i in range(5)
+    ]
+    for copy in p_copies:
+        copy.start()
+    out_copies = [
+        pltpu.make_async_copy(a, b, out_sems.at[i])
+        for i, (a, b) in enumerate(
+            [
+                (pz0, pz0_out),
+                (pt.at[pl.ds(0, 16)], pt_out.at[pl.ds(0, 16)]),
+                (pz1, pz1_out),
+                (pt.at[pl.ds(16, 16)], pt_out.at[pl.ds(16, 16)]),
+                (xs, xs_out),
+                (ys0, ys0_out),
+                (ys1, ys1_out),
+            ]
+        )
+    ]
     base = scal[0]
     copies = [
         pltpu.make_async_copy(a, b, sems.at[i])
@@ -70,7 +94,9 @@
     for copy in copies:
         copy.start()
     clear(main, rest)
-    spread(lambda row: p_ref[row], main, rest)
+    for i in range(5):
+        p_copies[i].wait()
+        spread(lambda row: p_ref[row], main, rest, i * chunk, chunk)
     for copy in copies:
         copy.wait()
 
@@ -105,6 +131,8 @@
             plane = plane + (pltpu.roll(b, R * xy, 1) if xy else b)
             pt[oz * 16 + xy] = jnp.concatenate([a.T, b.T[:8]], axis=0).astype(BF)
         pz[oz][16] = plane.astype(BF)
+        out_copies[2 * oz].start()
+        out_copies[2 * oz + 1].start()
     face = jnp.where(scal[3] == 0, 12, 0)
     for oz in range(2):
         for v in range(4):
@@ -114,13 +142,17 @@
         xs[8 + oz] = pz[oz][16]
         ys[0][8 + oz] = pz[oz][16]
         ys[1][8 + oz] = pz[oz][16]
+    for copy in out_copies[4:]:
+        copy.start()
+    for copy in out_copies:
+        copy.wait()
 
 
 def pack_call(*operands):
     return pl.pallas_call(
         pack_kernel,
-        in_specs=[smem()] + [anywhere()] * 3 + [vmem()],
-        out_specs=[smem()] + [vmem()] * 6,
+        in_specs=[smem()] + [anywhere()] * 4,
+        out_specs=[smem()] + [anywhere()] * 6,
         out_shape=[
             jax.ShapeDtypeStruct((40,), jnp.int32),
             jax.ShapeDtypeStruct((17, H, L), BF),
@@ -136,7 +168,16 @@
             pltpu.SMEM((6, E), jnp.int32),
             pltpu.SMEM((E,), jnp.int32),
             pltpu.SMEM((4,), jnp.int32),
+            pltpu.VMEM((W, E, W), BF),
+            pltpu.VMEM((17, H, L), BF),
+            pltpu.VMEM((17, H, L), BF),
+            pltpu.VMEM((10, H, L), BF),
+            pltpu.VMEM((10, H, L), BF),
+            pltpu.VMEM((10, H, L), BF),
+            pltpu.VMEM((E, H, H), BF),
             pltpu.SemaphoreType.DMA((3,)),
+            pltpu.SemaphoreType.DMA((5,)),
+            pltpu.SemaphoreType.DMA((7,)),
         ],
         compiler_params=pltpu.CompilerParams(vmem_limit_bytes=PACK_LIMIT),
         name="pack",
@@ -482,7 +523,7 @@
     jac = jnp.transpose(jacobian, (1, 2, 0, 3))
     pro = jnp.transpose(prolong, (1, 0, 2))
     meta, pz0, pz1, xs, ys0, ys1, pt = pack_call(
-        scal, stay(neighbours.T), stay(agg_map), stay(owners), pro
+        scal, stay(neighbours.T), stay(agg_map), stay(owners), stay(pro)
     )
     gz = ("zz", "yy")
     ghost_x = lax.ppermute(xs, "gx", [(0, 1), (1, 0)])

time: 103 us -> 102 us (level)
  local copies, waits for them, and re-layouts: 1.8 us -> 0.17 us
    unnamed x2 -> x0, local copies, waits for them, and re-layouts: 1.63 us -> none
    pallas_call x1, Pallas kernels: 5.11 us -> 6.59 us  [pack_call(): pl.pallas_call(pack_kernel, in_specs=[smem()] + [anywhere()] * 4, out_spe...]
  transfers between devices with their start and end apart: 14 -> 14, of which waited for: 4 -> 4; matrix products, arithmetic and copies ran while one was open for 0% -> 0% of each run, Pallas kernels for 32% -> 31%
where the time goes in v6:
time: 102 us
  Pallas kernels  44.5 us (44%)
  starting transfers between devices  25.1 us (25%)
  waiting for transfers between devices  21.5 us (21%)
  blocking collectives  9.86 us (10%)
    pallas_call x3, Pallas kernels, block_call(): pl.pallas_call(kernel, in_specs=[smem(), smem()] + [anywhere()] * (len(op...  32 us
    all_to_all x1, blocking collectives, to_owner_row(): return lax.all_to_all(rows, 'zz', split_axis=0, concat_axis=0, tiled=True)  9.86 us
    ppermute x2, waiting for transfers between devices, along_ring(): up = lax.ppermute(held, 'yy', UP)  9.7 us
    ppermute x2, waiting for transfers between devices, forward(): lax.ppermute(up[2:], 'yy', [(3, 0)])  6.94 us
    pallas_call x1, Pallas kernels, pack_call(): pl.pallas_call(pack_kernel, in_specs=[smem()] + [anywhere()] * 4, out_spe...  6.59 us
    ppermute x1, starting transfers between devices, body(): ghost_zp = lax.ppermute(pz0, gz, [((i + 1) % 16, i) for i in range(16)])  6.57 us
    ppermute x2, starting transfers between devices, along_ring(): down = lax.ppermute(held, 'yy', DOWN)  6.47 us
    pallas_call x1, Pallas kernels, final_call(): pl.pallas_call(final_kernel, in_specs=[smem()] + [vmem()] * 10, out_specs...  5.93 us
  transfers between devices with their start and end apart: 14, of which 4 were waited for; matrix products, arithmetic and copies ran while one was open for 0% of the time, Pallas kernels for 31%

profile of v6, /device:TPU:0, one launch (start us, length us, event | category | flops | bytes accessed | tf_op | source)
XLA Modules:
  0.0 102.0 jit_solution(10618086490219644175)
XLA Ops:
  0.6 0.1 stack.35.scal
  0.7 6.6 %pack.1 = (s32[40]{0:T(128)S(1)}, bf16[17,136,128]{2,1,0:T(8,128)(2,1)}, bf16[17,136,128]{2,1,0:T(8,128)(2,1)}, bf16[10,136,128]{2,1,0:T(8,128)(2,1)S(1)}, bf16[...) custom-call(s32[7]{0:T(128)S(1)} %stack.35.scal, ...), custom_call_target="tpu_custom_call" | custom-call | tf_op jit(solution)/shard_map/pack/pallas_call | solution.py:152
  7.3 0.1 collective-permute-start
  7.4 1.6 %collective-permute-start.1 = (bf16[10,136,128]{2,1,0:T(8,128)(2,1)S(1)}, bf16[10,136,128]{2,1,0:T(8,128)(2,1)S(1)}, u32[]{:S(2)}, u32[]{:S(2)}) collective-permute-start(bf16[10,136,128]{2,1,0:T(8,128)(2,1)S(1)} %get-tuple-element.22), channel_id=1, source_target_pairs={{0,16},{16,32},{32,48},{48,0},{1,17},{17,33},{33,49},{49,1},{2,18}... | collective-permute-start | bytes 1044488 | tf_op jit(solution)/shard_map/ppermute | solution.py:532
  9.1 1.7 %collective-permute-start.2 = (bf16[10,136,128]{2,1,0:T(8,128)(2,1)S(1)}, bf16[10,136,128]{2,1,0:T(8,128)(2,1)S(1)}, u32[]{:S(2)}, u32[]{:S(2)}) collective-permute-start(bf16[10,136,128]{2,1,0:T(8,128)(2,1)S(1)} %get-tuple-element.23), channel_id=1, source_target_pairs={{16,0},{32,16},{48,32},{0,48},{17,1},{33,17},{49,33},{1,49},{18,2}... | collective-permute-start | bytes 1044488 | tf_op jit(solution)/shard_map/ppermute | solution.py:533
  10.7 6.6 %collective-permute-start.4 = (bf16[17,136,128]{2,1,0:T(8,128)(2,1)}, bf16[17,136,128]{2,1,0:T(8,128)(2,1)}, u32[]{:S(2)}, u32[]{:S(2)}) collective-permute-start(bf16[17,136,128]{2,1,0:T(8,128)(2,1)} %get-tuple-element.18.pz0), channel_id=1, source_target_pairs={{1,0},{2,1},{3,2},{4,3},{5,4},{6,5},{7,6},{8,7},{9,8},{10,9},{11,1... | collective-permute-start | bytes 1775624 | tf_op jit(solution)/shard_map/ppermute | solution.py:531
  17.3 0.0 collective-permute-start.3
  17.3 14.3 %centre.1 = (bf16[4,5,136,128]{3,2,1,0:T(8,128)(2,1)}, f32[4,136,128]{2,1,0:T(8,128)}) custom-call(s32[7]{0:T(128)S(1)} %stack.35.scal, s32[40]{0:T(128)S(1)} %get-tuple-element.17.meta, bf16[7,135,32,135]{3,2,1,0:T(8,128)(2,1)} %bitcast.13, bf16[17,136,128]{2,1,0:T(8,128)(2,1)} %get-tuple-element.18.pz0, bf16[17,136,128]{2,1,0:T(8,128)(2,1)} %get-tuple-element.19.pz1, ...), custom_call_target="tpu_custom_call" | custom-call | flops 17999998976 | bytes 1000000 | tf_op jit(solution)/shard_map/centre/pallas_call | solution.py:415
  31.6 0.0 collective-permute-done.gx
  31.6 0.0 collective-permute-done.1.gym
  31.6 0.0 collective-permute-done.2.gyp
  31.6 11.3 %sides.1 = (bf16[4,5,136,128]{3,2,1,0:T(8,128)(2,1)}, f32[4,136,128]{2,1,0:T(8,128)}) custom-call(s32[7]{0:T(128)S(1)} %stack.35.scal, s32[40]{0:T(128)S(1)} %get-tuple-element.17.meta, bf16[7,135,32,135]{3,2,1,0:T(8,128)(2,1)} %bitcast.14, bf16[17,136,128]{2,1,0:T(8,128)(2,1)} %get-tuple-element.18.pz0, ...), custom_call_target="tpu_custom_call", output_to_operand_aliasing={{0}: (10, {})} | custom-call | flops 12000000000 | bytes 1000000 | tf_op jit(solution)/shard_map/sides/pallas_call | solution.py:415
  42.9 3.5 %all-to-all-start = ((bf16[4,5,136,128]{3,2,1,0:T(8,128)(2,1)}), bf16[4,5,136,128]{3,2,1,0:T(8,128)(2,1)S(1)}, u32[]{:S(2)}, u32[]{:S(2)}) async-start(bf16[4,5,136,128]{3,2,1,0:T(8,128)(2,1)} %get-tuple-element.26), calls=%async_computation | async-start | bytes 1392640 | tf_op jit(solution)/shard_map/all_to_all | solution.py:503
  46.4 0.0 collective-permute-done.4.gzp
  46.4 0.0 collective-permute-done.3.gzm
  46.4 6.5 %depth.1 = bf16[4,3,136,128]{3,2,1,0:T(8,128)(2,1)S(1)} custom-call(s32[7]{0:T(128)S(1)} %stack.35.scal, s32[40]{0:T(128)S(1)} %get-tuple-element.17.meta, bf16[7,135,32,135]{3,2,1,0:T(8,128)(2,1)} %bitcast.15, bf16[32,136,136]{2,1,0:T(8,128)(2,1)S(1)} %get-tuple-element.20.pt, bf16[17,136,128]{2,1,0:T(8,128)(2,1)} %collective-permute-done.3.gzm, ...), custom_call_target="tpu_custom_call" | custom-call | flops 8999999488 | bytes 1000000 | tf_op jit(solution)/shard_map/depth/pallas_call | solution.py:415
  52.9 4.8 %all-to-all-done.refs_0_ = bf16[4,5,136,128]{3,2,1,0:T(8,128)(2,1)S(1)} async-done(((bf16[4,5,136,128]{3,2,1,0:T(8,128)(2,1)}), bf16[4,5,136,128]{3,2,1,0:T(8,128)(2,1)S(1)}, u32[]{:S(2)}, u32[]{:S(2)}) %all-to-all-start) | async-done | bytes 696352 | tf_op jit(solution)/shard_map/all_to_all | solution.py:503
  57.7 0.0 collective-permute-start.6
  57.7 3.2 %collective-permute-start.5 = (bf16[4,5,136,128]{3,2,1,0:T(8,128)(2,1)S(1)}, bf16[4,5,136,128]{3,2,1,0:T(8,128)(2,1)S(1)}, u32[]{:S(2)}, u32[]{:S(2)}) collective-permute-start(bf16[4,5,136,128]{3,2,1,0:T(8,128)(2,1)S(1)} %all-to-all-done.refs_0_), channel_id=1, source_target_pairs={{1,0},{2,1},{3,2},{0,3},{5,4},{6,5},{7,6},{4,7},{9,8},{10,9},{11,1... | collective-permute-start | bytes 2088968 | tf_op jit(solution)/shard_map/ppermute | solution.py:507
  61.0 9.9 %all_to_all.10.refs_5_ = bf16[4,3,136,128]{3,2,1,0:T(8,128)(2,1)S(1)} all-to-all(bf16[4,3,136,128]{3,2,1,0:T(8,128)(2,1)S(1)} %depth.1), channel_id=1, replica_groups=mesh['gx'=2,'gy'=4,'zz'=4,'yy'=4] {'zz'}, dimensions={0} | all-to-all | bytes 835584 | tf_op jit(solution)/shard_map/all_to_all | solution.py:503
  70.8 0.0 collective-permute-start.10
  70.8 3.2 %collective-permute-start.9 = (bf16[4,3,136,128]{3,2,1,0:T(8,128)(2,1)S(1)}, bf16[4,3,136,128]{3,2,1,0:T(8,128)(2,1)S(1)}, u32[]{:S(2)}, u32[]{:S(2)}) collective-permute-start(bf16[4,3,136,128]{3,2,1,0:T(8,128)(2,1)S(1)} %all_to_all.10.refs_5_), channel_id=1, source_target_pairs={{1,0},{2,1},{3,2},{0,3},{5,4},{6,5},{7,6},{4,7},{9,8},{10,9},{11,1... | collective-permute-start | bytes 1253384 | tf_op jit(solution)/shard_map/ppermute | solution.py:507
  74.1 3.4 %collective-permute-done.6.refs_2_ = bf16[4,5,136,128]{3,2,1,0:T(8,128)(2,1)S(1)} collective-permute-done((bf16[4,5,136,128]{3,2,1,0:T(8,128)(2,1)S(1)}, bf16[4,5,136,128]{3,2,1,0:T(8,128)(2,1)S(1)}, u32[]{:S(2)}, u32[]{:S(2)}) %collective-permute-start.6) | collective-permute-done | bytes 696352 | tf_op jit(solution)/shard_map/ppermute | solution.py:508
  77.5 1.3 %collective-permute-start.8 = (bf16[2,5,136,128]{3,2,1,0:T(8,128)(2,1)S(1)}, bf16[2,5,136,128]{3,2,1,0:T(8,128)(2,1)S(1)}, u32[]{:S(2)}, u32[]{:S(2)}) collective-permute-start(bf16[2,5,136,128]{3,2,1,0:T(8,128)(2,1)S(1)} %slice.17), channel_id=1, source_target_pairs={{3,0},{7,4},{11,8},{15,12},{19,16},{23,20},{27,24},{31,28},{35,32}... | collective-permute-start | bytes 1044488 | tf_op jit(solution)/shard_map/ppermute | solution.py:513
  78.8 0.0 collective-permute-done.5.refs_1_
  78.9 1.3 %collective-permute-start.7 = (bf16[2,5,136,128]{3,2,1,0:T(8,128)(2,1)S(1)}, bf16[2,5,136,128]{3,2,1,0:T(8,128)(2,1)S(1)}, u32[]{:S(2)}, u32[]{:S(2)}) collective-permute-start(bf16[2,5,136,128]{3,2,1,0:T(8,128)(2,1)S(1)} %slice.16), channel_id=1, source_target_pairs={{1,0},{5,4},{9,8},{13,12},{17,16},{21,20},{25,24},{29,28},{33,32},... | collective-permute-start | bytes 1044488 | tf_op jit(solution)/shard_map/ppermute | solution.py:513
  80.2 6.3 %collective-permute-done.10.refs_7_ = bf16[4,3,136,128]{3,2,1,0:T(8,128)(2,1)S(1)} collective-permute-done((bf16[4,3,136,128]{3,2,1,0:T(8,128)(2,1)S(1)}, bf16[4,3,136,128]{3,2,1,0:T(8,128)(2,1)S(1)}, u32[]{:S(2)}, u32[]{:S(2)}) %collective-permute-start.10) | collective-permute-done | bytes 417824 | tf_op jit(solution)/shard_map/ppermute | solution.py:508
  86.5 1.3 %collective-permute-start.12 = (bf16[2,3,136,128]{3,2,1,0:T(8,128)(2,1)S(1)}, bf16[2,3,136,128]{3,2,1,0:T(8,128)(2,1)S(1)}, u32[]{:S(2)}, u32[]{:S(2)}) collective-permute-start(bf16[2,3,136,128]{3,2,1,0:T(8,128)(2,1)S(1)} %slice.19), channel_id=1, source_target_pairs={{3,0},{7,4},{11,8},{15,12},{19,16},{23,20},{27,24},{31,28},{35,32}... | collective-permute-start | bytes 626696 | tf_op jit(solution)/shard_map/ppermute | solution.py:513
  87.8 1.3 %collective-permute-start.11 = (bf16[2,3,136,128]{3,2,1,0:T(8,128)(2,1)S(1)}, bf16[2,3,136,128]{3,2,1,0:T(8,128)(2,1)S(1)}, u32[]{:S(2)}, u32[]{:S(2)}) collective-permute-start(bf16[2,3,136,128]{3,2,1,0:T(8,128)(2,1)S(1)} %slice.18), channel_id=1, source_target_pairs={{1,0},{5,4},{9,8},{13,12},{17,16},{21,20},{25,24},{29,28},{33,32},... | collective-permute-start | bytes 626696 | tf_op jit(solution)/shard_map/ppermute | solution.py:513
  89.1 6.9 %collective-permute-done.12.refs_9_ = bf16[2,3,136,128]{3,2,1,0:T(8,128)(2,1)S(1)} collective-permute-done((bf16[2,3,136,128]{3,2,1,0:T(8,128)(2,1)S(1)}, bf16[2,3,136,128]{3,2,1,0:T(8,128)(2,1)S(1)}, u32[]{:S(2)}, u32[]{:S(2)}) %collective-permute-start.12) | collective-permute-done | bytes 208928 | tf_op jit(solution)/shard_map/ppermute | solution.py:513
  96.0 0.0 collective-permute-done.7.refs_3_
  96.0 5.9 %assemble.1 = (bf16[7,135,16,135]{3,2,1,0:T(8,128)(2,1)}, bf16[16,135]{1,0:T(8,128)(2,1)}) custom-call(s32[7]{0:T(128)S(1)} %stack.35.scal, bf16[4,5,136,128]{3,2,1,0:T(8,128)(2,1)S(1)} %all-to-all-done.refs_0_, bf16[4,5,136,128]{3,2,1,0:T(8,128)(2,1)S(1)} %collective-permute-done.5.refs_1_, bf16[4,5,136,128]{3,2,1,0:T(8,128)(2,1)S(1)} %collective-permute-done.6.refs_2_, ...), custom_call_target="tpu_custom_call" | custom-call | tf_op jit(solution)/shard_map/assemble/pallas_call | solution.py:482
  (7 shorter events, 0.1 us)
Async XLA Ops:
  7.3 24.3 %collective-permute-start = (bf16[10,136,128]{2,1,0:T(8,128)(2,1)S(1)}, bf16[10,136,128]{2,1,0:T(8,128)(2,1)S(1)}, u32[]{:S(2)}, u32[]{:S(2)}) collective-permute-start(bf16[10,136,128]{2,1,0:T(8,128)(2,1)S(1)} %get-tuple-element.21), channel_id=1, source_target_pairs={{0,64},{64,0},{1,65},{65,1},{2,66},{66,2},{3,67},{67,3},{4,68},{68... | collective-permute-start | bytes 1044488 | tf_op jit(solution)/shard_map/ppermute | solution.py:529
  7.4 24.2 %collective-permute-start.1 = (bf16[10,136,128]{2,1,0:T(8,128)(2,1)S(1)}, bf16[10,136,128]{2,1,0:T(8,128)(2,1)S(1)}, u32[]{:S(2)}, u32[]{:S(2)}) collective-permute-start(bf16[10,136,128]{2,1,0:T(8,128)(2,1)S(1)} %get-tuple-element.22), channel_id=1, source_target_pairs={{0,16},{16,32},{32,48},{48,0},{1,17},{17,33},{33,49},{49,1},{2,18}... | collective-permute-start | bytes 1044488 | tf_op jit(solution)/shard_map/ppermute | solution.py:532
  9.1 22.5 %collective-permute-start.2 = (bf16[10,136,128]{2,1,0:T(8,128)(2,1)S(1)}, bf16[10,136,128]{2,1,0:T(8,128)(2,1)S(1)}, u32[]{:S(2)}, u32[]{:S(2)}) collective-permute-start(bf16[10,136,128]{2,1,0:T(8,128)(2,1)S(1)} %get-tuple-element.23), channel_id=1, source_target_pairs={{16,0},{32,16},{48,32},{0,48},{17,1},{33,17},{49,33},{1,49},{18,2}... | collective-permute-start | bytes 1044488 | tf_op jit(solution)/shard_map/ppermute | solution.py:533
  10.7 35.7 %collective-permute-start.4 = (bf16[17,136,128]{2,1,0:T(8,128)(2,1)}, bf16[17,136,128]{2,1,0:T(8,128)(2,1)}, u32[]{:S(2)}, u32[]{:S(2)}) collective-permute-start(bf16[17,136,128]{2,1,0:T(8,128)(2,1)} %get-tuple-element.18.pz0), channel_id=1, source_target_pairs={{1,0},{2,1},{3,2},{4,3},{5,4},{6,5},{7,6},{8,7},{9,8},{10,9},{11,1... | collective-permute-start | bytes 1775624 | tf_op jit(solution)/shard_map/ppermute | solution.py:531
  17.3 29.1 %collective-permute-start.3 = (bf16[17,136,128]{2,1,0:T(8,128)(2,1)}, bf16[17,136,128]{2,1,0:T(8,128)(2,1)}, u32[]{:S(2)}, u32[]{:S(2)}) collective-permute-start(bf16[17,136,128]{2,1,0:T(8,128)(2,1)} %get-tuple-element.19.pz1), channel_id=1, source_target_pairs={{0,1},{1,2},{2,3},{3,4},{4,5},{5,6},{6,7},{7,8},{8,9},{9,10},{10,1... | collective-permute-start | bytes 1775624 | tf_op jit(solution)/shard_map/ppermute | solution.py:530
  42.9 14.8 %all-to-all-start = ((bf16[4,5,136,128]{3,2,1,0:T(8,128)(2,1)}), bf16[4,5,136,128]{3,2,1,0:T(8,128)(2,1)S(1)}, u32[]{:S(2)}, u32[]{:S(2)}) async-start(bf16[4,5,136,128]{3,2,1,0:T(8,128)(2,1)} %get-tuple-element.26), calls=%async_computation | async-start | bytes 1392640 | tf_op jit(solution)/shard_map/all_to_all | solution.py:503
  57.7 19.8 %collective-permute-start.6 = (bf16[4,5,136,128]{3,2,1,0:T(8,128)(2,1)S(1)}, bf16[4,5,136,128]{3,2,1,0:T(8,128)(2,1)S(1)}, u32[]{:S(2)}, u32[]{:S(2)}) collective-permute-start(bf16[4,5,136,128]{3,2,1,0:T(8,128)(2,1)S(1)} %all-to-all-done.refs_0_), channel_id=1, source_target_pairs={{3,0},{0,1},{1,2},{2,3},{7,4},{4,5},{5,6},{6,7},{11,8},{8,9},{9,10... | collective-permute-start | bytes 2088968 | tf_op jit(solution)/shard_map/ppermute | solution.py:508
  57.7 21.1 %collective-permute-start.5 = (bf16[4,5,136,128]{3,2,1,0:T(8,128)(2,1)S(1)}, bf16[4,5,136,128]{3,2,1,0:T(8,128)(2,1)S(1)}, u32[]{:S(2)}, u32[]{:S(2)}) collective-permute-start(bf16[4,5,136,128]{3,2,1,0:T(8,128)(2,1)S(1)} %all-to-all-done.refs_0_), channel_id=1, source_target_pairs={{1,0},{2,1},{3,2},{0,3},{5,4},{6,5},{7,6},{4,7},{9,8},{10,9},{11,1... | collective-permute-start | bytes 2088968 | tf_op jit(solution)/shard_map/ppermute | solution.py:507
  70.8 15.6 %collective-permute-start.10 = (bf16[4,3,136,128]{3,2,1,0:T(8,128)(2,1)S(1)}, bf16[4,3,136,128]{3,2,1,0:T(8,128)(2,1)S(1)}, u32[]{:S(2)}, u32[]{:S(2)}) collective-permute-start(bf16[4,3,136,128]{3,2,1,0:T(8,128)(2,1)S(1)} %all_to_all.10.refs_5_), channel_id=1, source_target_pairs={{3,0},{0,1},{1,2},{2,3},{7,4},{4,5},{5,6},{6,7},{11,8},{8,9},{9,10... | collective-permute-start | bytes 1253384 | tf_op jit(solution)/shard_map/ppermute | solution.py:508
  70.8 16.9 %collective-permute-start.9 = (bf16[4,3,136,128]{3,2,1,0:T(8,128)(2,1)S(1)}, bf16[4,3,136,128]{3,2,1,0:T(8,128)(2,1)S(1)}, u32[]{:S(2)}, u32[]{:S(2)}) collective-permute-start(bf16[4,3,136,128]{3,2,1,0:T(8,128)(2,1)S(1)} %all_to_all.10.refs_5_), channel_id=1, source_target_pairs={{1,0},{2,1},{3,2},{0,3},{5,4},{6,5},{7,6},{4,7},{9,8},{10,9},{11,1... | collective-permute-start | bytes 1253384 | tf_op jit(solution)/shard_map/ppermute | solution.py:507
  77.5 18.5 %collective-permute-start.8 = (bf16[2,5,136,128]{3,2,1,0:T(8,128)(2,1)S(1)}, bf16[2,5,136,128]{3,2,1,0:T(8,128)(2,1)S(1)}, u32[]{:S(2)}, u32[]{:S(2)}) collective-permute-start(bf16[2,5,136,128]{3,2,1,0:T(8,128)(2,1)S(1)} %slice.17), channel_id=1, source_target_pairs={{3,0},{7,4},{11,8},{15,12},{19,16},{23,20},{27,24},{31,28},{35,32}... | collective-permute-start | bytes 1044488 | tf_op jit(solution)/shard_map/ppermute | solution.py:513
  78.9 17.2 %collective-permute-start.7 = (bf16[2,5,136,128]{3,2,1,0:T(8,128)(2,1)S(1)}, bf16[2,5,136,128]{3,2,1,0:T(8,128)(2,1)S(1)}, u32[]{:S(2)}, u32[]{:S(2)}) collective-permute-start(bf16[2,5,136,128]{3,2,1,0:T(8,128)(2,1)S(1)} %slice.16), channel_id=1, source_target_pairs={{1,0},{5,4},{9,8},{13,12},{17,16},{21,20},{25,24},{29,28},{33,32},... | collective-permute-start | bytes 1044488 | tf_op jit(solution)/shard_map/ppermute | solution.py:513
  86.5 9.6 %collective-permute-start.12 = (bf16[2,3,136,128]{3,2,1,0:T(8,128)(2,1)S(1)}, bf16[2,3,136,128]{3,2,1,0:T(8,128)(2,1)S(1)}, u32[]{:S(2)}, u32[]{:S(2)}) collective-permute-start(bf16[2,3,136,128]{3,2,1,0:T(8,128)(2,1)S(1)} %slice.19), channel_id=1, source_target_pairs={{3,0},{7,4},{11,8},{15,12},{19,16},{23,20},{27,24},{31,28},{35,32}... | collective-permute-start | bytes 626696 | tf_op jit(solution)/shard_map/ppermute | solution.py:513
  87.8 8.2 %collective-permute-start.11 = (bf16[2,3,136,128]{3,2,1,0:T(8,128)(2,1)S(1)}, bf16[2,3,136,128]{3,2,1,0:T(8,128)(2,1)S(1)}, u32[]{:S(2)}, u32[]{:S(2)}) collective-permute-start(bf16[2,3,136,128]{3,2,1,0:T(8,128)(2,1)S(1)} %slice.18), channel_id=1, source_target_pairs={{1,0},{5,4},{9,8},{13,12},{17,16},{21,20},{25,24},{29,28},{33,32},... | collective-permute-start | bytes 626696 | tf_op jit(solution)/shard_map/ppermute | solution.py:513

commit v7 on v6

--- a/solution.py
+++ b/solution.py
@@ -437,7 +437,7 @@
         return held[5 * part + which][row, plane].astype(F32)
 
     def out_copy(k):
-        return pltpu.make_async_copy(out.at[k % 2], coarse.at[k], out_sems.at[k])
+        return pltpu.make_async_copy(out.at[k % 3], coarse.at[k], out_sems.at[k])
 
     @pl.when(scal[4] == 0)
     def _():
@@ -456,14 +456,14 @@
                 s1[pl.ds(slot, H, stride=PS), :] = plane_of([4, 0, 1, 2, 3, 5, 6][k], slot)
                 tail = plane_of(7, slot)
                 s2[pl.ds(slot, H, stride=PS), :] = pltpu.roll(tail, L - R * k, 1) if k else tail
-            if k >= 2:
-                out_copy(k - 2).wait()
+            if k >= 3:
+                out_copy(k - 3).wait()
 
             def write(i, carry, k=k):
                 for u in range(27):
                     row = i * 27 + u
                     at = pl.ds(row * PS, 16)
-                    out[k % 2, row] = jnp.concatenate([s1[at, :], s2[at, :R]], axis=1).astype(BF)
+                    out[k % 3, row] = jnp.concatenate([s1[at, :], s2[at, :R]], axis=1).astype(BF)
                 return carry
 
             lax.fori_loop(0, W // 27, write, 0)
@@ -473,8 +473,8 @@
             turned = pltpu.roll(plane_of(7, slot), (slot - 49 + L) % L, 1)
             acc = jnp.where(lane == slot, turned, acc)
         restricted[...] = acc.T[:16, :W].astype(BF)
-        out_copy(5).wait()
-        out_copy(6).wait()
+        for k in range(4, 7):
+            out_copy(k).wait()
 
 
 def final_call(scal, rows):
@@ -485,7 +485,7 @@
         out_specs=[anywhere(), vmem()],
         out_shape=[jax.ShapeDtypeStruct((7, W, 16, W), BF), jax.ShapeDtypeStruct((16, W), BF)],
         scratch_shapes=[
-            pltpu.VMEM((2, W, 16, W), BF),
+            pltpu.VMEM((3, W, 16, W), BF),
             pltpu.VMEM((H * PS, L), F32),
             pltpu.VMEM((H * PS, L), F32),
             pltpu.SemaphoreType.DMA((7,)),

time: 102 us -> 102 us (level)
  transfers between devices with their start and end apart: 14 -> 14, of which waited for: 4 -> 4; matrix products, arithmetic and copies ran while one was open for 0% -> 0% of each run, Pallas kernels for 31% -> 32%
where the time goes in v7:
time: 102 us; the launch traced here: 101 us
  Pallas kernels  43.8 us (43%)
  starting transfers between devices  25.1 us (25%)
  waiting for transfers between devices  21.5 us (21%)
  blocking collectives  9.86 us (10%)
    pallas_call x3, Pallas kernels, block_call(): pl.pallas_call(kernel, in_specs=[smem(), smem()] + [anywhere()] * (len(op...  32 us
    all_to_all x1, blocking collectives, to_owner_row(): return lax.all_to_all(rows, 'zz', split_axis=0, concat_axis=0, tiled=True)  9.86 us
    ppermute x2, waiting for transfers between devices, along_ring(): up = lax.ppermute(held, 'yy', UP)  9.7 us
    ppermute x2, waiting for transfers between devices, forward(): lax.ppermute(up[2:], 'yy', [(3, 0)])  6.95 us
    pallas_call x1, Pallas kernels, pack_call(): pl.pallas_call(pack_kernel, in_specs=[smem()] + [anywhere()] * 4, out_spe...  6.59 us
    ppermute x1, starting transfers between devices, body(): ghost_zp = lax.ppermute(pz0, gz, [((i + 1) % 16, i) for i in range(16)])  6.57 us
    ppermute x2, starting transfers between devices, along_ring(): down = lax.ppermute(held, 'yy', DOWN)  6.47 us
    pallas_call x1, Pallas kernels, final_call(): pl.pallas_call(final_kernel, in_specs=[smem()] + [vmem()] * 10, out_specs...  5.17 us
  transfers between devices with their start and end apart: 14, of which 4 were waited for; matrix products, arithmetic and copies ran while one was open for 0% of the time, Pallas kernels for 32%

profile of v7, /device:TPU:0, one launch (start us, length us, event | category | flops | bytes accessed | tf_op | source)
XLA Modules:
  0.0 101.2 jit_solution(13130733958573817554)
XLA Ops:
  0.6 0.1 stack.35.scal
  0.7 6.6 %pack.1 = (s32[40]{0:T(128)S(1)}, bf16[17,136,128]{2,1,0:T(8,128)(2,1)}, bf16[17,136,128]{2,1,0:T(8,128)(2,1)}, bf16[10,136,128]{2,1,0:T(8,128)(2,1)S(1)}, bf16[...) custom-call(s32[7]{0:T(128)S(1)} %stack.35.scal, ...), custom_call_target="tpu_custom_call" | custom-call | tf_op jit(solution)/shard_map/pack/pallas_call | solution.py:152
  7.3 0.1 collective-permute-start
  7.4 1.6 %collective-permute-start.1 = (bf16[10,136,128]{2,1,0:T(8,128)(2,1)S(1)}, bf16[10,136,128]{2,1,0:T(8,128)(2,1)S(1)}, u32[]{:S(2)}, u32[]{:S(2)}) collective-permute-start(bf16[10,136,128]{2,1,0:T(8,128)(2,1)S(1)} %get-tuple-element.22), channel_id=1, source_target_pairs={{0,16},{16,32},{32,48},{48,0},{1,17},{17,33},{33,49},{49,1},{2,18}... | collective-permute-start | bytes 1044488 | tf_op jit(solution)/shard_map/ppermute | solution.py:532
  9.1 1.7 %collective-permute-start.2 = (bf16[10,136,128]{2,1,0:T(8,128)(2,1)S(1)}, bf16[10,136,128]{2,1,0:T(8,128)(2,1)S(1)}, u32[]{:S(2)}, u32[]{:S(2)}) collective-permute-start(bf16[10,136,128]{2,1,0:T(8,128)(2,1)S(1)} %get-tuple-element.23), channel_id=1, source_target_pairs={{16,0},{32,16},{48,32},{0,48},{17,1},{33,17},{49,33},{1,49},{18,2}... | collective-permute-start | bytes 1044488 | tf_op jit(solution)/shard_map/ppermute | solution.py:533
  10.7 6.6 %collective-permute-start.4 = (bf16[17,136,128]{2,1,0:T(8,128)(2,1)}, bf16[17,136,128]{2,1,0:T(8,128)(2,1)}, u32[]{:S(2)}, u32[]{:S(2)}) collective-permute-start(bf16[17,136,128]{2,1,0:T(8,128)(2,1)} %get-tuple-element.18.pz0), channel_id=1, source_target_pairs={{1,0},{2,1},{3,2},{4,3},{5,4},{6,5},{7,6},{8,7},{9,8},{10,9},{11,1... | collective-permute-start | bytes 1775624 | tf_op jit(solution)/shard_map/ppermute | solution.py:531
  17.3 0.0 collective-permute-start.3
  17.3 14.3 %centre.1 = (bf16[4,5,136,128]{3,2,1,0:T(8,128)(2,1)}, f32[4,136,128]{2,1,0:T(8,128)}) custom-call(s32[7]{0:T(128)S(1)} %stack.35.scal, s32[40]{0:T(128)S(1)} %get-tuple-element.17.meta, bf16[7,135,32,135]{3,2,1,0:T(8,128)(2,1)} %bitcast.13, bf16[17,136,128]{2,1,0:T(8,128)(2,1)} %get-tuple-element.18.pz0, bf16[17,136,128]{2,1,0:T(8,128)(2,1)} %get-tuple-element.19.pz1, ...), custom_call_target="tpu_custom_call" | custom-call | flops 17999998976 | bytes 1000000 | tf_op jit(solution)/shard_map/centre/pallas_call | solution.py:415
  31.6 0.0 collective-permute-done.1.gym
  31.6 0.0 collective-permute-done.2.gyp
  31.6 11.3 %sides.1 = (bf16[4,5,136,128]{3,2,1,0:T(8,128)(2,1)}, f32[4,136,128]{2,1,0:T(8,128)}) custom-call(s32[7]{0:T(128)S(1)} %stack.35.scal, s32[40]{0:T(128)S(1)} %get-tuple-element.17.meta, bf16[7,135,32,135]{3,2,1,0:T(8,128)(2,1)} %bitcast.14, bf16[17,136,128]{2,1,0:T(8,128)(2,1)} %get-tuple-element.18.pz0, ...), custom_call_target="tpu_custom_call", output_to_operand_aliasing={{0}: (10, {})} | custom-call | flops 12000000000 | bytes 1000000 | tf_op jit(solution)/shard_map/sides/pallas_call | solution.py:415
  42.9 3.5 %all-to-all-start = ((bf16[4,5,136,128]{3,2,1,0:T(8,128)(2,1)}), bf16[4,5,136,128]{3,2,1,0:T(8,128)(2,1)S(1)}, u32[]{:S(2)}, u32[]{:S(2)}) async-start(bf16[4,5,136,128]{3,2,1,0:T(8,128)(2,1)} %get-tuple-element.26), calls=%async_computation | async-start | bytes 1392640 | tf_op jit(solution)/shard_map/all_to_all | solution.py:503
  46.4 0.0 collective-permute-done.3.gzm
  46.4 6.5 %depth.1 = bf16[4,3,136,128]{3,2,1,0:T(8,128)(2,1)S(1)} custom-call(s32[7]{0:T(128)S(1)} %stack.35.scal, s32[40]{0:T(128)S(1)} %get-tuple-element.17.meta, bf16[7,135,32,135]{3,2,1,0:T(8,128)(2,1)} %bitcast.15, bf16[32,136,136]{2,1,0:T(8,128)(2,1)S(1)} %get-tuple-element.20.pt, bf16[17,136,128]{2,1,0:T(8,128)(2,1)} %collective-permute-done.3.gzm, ...), custom_call_target="tpu_custom_call" | custom-call | flops 8999999488 | bytes 1000000 | tf_op jit(solution)/shard_map/depth/pallas_call | solution.py:415
  52.9 4.8 %all-to-all-done.refs_0_ = bf16[4,5,136,128]{3,2,1,0:T(8,128)(2,1)S(1)} async-done(((bf16[4,5,136,128]{3,2,1,0:T(8,128)(2,1)}), bf16[4,5,136,128]{3,2,1,0:T(8,128)(2,1)S(1)}, u32[]{:S(2)}, u32[]{:S(2)}) %all-to-all-start) | async-done | bytes 696352 | tf_op jit(solution)/shard_map/all_to_all | solution.py:503
  57.7 0.0 collective-permute-start.6
  57.7 3.2 %collective-permute-start.5 = (bf16[4,5,136,128]{3,2,1,0:T(8,128)(2,1)S(1)}, bf16[4,5,136,128]{3,2,1,0:T(8,128)(2,1)S(1)}, u32[]{:S(2)}, u32[]{:S(2)}) collective-permute-start(bf16[4,5,136,128]{3,2,1,0:T(8,128)(2,1)S(1)} %all-to-all-done.refs_0_), channel_id=1, source_target_pairs={{1,0},{2,1},{3,2},{0,3},{5,4},{6,5},{7,6},{4,7},{9,8},{10,9},{11,1... | collective-permute-start | bytes 2088968 | tf_op jit(solution)/shard_map/ppermute | solution.py:507
  61.0 9.9 %all_to_all.10.refs_5_ = bf16[4,3,136,128]{3,2,1,0:T(8,128)(2,1)S(1)} all-to-all(bf16[4,3,136,128]{3,2,1,0:T(8,128)(2,1)S(1)} %depth.1), channel_id=1, replica_groups=mesh['gx'=2,'gy'=4,'zz'=4,'yy'=4] {'zz'}, dimensions={0} | all-to-all | bytes 835584 | tf_op jit(solution)/shard_map/all_to_all | solution.py:503
  70.8 0.0 collective-permute-start.10
  70.8 3.2 %collective-permute-start.9 = (bf16[4,3,136,128]{3,2,1,0:T(8,128)(2,1)S(1)}, bf16[4,3,136,128]{3,2,1,0:T(8,128)(2,1)S(1)}, u32[]{:S(2)}, u32[]{:S(2)}) collective-permute-start(bf16[4,3,136,128]{3,2,1,0:T(8,128)(2,1)S(1)} %all_to_all.10.refs_5_), channel_id=1, source_target_pairs={{1,0},{2,1},{3,2},{0,3},{5,4},{6,5},{7,6},{4,7},{9,8},{10,9},{11,1... | collective-permute-start | bytes 1253384 | tf_op jit(solution)/shard_map/ppermute | solution.py:507
  74.1 3.4 %collective-permute-done.6.refs_2_ = bf16[4,5,136,128]{3,2,1,0:T(8,128)(2,1)S(1)} collective-permute-done((bf16[4,5,136,128]{3,2,1,0:T(8,128)(2,1)S(1)}, bf16[4,5,136,128]{3,2,1,0:T(8,128)(2,1)S(1)}, u32[]{:S(2)}, u32[]{:S(2)}) %collective-permute-start.6) | collective-permute-done | bytes 696352 | tf_op jit(solution)/shard_map/ppermute | solution.py:508
  77.5 1.3 %collective-permute-start.8 = (bf16[2,5,136,128]{3,2,1,0:T(8,128)(2,1)S(1)}, bf16[2,5,136,128]{3,2,1,0:T(8,128)(2,1)S(1)}, u32[]{:S(2)}, u32[]{:S(2)}) collective-permute-start(bf16[2,5,136,128]{3,2,1,0:T(8,128)(2,1)S(1)} %slice.17), channel_id=1, source_target_pairs={{3,0},{7,4},{11,8},{15,12},{19,16},{23,20},{27,24},{31,28},{35,32}... | collective-permute-start | bytes 1044488 | tf_op jit(solution)/shard_map/ppermute | solution.py:513
  78.8 0.0 collective-permute-done.5.refs_1_
  78.9 1.3 %collective-permute-start.7 = (bf16[2,5,136,128]{3,2,1,0:T(8,128)(2,1)S(1)}, bf16[2,5,136,128]{3,2,1,0:T(8,128)(2,1)S(1)}, u32[]{:S(2)}, u32[]{:S(2)}) collective-permute-start(bf16[2,5,136,128]{3,2,1,0:T(8,128)(2,1)S(1)} %slice.16), channel_id=1, source_target_pairs={{1,0},{5,4},{9,8},{13,12},{17,16},{21,20},{25,24},{29,28},{33,32},... | collective-permute-start | bytes 1044488 | tf_op jit(solution)/shard_map/ppermute | solution.py:513
  80.2 6.3 %collective-permute-done.10.refs_7_ = bf16[4,3,136,128]{3,2,1,0:T(8,128)(2,1)S(1)} collective-permute-done((bf16[4,3,136,128]{3,2,1,0:T(8,128)(2,1)S(1)}, bf16[4,3,136,128]{3,2,1,0:T(8,128)(2,1)S(1)}, u32[]{:S(2)}, u32[]{:S(2)}) %collective-permute-start.10) | collective-permute-done | bytes 417824 | tf_op jit(solution)/shard_map/ppermute | solution.py:508
  86.5 1.3 %collective-permute-start.12 = (bf16[2,3,136,128]{3,2,1,0:T(8,128)(2,1)S(1)}, bf16[2,3,136,128]{3,2,1,0:T(8,128)(2,1)S(1)}, u32[]{:S(2)}, u32[]{:S(2)}) collective-permute-start(bf16[2,3,136,128]{3,2,1,0:T(8,128)(2,1)S(1)} %slice.19), channel_id=1, source_target_pairs={{3,0},{7,4},{11,8},{15,12},{19,16},{23,20},{27,24},{31,28},{35,32}... | collective-permute-start | bytes 626696 | tf_op jit(solution)/shard_map/ppermute | solution.py:513
  87.8 0.0 collective-permute-done.9.refs_6_
  87.8 1.3 %collective-permute-start.11 = (bf16[2,3,136,128]{3,2,1,0:T(8,128)(2,1)S(1)}, bf16[2,3,136,128]{3,2,1,0:T(8,128)(2,1)S(1)}, u32[]{:S(2)}, u32[]{:S(2)}) collective-permute-start(bf16[2,3,136,128]{3,2,1,0:T(8,128)(2,1)S(1)} %slice.18), channel_id=1, source_target_pairs={{1,0},{5,4},{9,8},{13,12},{17,16},{21,20},{25,24},{29,28},{33,32},... | collective-permute-start | bytes 626696 | tf_op jit(solution)/shard_map/ppermute | solution.py:513
  89.1 7.0 %collective-permute-done.12.refs_9_ = bf16[2,3,136,128]{3,2,1,0:T(8,128)(2,1)S(1)} collective-permute-done((bf16[2,3,136,128]{3,2,1,0:T(8,128)(2,1)S(1)}, bf16[2,3,136,128]{3,2,1,0:T(8,128)(2,1)S(1)}, u32[]{:S(2)}, u32[]{:S(2)}) %collective-permute-start.12) | collective-permute-done | bytes 208928 | tf_op jit(solution)/shard_map/ppermute | solution.py:513
  96.1 0.0 collective-permute-done.8.refs_4_
  96.1 0.0 collective-permute-done.7.refs_3_
  96.1 5.2 %assemble.1 = (bf16[7,135,16,135]{3,2,1,0:T(8,128)(2,1)}, bf16[16,135]{1,0:T(8,128)(2,1)}) custom-call(s32[7]{0:T(128)S(1)} %stack.35.scal, bf16[4,5,136,128]{3,2,1,0:T(8,128)(2,1)S(1)} %all-to-all-done.refs_0_, bf16[4,5,136,128]{3,2,1,0:T(8,128)(2,1)S(1)} %collective-permute-done.5.refs_1_, bf16[4,5,136,128]{3,2,1,0:T(8,128)(2,1)S(1)} %collective-permute-done.6.refs_2_, ...), custom_call_target="tpu_custom_call" | custom-call | tf_op jit(solution)/shard_map/assemble/pallas_call | solution.py:482
  (7 shorter events, 0.1 us)
Async XLA Ops:
  7.3 24.3 %collective-permute-start = (bf16[10,136,128]{2,1,0:T(8,128)(2,1)S(1)}, bf16[10,136,128]{2,1,0:T(8,128)(2,1)S(1)}, u32[]{:S(2)}, u32[]{:S(2)}) collective-permute-start(bf16[10,136,128]{2,1,0:T(8,128)(2,1)S(1)} %get-tuple-element.21), channel_id=1, source_target_pairs={{0,64},{64,0},{1,65},{65,1},{2,66},{66,2},{3,67},{67,3},{4,68},{68... | collective-permute-start | bytes 1044488 | tf_op jit(solution)/shard_map/ppermute | solution.py:529
  7.4 24.2 %collective-permute-start.1 = (bf16[10,136,128]{2,1,0:T(8,128)(2,1)S(1)}, bf16[10,136,128]{2,1,0:T(8,128)(2,1)S(1)}, u32[]{:S(2)}, u32[]{:S(2)}) collective-permute-start(bf16[10,136,128]{2,1,0:T(8,128)(2,1)S(1)} %get-tuple-element.22), channel_id=1, source_target_pairs={{0,16},{16,32},{32,48},{48,0},{1,17},{17,33},{33,49},{49,1},{2,18}... | collective-permute-start | bytes 1044488 | tf_op jit(solution)/shard_map/ppermute | solution.py:532
  9.1 22.5 %collective-permute-start.2 = (bf16[10,136,128]{2,1,0:T(8,128)(2,1)S(1)}, bf16[10,136,128]{2,1,0:T(8,128)(2,1)S(1)}, u32[]{:S(2)}, u32[]{:S(2)}) collective-permute-start(bf16[10,136,128]{2,1,0:T(8,128)(2,1)S(1)} %get-tuple-element.23), channel_id=1, source_target_pairs={{16,0},{32,16},{48,32},{0,48},{17,1},{33,17},{49,33},{1,49},{18,2}... | collective-permute-start | bytes 1044488 | tf_op jit(solution)/shard_map/ppermute | solution.py:533
  10.7 35.7 %collective-permute-start.4 = (bf16[17,136,128]{2,1,0:T(8,128)(2,1)}, bf16[17,136,128]{2,1,0:T(8,128)(2,1)}, u32[]{:S(2)}, u32[]{:S(2)}) collective-permute-start(bf16[17,136,128]{2,1,0:T(8,128)(2,1)} %get-tuple-element.18.pz0), channel_id=1, source_target_pairs={{1,0},{2,1},{3,2},{4,3},{5,4},{6,5},{7,6},{8,7},{9,8},{10,9},{11,1... | collective-permute-start | bytes 1775624 | tf_op jit(solution)/shard_map/ppermute | solution.py:531
  17.3 29.1 %collective-permute-start.3 = (bf16[17,136,128]{2,1,0:T(8,128)(2,1)}, bf16[17,136,128]{2,1,0:T(8,128)(2,1)}, u32[]{:S(2)}, u32[]{:S(2)}) collective-permute-start(bf16[17,136,128]{2,1,0:T(8,128)(2,1)} %get-tuple-element.19.pz1), channel_id=1, source_target_pairs={{0,1},{1,2},{2,3},{3,4},{4,5},{5,6},{6,7},{7,8},{8,9},{9,10},{10,1... | collective-permute-start | bytes 1775624 | tf_op jit(solution)/shard_map/ppermute | solution.py:530
  42.9 14.8 %all-to-all-start = ((bf16[4,5,136,128]{3,2,1,0:T(8,128)(2,1)}), bf16[4,5,136,128]{3,2,1,0:T(8,128)(2,1)S(1)}, u32[]{:S(2)}, u32[]{:S(2)}) async-start(bf16[4,5,136,128]{3,2,1,0:T(8,128)(2,1)} %get-tuple-element.26), calls=%async_computation | async-start | bytes 1392640 | tf_op jit(solution)/shard_map/all_to_all | solution.py:503
  57.7 19.8 %collective-permute-start.6 = (bf16[4,5,136,128]{3,2,1,0:T(8,128)(2,1)S(1)}, bf16[4,5,136,128]{3,2,1,0:T(8,128)(2,1)S(1)}, u32[]{:S(2)}, u32[]{:S(2)}) collective-permute-start(bf16[4,5,136,128]{3,2,1,0:T(8,128)(2,1)S(1)} %all-to-all-done.refs_0_), channel_id=1, source_target_pairs={{3,0},{0,1},{1,2},{2,3},{7,4},{4,5},{5,6},{6,7},{11,8},{8,9},{9,10... | collective-permute-start | bytes 2088968 | tf_op jit(solution)/shard_map/ppermute | solution.py:508
  57.7 21.1 %collective-permute-start.5 = (bf16[4,5,136,128]{3,2,1,0:T(8,128)(2,1)S(1)}, bf16[4,5,136,128]{3,2,1,0:T(8,128)(2,1)S(1)}, u32[]{:S(2)}, u32[]{:S(2)}) collective-permute-start(bf16[4,5,136,128]{3,2,1,0:T(8,128)(2,1)S(1)} %all-to-all-done.refs_0_), channel_id=1, source_target_pairs={{1,0},{2,1},{3,2},{0,3},{5,4},{6,5},{7,6},{4,7},{9,8},{10,9},{11,1... | collective-permute-start | bytes 2088968 | tf_op jit(solution)/shard_map/ppermute | solution.py:507
  70.8 15.6 %collective-permute-start.10 = (bf16[4,3,136,128]{3,2,1,0:T(8,128)(2,1)S(1)}, bf16[4,3,136,128]{3,2,1,0:T(8,128)(2,1)S(1)}, u32[]{:S(2)}, u32[]{:S(2)}) collective-permute-start(bf16[4,3,136,128]{3,2,1,0:T(8,128)(2,1)S(1)} %all_to_all.10.refs_5_), channel_id=1, source_target_pairs={{3,0},{0,1},{1,2},{2,3},{7,4},{4,5},{5,6},{6,7},{11,8},{8,9},{9,10... | collective-permute-start | bytes 1253384 | tf_op jit(solution)/shard_map/ppermute | solution.py:508
  70.8 16.9 %collective-permute-start.9 = (bf16[4,3,136,128]{3,2,1,0:T(8,128)(2,1)S(1)}, bf16[4,3,136,128]{3,2,1,0:T(8,128)(2,1)S(1)}, u32[]{:S(2)}, u32[]{:S(2)}) collective-permute-start(bf16[4,3,136,128]{3,2,1,0:T(8,128)(2,1)S(1)} %all_to_all.10.refs_5_), channel_id=1, source_target_pairs={{1,0},{2,1},{3,2},{0,3},{5,4},{6,5},{7,6},{4,7},{9,8},{10,9},{11,1... | collective-permute-start | bytes 1253384 | tf_op jit(solution)/shard_map/ppermute | solution.py:507
  77.5 18.5 %collective-permute-start.8 = (bf16[2,5,136,128]{3,2,1,0:T(8,128)(2,1)S(1)}, bf16[2,5,136,128]{3,2,1,0:T(8,128)(2,1)S(1)}, u32[]{:S(2)}, u32[]{:S(2)}) collective-permute-start(bf16[2,5,136,128]{3,2,1,0:T(8,128)(2,1)S(1)} %slice.17), channel_id=1, source_target_pairs={{3,0},{7,4},{11,8},{15,12},{19,16},{23,20},{27,24},{31,28},{35,32}... | collective-permute-start | bytes 1044488 | tf_op jit(solution)/shard_map/ppermute | solution.py:513
  78.9 17.2 %collective-permute-start.7 = (bf16[2,5,136,128]{3,2,1,0:T(8,128)(2,1)S(1)}, bf16[2,5,136,128]{3,2,1,0:T(8,128)(2,1)S(1)}, u32[]{:S(2)}, u32[]{:S(2)}) collective-permute-start(bf16[2,5,136,128]{3,2,1,0:T(8,128)(2,1)S(1)} %slice.16), channel_id=1, source_target_pairs={{1,0},{5,4},{9,8},{13,12},{17,16},{21,20},{25,24},{29,28},{33,32},... | collective-permute-start | bytes 1044488 | tf_op jit(solution)/shard_map/ppermute | solution.py:513
  86.5 9.6 %collective-permute-start.12 = (bf16[2,3,136,128]{3,2,1,0:T(8,128)(2,1)S(1)}, bf16[2,3,136,128]{3,2,1,0:T(8,128)(2,1)S(1)}, u32[]{:S(2)}, u32[]{:S(2)}) collective-permute-start(bf16[2,3,136,128]{3,2,1,0:T(8,128)(2,1)S(1)} %slice.19), channel_id=1, source_target_pairs={{3,0},{7,4},{11,8},{15,12},{19,16},{23,20},{27,24},{31,28},{35,32}... | collective-permute-start | bytes 626696 | tf_op jit(solution)/shard_map/ppermute | solution.py:513
  87.8 8.3 %collective-permute-start.11 = (bf16[2,3,136,128]{3,2,1,0:T(8,128)(2,1)S(1)}, bf16[2,3,136,128]{3,2,1,0:T(8,128)(2,1)S(1)}, u32[]{:S(2)}, u32[]{:S(2)}) collective-permute-start(bf16[2,3,136,128]{3,2,1,0:T(8,128)(2,1)S(1)} %slice.18), channel_id=1, source_target_pairs={{1,0},{5,4},{9,8},{13,12},{17,16},{21,20},{25,24},{29,28},{33,32},... | collective-permute-start | bytes 626696 | tf_op jit(solution)/shard_map/ppermute | solution.py:513
